TPU v7x, 128 devices: a whole 4x4x4 slice. The times are simulated.
128 devices in a mesh: cluster: 8 (over y, core), member: 16 (over z, x).
Axes of the slice: x: 4, y: 4, z: 4, core: 2. Of those that a mesh axis runs over, the one named last changes fastest.
Arguments:
- features: bfloat16 [131072, 512], P(('cluster', 'member')), may hold values from -6 to 6
- aggregated: bfloat16 [131072, 512], P(('cluster', 'member')), may hold values from -6 to 6
- cotangent: bfloat16 [131072, 512], P(('cluster', 'member')), may hold values from -6 to 6
- w_self: bfloat16 [512, 512], replicated, may hold values from -0.25 to 0.25
- w_neigh: bfloat16 [512, 512], replicated, may hold values from -0.25 to 0.25
- degrees: int32 [131072], P(('cluster', 'member')), may hold values from 16 to 128
- tile_rows: int32 [49152], P(('cluster', 'member')), may hold values from 0 to 7
- tile_cols: int32 [49152], P(('cluster', 'member')), may hold values from 0 to 15, as said below
- tile_vals: bfloat16 [49152, 128, 128], P(('cluster', 'member')), may hold values from 0 to 1
- recv_rows: int32 [128, 128, 16], P(('cluster', 'member')), may hold values from 0 to 1024, as said below
Outputs:
- grad_nodes: float32 [131072, 512], P(('cluster', 'member'))
- grad_hubs: float32 [2048, 512], P(('cluster', 'member'))
- grad_weights: float32 [2, 512, 512], replicated
Inputs may be any that keep to these rules, and one draw needn't show every extreme that they name: `tile_cols`: tiles of the hub region name blocks below 16, own tiles below 8, boundary tiles below 16. `recv_rows`: every receiver gets 16 live rows from some sender; live rows of a sender come first.
All inputs are finite; a program needn't handle non-finite values.
Results may differ from a plain program's by a relative error of at most 0.0029.
Values may be sent and summed in bfloat16 or wider, within the bound.
No kernel may reach another device: no remote copies, remote signals or barrier semaphores. Data moves between devices by JAX's collectives and lax.ppermute only.
A program may use at most 192 MiB of HBM per device.

v0:
```python
import jax
import jax.numpy as jnp
from jax import lax
from jax.sharding import PartitionSpec as P

HUBS = 2048


def spread(vals, rows, cols, msg_blocks, nblocks):
    src_blocks = msg_blocks.shape[0]
    width = msg_blocks.shape[2]
    acc = jnp.zeros((nblocks, 128, width), jnp.float32)
    count = vals.shape[0]
    step = min(32, count)
    src_ids = jnp.arange(src_blocks, dtype=jnp.int32)[None, :]
    dst_ids = jnp.arange(nblocks, dtype=jnp.int32)[None, :]
    for start in range(0, count, step):
        picker = (rows[start : start + step][:, None] == src_ids).astype(jnp.bfloat16)
        gathered = jnp.einsum(
            "tb,bid->tid", picker, msg_blocks, preferred_element_type=jnp.float32
        ).astype(jnp.bfloat16)
        product = jnp.einsum(
            "tij,tid->tjd", vals[start : start + step], gathered, preferred_element_type=jnp.float32
        )
        placer = (cols[start : start + step][:, None] == dst_ids).astype(jnp.float32)
        acc = acc + jnp.einsum("tc,tjd->cjd", placer, product, precision=lax.Precision.HIGHEST)
    return acc.reshape(nblocks * 128, width)


def local(
    features,
    aggregated,
    cotangent,
    w_self,
    w_neigh,
    degrees,
    tile_rows,
    tile_cols,
    tile_vals,
    recv_rows,
):
    nodes = cotangent.shape[0]
    width = cotangent.shape[1]
    reg = tile_rows.shape[0] // 3
    devices_all = recv_rows.shape[1]
    slots = recv_rows.shape[2]
    message = jnp.dot(cotangent, w_neigh.T, preferred_element_type=jnp.float32) / degrees[
        :, None
    ].astype(jnp.float32)
    msg_blocks = message.astype(jnp.bfloat16).reshape(nodes // 128, 128, width)
    hub_part = spread(tile_vals[:reg], tile_rows[:reg], tile_cols[:reg], msg_blocks, HUBS // 128)
    hub_share = lax.psum_scatter(hub_part, ("cluster", "member"), scatter_dimension=0, tiled=True)
    ghost = spread(
        tile_vals[2 * reg :],
        tile_rows[2 * reg :],
        tile_cols[2 * reg :],
        msg_blocks,
        devices_all * slots // 128,
    )
    ghost = ghost.astype(jnp.bfloat16).reshape(devices_all, slots, width)
    arrived = lax.all_to_all(ghost, ("cluster", "member"), split_axis=0, concat_axis=0, tiled=True)
    own_part = spread(
        tile_vals[reg : 2 * reg],
        tile_rows[reg : 2 * reg],
        tile_cols[reg : 2 * reg],
        msg_blocks,
        nodes // 128,
    )
    own_part = own_part + jnp.dot(cotangent, w_self.T, preferred_element_type=jnp.float32)
    local_weights = jnp.stack(
        [
            jnp.einsum("nd,ne->de", features, cotangent, preferred_element_type=jnp.float32),
            jnp.einsum("nd,ne->de", aggregated, cotangent, preferred_element_type=jnp.float32),
        ]
    )
    grad_weights = lax.psum(local_weights, ("cluster", "member"))
    targets = recv_rows.reshape(-1)
    landing = (targets[:, None] == jnp.arange(nodes, dtype=jnp.int32)[None, :]).astype(jnp.bfloat16)
    received = jnp.einsum(
        "sn,sd->nd", landing, arrived.reshape(-1, width), preferred_element_type=jnp.float32
    )
    grad_nodes = own_part + received
    return (grad_nodes, hub_share, grad_weights)


def solution(mesh):
    in_specs = (
        P(("cluster", "member"), None),
        P(("cluster", "member"), None),
        P(("cluster", "member"), None),
        P(),
        P(),
        P(("cluster", "member")),
        P(("cluster", "member")),
        P(("cluster", "member")),
        P(("cluster", "member"), None, None),
        P(("cluster", "member"), None, None),
    )
    out_specs = (P(("cluster", "member"), None), P(("cluster", "member"), None), P())
    return jax.shard_map(local, mesh=mesh, in_specs=in_specs, out_specs=out_specs, check_vma=False)
```

profile of v0, /device:TPU:0, one launch (start us, length us, event | category | flops | bytes accessed | tf_op | source)
XLA Modules:
  0.0 825.6 jit_solution(16626897047204534492)
XLA Ops:
  8.4 1.9 convolution_bitcast_fusion
  11.1 1.5 pad_maximum_fusion
  16.0 9.3 %fusion.36 = f32[32,512,128]{2,1,0:T(8,128)} fusion(bf16[32,128,512]{2,0,1:T(8,128)(2,1)S(1)} %fusion.91, bf16[384,128,128]{2,1,0:T(8,128)(2,1)} %param.18), kind=kOutput, calls=%fused_computation.49 | convolution fusion | flops 536870912 | bytes 13631488 | tf_op jit(solution)/shard_map/tij,tid->tjd/dot_general | solution.py:22
  25.3 10.6 %copy.41 = f32[32,512,128]{1,0,2:T(8,128)} copy(f32[32,512,128]{2,1,0:T(8,128)} %fusion.36) | data formatting | bytes 16777216 | tf_op jit(solution)/shard_map/tij,tid->tjd/dot_general | solution.py:22
  37.1 9.3 %fusion.35 = f32[32,512,128]{2,1,0:T(8,128)} fusion(bf16[32,128,512]{2,0,1:T(8,128)(2,1)S(1)} %fusion.88, bf16[384,128,128]{2,1,0:T(8,128)(2,1)} %param.18), kind=kOutput, calls=%fused_computation.48 | convolution fusion | flops 536870912 | bytes 13631488 | tf_op jit(solution)/shard_map/tij,tid->tjd/dot_general | solution.py:22
  46.5 10.6 %copy.39 = f32[32,512,128]{1,0,2:T(8,128)} copy(f32[32,512,128]{2,1,0:T(8,128)} %fusion.35) | data formatting | bytes 16777216 | tf_op jit(solution)/shard_map/tij,tid->tjd/dot_general | solution.py:22
  58.3 9.3 %fusion.34 = f32[32,512,128]{2,1,0:T(8,128)} fusion(bf16[32,128,512]{2,0,1:T(8,128)(2,1)S(1)} %fusion.85, bf16[384,128,128]{2,1,0:T(8,128)(2,1)} %param.18), kind=kOutput, calls=%fused_computation.47 | convolution fusion | flops 536870912 | bytes 13631488 | tf_op jit(solution)/shard_map/tij,tid->tjd/dot_general | solution.py:22
  67.6 10.9 %copy.37 = f32[32,512,128]{1,0,2:T(8,128)} copy(f32[32,512,128]{2,1,0:T(8,128)} %fusion.34) | data formatting | bytes 16777216 | tf_op jit(solution)/shard_map/tij,tid->tjd/dot_general | solution.py:22
  78.5 1.3 fusion.82
  79.8 10.0 %fusion.33 = f32[32,512,128]{2,1,0:T(8,128)} fusion(bf16[32,128,512]{2,0,1:T(8,128)(2,1)S(1)} %fusion.82, bf16[384,128,128]{2,1,0:T(8,128)(2,1)} %param.18), kind=kOutput, calls=%fused_computation.46 | convolution fusion | flops 536870912 | bytes 13631488 | tf_op jit(solution)/shard_map/tij,tid->tjd/dot_general | solution.py:22
  89.8 4.5 fusion
  94.3 4.4 fusion.2
  98.8 4.4 fusion.4
  103.1 10.5 %copy.35 = f32[32,512,128]{1,0,2:T(8,128)} copy(f32[32,512,128]{2,1,0:T(8,128)} %fusion.33) | data formatting | bytes 16777216 | tf_op jit(solution)/shard_map/tij,tid->tjd/dot_general | solution.py:22
  113.7 11.3 %add_add_fusion = f32[16,128,512]{2,0,1:T(8,128)S(1)} fusion(f32[16,128,512]{2,0,1:T(8,128)} %fusion, f32[16,128,512]{2,0,1:T(8,128)} %fusion.2, f32[16,128,512]{2,0,1:T(8,128)} %fusion.4, f32[32,512,128]{1,0,2:T(8,128)} %copy.35, s32[32]{0:T(128)S(1)} %get-tuple-element.3), kind=kOutput, calls=%fused_computation.50 | convolution fusion | flops 405799424 | bytes 25165952 | tf_op jit(solution)/shard_map/tc,tjd->cjd/dot_general | solution.py:26
  125.0 4.4 copy.16
  130.7 9.5 %fusion.31 = f32[32,512,128]{2,1,0:T(8,128)} fusion(bf16[32,128,512]{2,0,1:T(8,128)(2,1)S(1)} %fusion.76, bf16[384,128,128]{2,1,0:T(8,128)(2,1)} %param.18), kind=kOutput, calls=%fused_computation.44 | convolution fusion | flops 536870912 | bytes 13631488 | tf_op jit(solution)/shard_map/tij,tid->tjd/dot_general | solution.py:22
  140.3 10.4 %copy.31 = f32[32,512,128]{1,0,2:T(8,128)} copy(f32[32,512,128]{2,1,0:T(8,128)} %fusion.31) | data formatting | bytes 16777216 | tf_op jit(solution)/shard_map/tij,tid->tjd/dot_general | solution.py:22
  150.7 1.3 fusion.73
  152.0 9.3 %fusion.30 = f32[32,512,128]{2,1,0:T(8,128)} fusion(bf16[32,128,512]{2,0,1:T(8,128)(2,1)S(1)} %fusion.73, bf16[384,128,128]{2,1,0:T(8,128)(2,1)} %param.18), kind=kOutput, calls=%fused_computation.43 | convolution fusion | flops 536870912 | bytes 13631488 | tf_op jit(solution)/shard_map/tij,tid->tjd/dot_general | solution.py:22
  161.3 10.8 %copy.29 = f32[32,512,128]{1,0,2:T(8,128)} copy(f32[32,512,128]{2,1,0:T(8,128)} %fusion.30) | data formatting | bytes 16777216 | tf_op jit(solution)/shard_map/tij,tid->tjd/dot_general | solution.py:22
  173.4 9.3 %fusion.32 = f32[32,512,128]{2,1,0:T(8,128)} fusion(bf16[32,128,512]{2,0,1:T(8,128)(2,1)S(1)} %fusion.79, bf16[384,128,128]{2,1,0:T(8,128)(2,1)} %param.18), kind=kOutput, calls=%fused_computation.45 | convolution fusion | flops 536870912 | bytes 13631488 | tf_op jit(solution)/shard_map/tij,tid->tjd/dot_general | solution.py:22
  184.0 9.9 %fusion.29 = f32[32,512,128]{2,1,0:T(8,128)} fusion(bf16[32,128,512]{2,0,1:T(8,128)(2,1)S(1)} %fusion.70, bf16[384,128,128]{2,1,0:T(8,128)(2,1)} %param.18), kind=kOutput, calls=%fused_computation.42 | convolution fusion | flops 536870912 | bytes 13631488 | tf_op jit(solution)/shard_map/tij,tid->tjd/dot_general | solution.py:22
  194.1 4.5 fusion.10
  198.6 4.5 fusion.12
  203.1 10.3 %copy.33 = f32[32,512,128]{1,0,2:T(8,128)} copy(f32[32,512,128]{2,1,0:T(8,128)} %fusion.32) | data formatting | bytes 16777216 | tf_op jit(solution)/shard_map/tij,tid->tjd/dot_general | solution.py:22
  213.5 10.3 %copy.27 = f32[32,512,128]{1,0,2:T(8,128)} copy(f32[32,512,128]{2,1,0:T(8,128)} %fusion.29) | data formatting | bytes 16777216 | tf_op jit(solution)/shard_map/tij,tid->tjd/dot_general | solution.py:22
  223.8 8.5 %fusion.8 = f32[16,128,512]{2,0,1:T(8,128)S(1)} fusion(f32[32,512,128]{1,0,2:T(8,128)} %copy.33, s32[32]{0:T(128)S(1)} %get-tuple-element.5), kind=kOutput, calls=%fused_computation.8 | convolution fusion | flops 402653696 | bytes 12583040 | tf_op jit(solution)/shard_map/tc,tjd->cjd/dot_general | solution.py:26
  232.3 6.7 add_convert_fusion
  239.0 4.1 copy.15
  243.1 11.9 %all-to-all-start = ((bf16[128,16,512]{2,1,0:T(8,128)(2,1)}), bf16[128,16,512]{2,1,0:T(8,128)(2,1)}, u32[]{:S(2)}, u32[]{:S(2)}) async-start(bf16[128,16,512]{2,1,0:T(8,128)(2,1)} %bitcast.160), calls=%async_computation | async-start | bytes 4194304 | tf_op jit(solution)/shard_map/all_to_all | solution.py:61
  255.2 1.3 fusion.67
  256.5 9.3 %fusion.28 = f32[32,512,128]{2,1,0:T(8,128)} fusion(bf16[32,128,512]{2,0,1:T(8,128)(2,1)S(1)} %fusion.67, bf16[384,128,128]{2,1,0:T(8,128)(2,1)} %param.18), kind=kOutput, calls=%fused_computation.41 | convolution fusion | flops 536870912 | bytes 13631488 | tf_op jit(solution)/shard_map/tij,tid->tjd/dot_general | solution.py:22
  265.8 10.6 %copy.25 = f32[32,512,128]{1,0,2:T(8,128)} copy(f32[32,512,128]{2,1,0:T(8,128)} %fusion.28) | data formatting | bytes 16777216 | tf_op jit(solution)/shard_map/tij,tid->tjd/dot_general | solution.py:22
  277.7 9.3 %fusion.27 = f32[32,512,128]{2,1,0:T(8,128)} fusion(bf16[32,128,512]{2,0,1:T(8,128)(2,1)S(1)} %fusion.64, bf16[384,128,128]{2,1,0:T(8,128)(2,1)} %param.18), kind=kOutput, calls=%fused_computation.40 | convolution fusion | flops 536870912 | bytes 13631488 | tf_op jit(solution)/shard_map/tij,tid->tjd/dot_general | solution.py:22
  287.0 10.8 %copy.23 = f32[32,512,128]{1,0,2:T(8,128)} copy(f32[32,512,128]{2,1,0:T(8,128)} %fusion.27) | data formatting | bytes 16777216 | tf_op jit(solution)/shard_map/tij,tid->tjd/dot_general | solution.py:22
  299.1 9.3 %fusion.26 = f32[32,512,128]{2,1,0:T(8,128)} fusion(bf16[32,128,512]{2,0,1:T(8,128)(2,1)S(1)} %fusion.61, bf16[384,128,128]{2,1,0:T(8,128)(2,1)} %param.18), kind=kOutput, calls=%fused_computation.39 | convolution fusion | flops 536870912 | bytes 13631488 | tf_op jit(solution)/shard_map/tij,tid->tjd/dot_general | solution.py:22
  308.3 10.5 %copy.21 = f32[32,512,128]{1,0,2:T(8,128)} copy(f32[32,512,128]{2,1,0:T(8,128)} %fusion.26) | data formatting | bytes 16777216 | tf_op jit(solution)/shard_map/tij,tid->tjd/dot_general | solution.py:22
  320.2 9.3 %fusion.25 = f32[32,512,128]{2,1,0:T(8,128)} fusion(bf16[32,128,512]{2,0,1:T(8,128)(2,1)S(1)} %fusion.58, bf16[384,128,128]{2,1,0:T(8,128)(2,1)} %param.18), kind=kOutput, calls=%fused_computation.38 | convolution fusion | flops 536870912 | bytes 13631488 | tf_op jit(solution)/shard_map/tij,tid->tjd/dot_general | solution.py:22
  329.5 10.4 %copy.19 = f32[32,512,128]{1,0,2:T(8,128)} copy(f32[32,512,128]{2,1,0:T(8,128)} %fusion.25) | data formatting | bytes 16777216 | tf_op jit(solution)/shard_map/tij,tid->tjd/dot_general | solution.py:22
  339.9 6.3 fusion.16
  346.2 6.5 fusion.18
  352.7 6.7 fusion.20
  359.5 3.3 add_add_fusion.1
  364.0 4.5 fusion.24
  368.5 2.2 fusion.42
  370.7 444.8 %reduce-scatter.2.cloned.1.call-done = f32[16,512]{1,0:T(8,128)} async-done(((f32[2048,512]{1,0:T(8,128)}), f32[16,512]{1,0:T(8,128)}) %reduce-scatter.2.cloned.1.call-update) | async-done | bytes 32784 | tf_op jit(solution)/shard_map/reduce_scatter | solution.py:52
  815.5 3.1 copy.91
  (83 shorter events, 17.0 us)
Async XLA Ops:
  7.2 1.2 copy-start
  7.2 3.2 copy-start.13
  7.2 363.5 %all-reduce.2.cloned.1.call-start = ((), (), s32[]{:S(2)}) async-start(), calls=%async_computation.3 | async-start | bytes 4194304 | tf_op jit(solution)/shard_map/psum | solution.py:76
  11.1 1.7 copy-start.7
  11.1 1.7 copy-start.4
  11.1 2.2 copy-start.5
  11.1 2.8 copy-start.14
  12.7 802.8 %reduce-scatter.2.cloned.1.call-start = ((), (), s32[]{:S(2)}) async-start(), calls=%async_computation.2 | async-start | bytes 4227072 | tf_op jit(solution)/shard_map/reduce_scatter | solution.py:52
  78.5 11.3 %slice-start.2 = ((s8[8388608]{0:T(1024)(128)(4,1)}), s8[4194304]{0:T(1024)(128)(4,1)S(1)}, s32[]{:S(2)}) async-start(s8[8388608]{0:T(1024)(128)(4,1)} %bitcast.149), calls=%async_computation.6 | async-start | bytes 8388608
  78.5 15.8 %slice-start.6 = ((s8[8388608]{0:T(1024)(128)(4,1)}), s8[4194304]{0:T(1024)(128)(4,1)S(1)}, s32[]{:S(2)}) async-start(s8[8388608]{0:T(1024)(128)(4,1)} %bitcast.153), calls=%async_computation.10 | async-start | bytes 8388608
  79.8 10.0 %slice-start.3 = ((s8[8388608]{0:T(1024)(128)(4,1)}), s8[4194304]{0:T(1024)(128)(4,1)S(1)}, s32[]{:S(2)}) async-start(s8[8388608]{0:T(1024)(128)(4,1)} %bitcast.149), calls=%async_computation.7 | async-start | bytes 8388608
  79.8 14.5 %slice-start.7 = ((s8[8388608]{0:T(1024)(128)(4,1)}), s8[4194304]{0:T(1024)(128)(4,1)S(1)}, s32[]{:S(2)}) async-start(s8[8388608]{0:T(1024)(128)(4,1)} %bitcast.153), calls=%async_computation.11 | async-start | bytes 8388608
  89.8 8.9 %slice-start.10 = ((s8[8388608]{0:T(1024)(128)(4,1)}), s8[4194304]{0:T(1024)(128)(4,1)S(1)}, s32[]{:S(2)}) async-start(s8[8388608]{0:T(1024)(128)(4,1)} %bitcast.157), calls=%async_computation.14 | async-start | bytes 8388608
  94.3 4.4 slice-start.11
  182.7 11.3 %slice-start.4 = ((s8[8388608]{0:T(1024)(128)(4,1)}), s8[4194304]{0:T(1024)(128)(4,1)S(1)}, s32[]{:S(2)}) async-start(s8[8388608]{0:T(1024)(128)(4,1)} %bitcast.151), calls=%async_computation.8 | async-start | bytes 8388608
  182.7 15.9 %slice-start.8 = ((s8[8388608]{0:T(1024)(128)(4,1)}), s8[4194304]{0:T(1024)(128)(4,1)S(1)}, s32[]{:S(2)}) async-start(s8[8388608]{0:T(1024)(128)(4,1)} %bitcast.155), calls=%async_computation.12 | async-start | bytes 8388608
  184.0 10.1 %slice-start.5 = ((s8[8388608]{0:T(1024)(128)(4,1)}), s8[4194304]{0:T(1024)(128)(4,1)S(1)}, s32[]{:S(2)}) async-start(s8[8388608]{0:T(1024)(128)(4,1)} %bitcast.151), calls=%async_computation.9 | async-start | bytes 8388608
  184.0 14.6 %slice-start.9 = ((s8[8388608]{0:T(1024)(128)(4,1)}), s8[4194304]{0:T(1024)(128)(4,1)S(1)}, s32[]{:S(2)}) async-start(s8[8388608]{0:T(1024)(128)(4,1)} %bitcast.155), calls=%async_computation.13 | async-start | bytes 8388608
  223.8 8.5 %copy-start.1 = (f32[32,512,128]{1,0,2:T(8,128)S(1)}, f32[32,512,128]{1,0,2:T(8,128)}, u32[]{:S(2)}) copy-start(f32[32,512,128]{1,0,2:T(8,128)} %copy.27) | copy-start | bytes 25165828
  223.8 8.5 %copy-start.2 = (f32[16,128,512]{2,0,1:T(8,128)S(1)}, f32[16,128,512]{2,0,1:T(8,128)}, u32[]{:S(2)}) copy-start(f32[16,128,512]{2,0,1:T(8,128)} %fusion.10) | copy-start | bytes 12582916
  239.0 16.0 %copy-start.6 = (s32[1,128,16]{1,2,0:T(8,128)S(1)}, s32[1,128,16]{1,2,0:T(8,128)}, u32[]{:S(2)}) copy-start(s32[1,128,16]{1,2,0:T(8,128)} %param.19) | copy-start | bytes 24580
  243.1 120.9 %all-to-all-start = ((bf16[128,16,512]{2,1,0:T(8,128)(2,1)}), bf16[128,16,512]{2,1,0:T(8,128)(2,1)}, u32[]{:S(2)}, u32[]{:S(2)}) async-start(bf16[128,16,512]{2,1,0:T(8,128)(2,1)} %bitcast.160), calls=%async_computation | async-start | bytes 4194304 | tf_op jit(solution)/shard_map/all_to_all | solution.py:61
  308.3 10.5 %copy-start.9 = (s32[32]{0:T(128)S(1)}, s32[32]{0:T(128)}, u32[]{:S(2)}) copy-start(s32[32]{0:T(128)} %get-tuple-element.24) | copy-start | bytes 388
  329.5 10.4 %copy-start.12 = (s32[32]{0:T(128)S(1)}, s32[32]{0:T(128)}, u32[]{:S(2)}) copy-start(s32[32]{0:T(128)} %get-tuple-element.9) | copy-start | bytes 388
  339.9 6.3 copy-start.11
  346.2 6.5 copy-start.10
  346.2 13.2 %slice-start = ((s8[8388608]{0:T(1024)(128)(4,1)}), s8[4194304]{0:T(1024)(128)(4,1)S(1)}, s32[]{:S(2)}) async-start(s8[8388608]{0:T(1024)(128)(4,1)} %bitcast.147), calls=%async_computation.4 | async-start | bytes 8388608
  352.7 6.7 slice-start.1
  352.7 6.7 copy-start.8
  364.0 4.5 copy-start.3
Sparse Core Ops, SparseCore 0:
  12.9 152.8 all-reduce.1
  168.7 646.7 reduce-scatter.1
where the time goes:
time: 834 us; the launch traced here: 826 us
  waiting for transfers between devices  445 us (53%)
  matrix products  210 us (25%)
  local copies, waits for them, and re-layouts  142 us (17%)
  between operations  14.9 us (2%)
  starting transfers between devices  12 us (1%)
    reduce_scatter x1, waiting for transfers between devices, local(): lax.psum_scatter(hub_part, ('cluster', 'member'), scatter_dimension=0, ti...  445 us
    dot_general x12, local copies, waits for them, and re-layouts, spread(): jnp.einsum('tij,tid->tjd', vals[start:start + step], gathered, preferred_...  127 us
    dot_general x12, matrix products, spread(): jnp.einsum('tij,tid->tjd', vals[start:start + step], gathered, preferred_...  113 us
    dot_general x12, matrix products, spread(): jnp.einsum('tc,tjd->cjd', placer, product, precision=lax.Precision.HIGHEST)  71.6 us
  transfers between devices with their start and end apart: 3, of which 1 were waited for; matrix products, arithmetic and copies ran while one was open for 42% of the time, Pallas kernels for 0%

commit v1 on v0

v1 whole, which is shorter than its diff:
```python
import functools

import jax
import jax.numpy as jnp
from jax import lax
from jax.experimental import pallas as pl
from jax.experimental.pallas import tpu as pltpu
from jax.sharding import Mesh, PartitionSpec as P

F32 = jnp.float32
BF16 = jnp.bfloat16
ALL = ("y", "core", "z", "x")
TILE = 128
REG = 128
WIDTH = 512
NODES = 1024
HUB_BLOCKS = 16
OWN_BLOCKS = 8
UNROLL = 8
PLAN = 256
VMEM = 56 << 20


def contract(a, b, da, db):
    return lax.dot_general(a, b, (((da,), (db,)), ((), ())), preferred_element_type=F32)


def write_plan(region, rows_ref, cols_ref, plan_vmem, blocks):
    cols = cols_ref[region : region + 1, :]
    rows = rows_ref[region : region + 1, :]
    hot = (lax.broadcasted_iota(jnp.int32, (16, REG), 0) == cols).astype(F32)
    before = (
        lax.broadcasted_iota(jnp.int32, (REG, REG), 0) < lax.broadcasted_iota(jnp.int32, (REG, REG), 1)
    ).astype(BF16)
    rank = jnp.sum(hot * contract(hot.astype(BF16), before, 1, 0), axis=0, keepdims=True)
    counts = jnp.sum(hot, axis=1, keepdims=True)
    groups = jnp.floor((counts + 1.0) * 0.5)
    upto = (
        lax.broadcasted_iota(jnp.int32, (16, 16), 1) <= lax.broadcasted_iota(jnp.int32, (16, 16), 0)
    ).astype(BF16)
    ends = contract(upto, jnp.broadcast_to(groups, (16, REG)).astype(BF16), 1, 0)
    starts = ends - groups
    slot = 2.0 * jnp.sum(hot * starts, axis=0, keepdims=True) + rank
    match = (lax.broadcasted_iota(jnp.int32, (PLAN, REG), 0) == slot.astype(jnp.int32)).astype(BF16)
    which = lax.broadcasted_iota(jnp.int32, (8, REG), 1).astype(F32) - REG
    line = lax.broadcasted_iota(jnp.int32, (8, REG), 0)
    values = jnp.where(line == 0, which, jnp.where(line == 1, rows.astype(F32), 0.0))
    slots = contract(values.astype(BF16), match, 1, 1)
    group = lax.broadcasted_iota(jnp.int32, (16, REG), 1).astype(F32)
    column = jnp.sum((ends <= group).astype(F32), axis=0, keepdims=True)
    column = jnp.minimum(column, blocks - 1.0)
    column = jnp.concatenate([column, column], axis=1)
    line = lax.broadcasted_iota(jnp.int32, (8, PLAN), 0)
    plan_vmem[...] = jnp.where(line == 2, column, slots).astype(jnp.int32)


def tile_products(blocks, plan, vals, msg_ref, acc):
    groups = (REG + blocks) // 2

    def one(g):
        first = plan[0, 2 * g] + REG
        second = plan[0, 2 * g + 1] + REG
        row_a = pl.multiple_of(plan[1, 2 * g] * TILE, TILE)
        row_b = pl.multiple_of(plan[1, 2 * g + 1] * TILE, TILE)
        lhs = jnp.concatenate([vals[first], vals[second]], axis=0)
        rhs = jnp.concatenate([msg_ref[pl.ds(row_a, TILE), :], msg_ref[pl.ds(row_b, TILE), :]], axis=0)
        place = pl.ds(pl.multiple_of(plan[2, g] * TILE, TILE), TILE)
        acc[place, :] += contract(lhs, rhs, 0, 0)

    def body(step, carry):
        for k in range(UNROLL):
            one(step * UNROLL + k)
        return carry

    lax.fori_loop(0, groups // UNROLL, body, 0)
    for g in range(groups // UNROLL * UNROLL, groups):
        one(g)


def load_tiles(region, vals_hbm, vals, sem):
    copy = pltpu.make_async_copy(vals_hbm.at[pl.ds(region * REG, REG)], vals.at[pl.ds(0, REG)], sem)
    copy.start()
    vals[REG] = jnp.zeros((TILE, TILE), BF16)
    return copy


def make_plan(region, rows_ref, cols_ref, plan_vmem, plan, plan_sem, blocks):
    write_plan(region, rows_ref, cols_ref, plan_vmem, blocks)
    copy = pltpu.make_async_copy(plan_vmem, plan, plan_sem)
    copy.start()
    return copy


def hub_kernel(core, rows_ref, cols_ref, deg_ref, cot_ref, w_ref, vals_hbm, msg_ref, keep_ref, send_ref,
               vals, acc, plan_vmem, plan, sem, plan_sem):
    tiles = load_tiles(0, vals_hbm, vals, sem)
    ready = make_plan(0, rows_ref, cols_ref, plan_vmem, plan, plan_sem, HUB_BLOCKS)
    scale = jnp.transpose(1.0 / deg_ref[...].astype(F32))
    for r in range(NODES // TILE):
        part = contract(cot_ref[r * TILE : (r + 1) * TILE, :], w_ref[...], 1, 1)
        msg_ref[r * TILE : (r + 1) * TILE, :] = (part * scale[:, r : r + 1]).astype(BF16)
    acc[...] = jnp.zeros_like(acc)
    ready.wait()
    tiles.wait()
    tile_products(HUB_BLOCKS, plan, vals, msg_ref, acc)
    half = WIDTH // 2

    @pl.when(core[0] == 0)
    def _():
        keep_ref[...] = acc[:, :half]
        send_ref[...] = acc[:, half:]

    @pl.when(core[0] != 0)
    def _():
        keep_ref[...] = acc[:, half:]
        send_ref[...] = acc[:, :half]


def ghost_kernel(rows_ref, cols_ref, msg_ref, vals_hbm, out_ref, vals, acc, plan_vmem, plan, sem, plan_sem):
    tiles = load_tiles(2, vals_hbm, vals, sem)
    ready = make_plan(2, rows_ref, cols_ref, plan_vmem, plan, plan_sem, HUB_BLOCKS)
    acc[...] = jnp.zeros_like(acc)
    ready.wait()
    tiles.wait()
    tile_products(HUB_BLOCKS, plan, vals, msg_ref, acc)
    out_ref[...] = acc[...].astype(BF16)


def own_kernel(rows_ref, cols_ref, msg_ref, cot_ref, w_ref, vals_hbm, out_ref, vals, plan_vmem, plan, sem, plan_sem):
    tiles = load_tiles(1, vals_hbm, vals, sem)
    ready = make_plan(1, rows_ref, cols_ref, plan_vmem, plan, plan_sem, OWN_BLOCKS)
    for r in range(NODES // TILE):
        block = slice(r * TILE, (r + 1) * TILE)
        out_ref[block, :] = contract(cot_ref[block, :], w_ref[...], 1, 1)
    ready.wait()
    tiles.wait()
    tile_products(OWN_BLOCKS, plan, vals, msg_ref, out_ref)


def pack_kernel(keep_ref, came_ref, packed_hbm, out_ref):
    del packed_hbm
    out_ref[...] = (keep_ref[...] + came_ref[...]).astype(BF16)


def weights_kernel(core, feat_ref, agg_ref, cot_ref, keep_ref, send_ref):
    @pl.when(core[0] == 0)
    def _():
        keep_ref[...] = contract(feat_ref[...], cot_ref[...], 0, 0)
        send_ref[...] = contract(agg_ref[...], cot_ref[...], 0, 0)

    @pl.when(core[0] != 0)
    def _():
        keep_ref[...] = contract(agg_ref[...], cot_ref[...], 0, 0)
        send_ref[...] = contract(feat_ref[...], cot_ref[...], 0, 0)


def landing_kernel(targets_ref, own_ref, arrived_ref, nodes_ref, hubs_ref):
    chunk = 256
    slots = arrived_ref.shape[0]
    for s in range(slots // chunk):
        goal = targets_ref[s : s + 1, :]
        place = (lax.broadcasted_iota(jnp.int32, (NODES, chunk), 0) == goal).astype(BF16)
        part = contract(place, arrived_ref[s * chunk : (s + 1) * chunk, :WIDTH], 1, 0)
        if s == 0:
            nodes_ref[...] = own_ref[...] + part
        else:
            nodes_ref[...] += part
    half = WIDTH // 2
    for c in range(2):
        total = jnp.zeros((16, half), F32)
        for y in range(4):
            start = (2 * y + c) * 256
            for m in range(16):
                total += arrived_ref[start + 16 * m : start + 16 * m + 16, WIDTH:].astype(F32)
        hubs_ref[:, c * half : (c + 1) * half] = total


def whole(*shape):
    return pl.BlockSpec(shape, lambda i, *_: (0,) * len(shape))


ANY = pl.BlockSpec(memory_space=pl.ANY)


def call(kernel, name, scalars, ins, outs, shapes, scratch, flops, moved, **more):
    return pl.pallas_call(
        kernel,
        grid_spec=pltpu.PrefetchScalarGridSpec(
            num_scalar_prefetch=scalars, grid=(1,), in_specs=ins, out_specs=outs, scratch_shapes=scratch
        ),
        out_shape=shapes,
        compiler_params=pltpu.CompilerParams(vmem_limit_bytes=VMEM),
        cost_estimate=pl.CostEstimate(flops=flops, bytes_accessed=moved, transcendentals=0),
        name=name,
        **more,
    )


def tile_scratch(acc):
    kept = [pltpu.VMEM((REG + 1, TILE, TILE), BF16)]
    if acc:
        kept.append(pltpu.VMEM((HUB_BLOCKS * TILE, WIDTH), F32))
    return kept + [
        pltpu.VMEM((8, PLAN), jnp.int32),
        pltpu.SMEM((8, PLAN), jnp.int32),
        pltpu.SemaphoreType.DMA,
        pltpu.SemaphoreType.DMA,
    ]


def shift(k, n):
    return [(i, (i + k) % n) for i in range(n)]


def others(pieces, axis):
    return [lax.ppermute(pieces(k), axis, shift(k, 4)) for k in (1, 2, 3)]


def scatter_sum(x, axis, kind):
    me = lax.axis_index(axis)
    parts = x.reshape(4, x.shape[0] // 4, x.shape[1])

    def piece(k):
        return lax.dynamic_index_in_dim(parts, (me + k) % 4, 0, keepdims=False).astype(kind)

    came = others(piece, axis)
    total = lax.dynamic_index_in_dim(parts, me, 0, keepdims=False)
    for part in came:
        total = total + part.astype(F32)
    return total


def by_index(mine, came, axis):
    me = lax.axis_index(axis)
    held = [mine] + came
    out = []
    for i in range(4):
        back = (me - i) % 4
        pick = held[0]
        for k in (1, 2, 3):
            pick = jnp.where(back == k, held[k], pick)
        out.append(pick)
    return out


def gather(x, axis):
    return jnp.concatenate(by_index(x, others(lambda k: x, axis), axis), axis=0)


def all_sum(x, axis):
    a, b, c, d = by_index(x, others(lambda k: x, axis), axis)
    return (a + b) + (c + d)


def local(features, aggregated, cotangent, w_self, w_neigh, degrees, tile_rows, tile_cols, tile_vals, recv_rows):
    core = lax.axis_index("core")
    core_arg = core.reshape(1).astype(jnp.int32)
    rows = tile_rows.reshape(3, REG)
    cols = tile_cols.reshape(3, REG)
    deg = degrees.reshape(NODES // TILE, TILE)
    targets = recv_rows.reshape(8, 256)
    half = WIDTH // 2
    spec_rc = whole(3, REG)
    spec_nodes = whole(NODES, WIDTH)
    spec_w = whole(WIDTH, WIDTH)
    slots = HUB_BLOCKS * TILE
    region_flops = 2 * REG * TILE * TILE * WIDTH
    region_bytes = REG * TILE * TILE * 2 + NODES * WIDTH * 2 + slots * WIDTH * 2

    w_keep, w_send = call(
        weights_kernel, "weights", 1, [spec_nodes] * 3, [spec_w] * 2,
        [jax.ShapeDtypeStruct((WIDTH, WIDTH), F32)] * 2, [], 4 * NODES * WIDTH * WIDTH, 5 << 20,
    )(core_arg, features, aggregated, cotangent)
    w_came = lax.ppermute(w_send, "core", shift(1, 2))

    msg, hub_keep, hub_send = call(
        hub_kernel, "hub", 1,
        [spec_rc, spec_rc, whole(8, TILE), spec_nodes, spec_w, ANY],
        [spec_nodes, whole(slots, half), whole(slots, half)],
        [
            jax.ShapeDtypeStruct((NODES, WIDTH), BF16),
            jax.ShapeDtypeStruct((slots, half), F32),
            jax.ShapeDtypeStruct((slots, half), F32),
        ],
        tile_scratch(True), region_flops + 2 * NODES * WIDTH * WIDTH, region_bytes + (2 << 20),
    )(core_arg, rows, cols, deg, cotangent, w_neigh, tile_vals)
    hub_came = lax.ppermute(hub_send, "core", shift(1, 2))

    packed = call(
        ghost_kernel, "ghost", 0, [spec_rc, spec_rc, spec_nodes, ANY], whole(slots, WIDTH),
        jax.ShapeDtypeStruct((slots, WIDTH + half), BF16),
        tile_scratch(True), region_flops, region_bytes,
    )(rows, cols, msg, tile_vals)
    packed = call(
        pack_kernel, "pack", 0, [whole(slots, half), whole(slots, half), ANY],
        pl.BlockSpec((slots, half), lambda i: (0, 2)),
        jax.ShapeDtypeStruct((slots, WIDTH + half), BF16),
        [], slots * half, 5 << 20, input_output_aliases={2: 0},
    )(hub_keep, hub_came, packed)
    arrived = lax.all_to_all(
        packed.reshape(128, 16, WIDTH + half), ALL, split_axis=0, concat_axis=0, tiled=True
    ).reshape(slots, WIDTH + half)

    own = call(
        own_kernel, "own", 0, [spec_rc, spec_rc, spec_nodes, spec_nodes, spec_w, ANY], spec_nodes,
        jax.ShapeDtypeStruct((NODES, WIDTH), F32),
        tile_scratch(False), region_flops + 2 * NODES * WIDTH * WIDTH, region_bytes,
    )(rows, cols, msg, cotangent, w_self, tile_vals)

    mine = w_keep + w_came
    mine = scatter_sum(mine, "x", BF16)
    mine = scatter_sum(mine, "z", F32)
    mine = all_sum(mine, "y").astype(BF16)
    mine = gather(gather(mine, "z"), "x")
    other = lax.ppermute(mine, "core", shift(1, 2))
    grad_weights = jnp.where(
        core == 0, jnp.stack([mine, other]), jnp.stack([other, mine])
    ).astype(F32)

    grad_nodes, grad_hubs = call(
        landing_kernel, "landing", 0,
        [whole(8, 256), spec_nodes, whole(slots, WIDTH + half)],
        [spec_nodes, whole(16, WIDTH)],
        [jax.ShapeDtypeStruct((NODES, WIDTH), F32), jax.ShapeDtypeStruct((16, WIDTH), F32)],
        [], 2 * slots * NODES * WIDTH, 7 << 20,
    )(targets, own, arrived)
    return (grad_nodes, grad_hubs, grad_weights)


def solution(mesh):
    fine = Mesh(mesh.devices.reshape(4, 2, 4, 4), ALL)
    rows = P(ALL, None)
    in_specs = (
        rows, rows, rows, P(), P(), P(ALL), P(ALL), P(ALL), P(ALL, None, None), P(ALL, None, None),
    )
    out_specs = (rows, rows, P())
    return jax.shard_map(local, mesh=fine, in_specs=in_specs, out_specs=out_specs, check_vma=False)
```

time: 834 us -> 150 us (0.18)
  the two profiles are of different devices: /device:TPU:0 before, /device:TPU:1 now
where the time goes in v1:
time: 150 us; the launch traced here: 149 us
  waiting for transfers between devices  51.3 us (34%)
  Pallas kernels  44.4 us (30%)
  starting transfers between devices  35.3 us (24%)
  other arithmetic  10.2 us (7%)
  local copies, waits for them, and re-layouts  7.43 us (5%)
    ppermute x15, waiting for transfers between devices, others(): return [lax.ppermute(pieces(k), axis, shift(k, 4)) for k in (1, 2, 3)]  51.3 us
    ppermute x15, starting transfers between devices, others(): return [lax.ppermute(pieces(k), axis, shift(k, 4)) for k in (1, 2, 3)]  16.9 us
    all_to_all x1, starting transfers between devices, local(): lax.all_to_all(packed.reshape(128, 16, WIDTH + half), ALL, split_axis=0,...  10.6 us
    pallas_call x1, Pallas kernels, local(): call(hub_kernel, 'hub', 1, [spec_rc, spec_rc, whole(8, TILE), spec_nodes,...  10.5 us
    pallas_call x1, Pallas kernels, local(): call(ghost_kernel, 'ghost', 0, [spec_rc, spec_rc, spec_nodes, ANY], whole...  10 us
    pallas_call x1, Pallas kernels, local(): call(own_kernel, 'own', 0, [spec_rc, spec_rc, spec_nodes, spec_nodes, spe...  9.7 us
    ppermute x1, starting transfers between devices, local(): other = lax.ppermute(mine, 'core', shift(1, 2))  6.22 us
    pallas_call x1, Pallas kernels, local(): call(landing_kernel, 'landing', 0, [whole(8, 256), spec_nodes, whole(slot...  6.18 us
  transfers between devices with their start and end apart: 19, of which 14 were waited for; matrix products, arithmetic and copies ran while one was open for 8% of the time, Pallas kernels for 19%

profile of v1, /device:TPU:1, one launch (start us, length us, event | category | flops | bytes accessed | tf_op | source)
XLA Modules:
  0.0 149.5 jit_solution(692183858459430863)
XLA Ops:
  0.6 10.5 %hub.1 = (bf16[1024,512]{1,0:T(8,128)(2,1)}, f32[2048,256]{1,0:T(8,128)}, f32[2048,256]{1,0:T(8,128)}) custom-call(s32[1]{0:T(128)} %bitcast.2.core, s32[3,128]{1,0:T(4,128)} %bitcast.41, s32[3,128]{1,0:T(4,128)} %bitcast.44, s32[8,128]{1,0:T(8,128)} %bitcast.47, bf16[1024,512]{1,0:T(8,128)(2,1)} %cot_ref.5, bf16[512,512]{1,0:T(8,128)(2,1)} %w_ref.2, ...), custom_call_target="tpu_custom_call" | custom-call | flops 2684354560 | bytes 9437184 | tf_op jit(solution)/shard_map/hub/pallas_call | solution.py:276
  11.2 1.5 %collective-permute-start = (f32[2048,256]{1,0:T(8,128)}, f32[2048,256]{1,0:T(8,128)S(1)}, u32[]{:S(2)}, u32[]{:S(2)}) collective-permute-start(f32[2048,256]{1,0:T(8,128)} %get-tuple-element.12), channel_id=1, source_target_pairs={{0,16},{16,0},{1,17},{17,1},{2,18},{18,2},{3,19},{19,3},{4,20},{20... | collective-permute-start | bytes 6291464 | tf_op jit(solution)/shard_map/ppermute | solution.py:287
  12.7 4.5 %weights.1 = (f32[512,512]{1,0:T(8,128)}, f32[512,512]{1,0:T(8,128)}) custom-call(s32[1]{0:T(128)} %bitcast.2.core, bf16[1024,512]{1,0:T(8,128)(2,1)} %feat_ref.1, bf16[1024,512]{1,0:T(8,128)(2,1)} %agg_ref.1, bf16[1024,512]{1,0:T(8,128)(2,1)} %cot_ref.5), custom_call_target="tpu_custom_call" | custom-call | flops 1073741824 | bytes 5242880 | tf_op jit(solution)/shard_map/weights/pallas_call | solution.py:270
  17.2 10.0 %ghost.1.packed_hbm = bf16[2048,768]{1,0:T(8,128)(2,1)} custom-call(s32[3,128]{1,0:T(4,128)} %bitcast.42, s32[3,128]{1,0:T(4,128)} %bitcast.45, bf16[1024,512]{1,0:T(8,128)(2,1)} %get-tuple-element.10.msg_ref, bf16[384,128,128]{2,1,0:T(8,128)(2,1)} %vals_hbm.5), custom_call_target="tpu_custom_call" | custom-call | flops 2147483648 | bytes 7340032 | tf_op jit(solution)/shard_map/ghost/pallas_call | solution.py:289
  27.2 1.3 copy-done.2
  28.5 3.5 %pack.1 = bf16[2048,768]{1,0:T(8,128)(2,1)} custom-call(f32[2048,256]{1,0:T(8,128)} %get-tuple-element.11.keep_ref, f32[2048,256]{1,0:T(8,128)} %copy-done.2, bf16[2048,768]{1,0:T(8,128)(2,1)} %ghost.1.packed_hbm), custom_call_target="tpu_custom_call", output_to_operand_aliasing={{}: (2, {})} | custom-call | flops 524288 | bytes 5242880 | tf_op jit(solution)/shard_map/pack/pallas_call | solution.py:294
  32.0 10.6 %all-to-all-start = ((bf16[128,16,768]{2,1,0:T(8,128)(2,1)}), bf16[128,16,768]{2,1,0:T(8,128)(2,1)S(1)}, u32[]{:S(2)}, u32[]{:S(2)}) async-start(bf16[128,16,768]{2,1,0:T(8,128)(2,1)} %bitcast.35), calls=%async_computation | async-start | bytes 6291456 | tf_op jit(solution)/shard_map/all_to_all | solution.py:300
  42.7 1.7 %add.141 = f32[512,512]{1,0:T(8,128)S(1)} add(f32[512,512]{1,0:T(8,128)} %get-tuple-element.15, f32[512,512]{1,0:T(8,128)} %collective-permute-done.1) | non-fusion elementwise | flops 262144 | bytes 3145728 | tf_op jit(solution)/shard_map/add | solution.py:310
  44.4 1.0 copy-done.1
  45.4 0.7 fusion.3
  46.1 2.6 %collective-permute-start.4 = (bf16[128,512]{1,0:T(8,128)(2,1)}, bf16[128,512]{1,0:T(8,128)(2,1)S(1)}, u32[]{:S(2)}, u32[]{:S(2)}) collective-permute-start(bf16[128,512]{1,0:T(8,128)(2,1)} %get-tuple-element.18), channel_id=1, source_target_pairs={{0,3},{1,0},{2,1},{3,2},{4,7},{5,4},{6,5},{7,6},{8,11},{9,8},{10,9... | collective-permute-start | bytes 393224 | tf_op jit(solution)/shard_map/ppermute | solution.py:216
  49.9 30.7 %collective-permute-done.4 = bf16[128,512]{1,0:T(8,128)(2,1)S(1)} collective-permute-done((bf16[128,512]{1,0:T(8,128)(2,1)}, bf16[128,512]{1,0:T(8,128)(2,1)S(1)}, u32[]{:S(2)}, u32[]{:S(2)}) %collective-permute-start.4) | collective-permute-done | bytes 131104 | tf_op jit(solution)/shard_map/ppermute | solution.py:216
  80.6 1.5 %collective-permute-done.3 = bf16[128,512]{1,0:T(8,128)(2,1)S(1)} collective-permute-done((bf16[128,512]{1,0:T(8,128)(2,1)}, bf16[128,512]{1,0:T(8,128)(2,1)S(1)}, u32[]{:S(2)}, u32[]{:S(2)}) %collective-permute-start.3) | collective-permute-done | bytes 131104 | tf_op jit(solution)/shard_map/ppermute | solution.py:216
  82.1 0.7 copy-done.8
  82.8 2.0 %collective-permute-done.2 = bf16[128,512]{1,0:T(8,128)(2,1)} collective-permute-done((bf16[128,512]{1,0:T(8,128)(2,1)S(1)}, bf16[128,512]{1,0:T(8,128)(2,1)}, u32[]{:S(2)}, u32[]{:S(2)}) %collective-permute-start.2) | collective-permute-done | bytes 131104 | tf_op jit(solution)/shard_map/ppermute | solution.py:216
  84.8 1.1 fusion.2
  85.9 0.7 dynamic-slice_bitcast_fusion.2
  86.6 3.1 %collective-permute-start.7 = (f32[32,512]{1,0:T(8,128)}, f32[32,512]{1,0:T(8,128)S(1)}, u32[]{:S(2)}, u32[]{:S(2)}) collective-permute-start(f32[32,512]{1,0:T(8,128)} %get-tuple-element.27), channel_id=1, source_target_pairs={{0,12},{4,0},{8,4},{12,8},{1,13},{5,1},{9,5},{13,9},{2,14},{6,2},{... | collective-permute-start | bytes 196616 | tf_op jit(solution)/shard_map/ppermute | solution.py:216
  89.7 0.8 collective-permute-start.5
  90.6 0.8 collective-permute-done.7
  91.3 3.3 %collective-permute-done.6 = f32[32,512]{1,0:T(8,128)S(1)} collective-permute-done((f32[32,512]{1,0:T(8,128)}, f32[32,512]{1,0:T(8,128)S(1)}, u32[]{:S(2)}, u32[]{:S(2)}) %collective-permute-start.6) | collective-permute-done | bytes 65568 | tf_op jit(solution)/shard_map/ppermute | solution.py:216
  94.6 0.6 copy-done.9
  95.3 0.9 fusion.7
  96.2 2.7 %collective-permute-start.8 = (f32[32,512]{1,0:T(8,128)S(1)}, f32[32,512]{1,0:T(8,128)S(1)}, u32[]{:S(2)}, u32[]{:S(2)}) collective-permute-start(f32[32,512]{1,0:T(8,128)S(1)} %fusion.7), channel_id=1, source_target_pairs={{0,96},{32,0},{64,32},{96,64},{1,97},{33,1},{65,33},{97,65},{2,98}... | collective-permute-start | bytes 196616 | tf_op jit(solution)/shard_map/ppermute | solution.py:216
  99.3 0.6 collective-permute-start.10
  100.2 3.3 %collective-permute-done.9 = f32[32,512]{1,0:T(8,128)S(1)} collective-permute-done((f32[32,512]{1,0:T(8,128)S(1)}, f32[32,512]{1,0:T(8,128)S(1)}, u32[]{:S(2)}, u32[]{:S(2)}) %collective-permute-start.9) | collective-permute-done | bytes 65568 | tf_op jit(solution)/shard_map/ppermute | solution.py:216
  103.5 0.6 collective-permute-done.10
  104.2 0.6 collective-permute-start.11
  104.8 1.1 collective-permute-start.12
  105.9 0.8 collective-permute-start.13
  106.7 0.7 collective-permute-done.11
  107.3 1.7 %collective-permute-done.12 = bf16[32,512]{1,0:T(8,128)(2,1)S(1)} collective-permute-done((bf16[32,512]{1,0:T(8,128)(2,1)S(1)}, bf16[32,512]{1,0:T(8,128)(2,1)S(1)}, u32[]{:S(2)}, u32[]{:S(2)}) %collective-permute-start.12) | collective-permute-done | bytes 32800 | tf_op jit(solution)/shard_map/ppermute | solution.py:216
  109.1 0.8 collective-permute-done.13
  109.9 0.7 pad_maximum_fusion.1
  110.6 1.7 %collective-permute-start.14 = (bf16[128,512]{1,0:T(8,128)(2,1)}, bf16[128,512]{1,0:T(8,128)(2,1)S(1)}, u32[]{:S(2)}, u32[]{:S(2)}) collective-permute-start(bf16[128,512]{1,0:T(8,128)(2,1)} %pad_maximum_fusion.1), channel_id=1, source_target_pairs={{0,3},{1,0},{2,1},{3,2},{4,7},{5,4},{6,5},{7,6},{8,11},{9,8},{10,9... | collective-permute-start | bytes 393224 | tf_op jit(solution)/shard_map/ppermute | solution.py:216
  112.3 1.2 collective-permute-start.15
  113.7 2.3 %collective-permute-done.14 = bf16[128,512]{1,0:T(8,128)(2,1)S(1)} collective-permute-done((bf16[128,512]{1,0:T(8,128)(2,1)}, bf16[128,512]{1,0:T(8,128)(2,1)S(1)}, u32[]{:S(2)}, u32[]{:S(2)}) %collective-permute-start.14) | collective-permute-done | bytes 131104 | tf_op jit(solution)/shard_map/ppermute | solution.py:216
  116.0 1.9 %collective-permute-done.15 = bf16[128,512]{1,0:T(8,128)(2,1)S(1)} collective-permute-done((bf16[128,512]{1,0:T(8,128)(2,1)}, bf16[128,512]{1,0:T(8,128)(2,1)S(1)}, u32[]{:S(2)}, u32[]{:S(2)}) %collective-permute-start.15) | collective-permute-done | bytes 131104 | tf_op jit(solution)/shard_map/ppermute | solution.py:216
  117.9 1.4 collective-permute-done.16
  119.3 0.9 select_select_fusion.3
  120.2 0.9 select_select_fusion.2
  121.1 1.0 fusion.8
  122.1 6.2 %collective-permute-start.17 = (bf16[512,512]{1,0:T(8,128)(2,1)}, bf16[512,512]{1,0:T(8,128)(2,1)}, u32[]{:S(2)}, u32[]{:S(2)}) collective-permute-start(bf16[512,512]{1,0:T(8,128)(2,1)} %get-tuple-element.21), channel_id=1, source_target_pairs={{0,16},{16,0},{1,17},{17,1},{2,18},{18,2},{3,19},{19,3},{4,20},{20... | collective-permute-start | bytes 1572872 | tf_op jit(solution)/shard_map/ppermute | solution.py:315
  128.4 0.7 reshape.36.targets_ref
  129.1 9.7 %own.1.own_ref = f32[1024,512]{1,0:T(8,128)} custom-call(s32[3,128]{1,0:T(4,128)} %bitcast.43, s32[3,128]{1,0:T(4,128)} %bitcast.46, bf16[1024,512]{1,0:T(8,128)(2,1)} %get-tuple-element.10.msg_ref, bf16[1024,512]{1,0:T(8,128)(2,1)} %cot_ref.5, bf16[512,512]{1,0:T(8,128)(2,1)} %w_ref.3, bf16[384,128,128]{2,1,0:T(8,128)(2,1)} %vals_hbm.5), custom_call_target="tpu_custom_call" | custom-call | flops 2684354560 | bytes 7340032 | tf_op jit(solution)/shard_map/own/pallas_call | solution.py:304
  138.9 2.8 %fusion = f32[2,512,512]{2,1,0:T(8,128)} fusion(bf16[1,512,512]{2,1,0:T(8,128)(2,1)} %bitcast.17, bf16[1,512,512]{2,1,0:T(8,128)(2,1)S(1)} %copy-done.3, pred[]{:T(512)S(6)} %eq.130), kind=kLoop, calls=%fused_computation.1 | loop fusion | flops 2097152 | bytes 3145729 | tf_op jit(solution)/shard_map/convert_element_type | solution.py:318
  141.7 1.6 %copy-done = bf16[128,16,768]{2,1,0:T(8,128)(2,1)} copy-done((bf16[128,16,768]{2,1,0:T(8,128)(2,1)}, bf16[128,16,768]{2,1,0:T(8,128)(2,1)S(1)}, u32[]{:S(2)}) %copy-start) | copy-done | bytes 3145752
  143.3 6.2 %landing.1 = (f32[1024,512]{1,0:T(8,128)}, f32[16,512]{1,0:T(8,128)}) custom-call(s32[8,256]{1,0:T(8,128)} %reshape.36.targets_ref, f32[1024,512]{1,0:T(8,128)} %own.1.own_ref, bf16[2048,768]{1,0:T(8,128)(2,1)} %bitcast.36), custom_call_target="tpu_custom_call" | custom-call | flops 2147483648 | bytes 7340032 | tf_op jit(solution)/shard_map/landing/pallas_call | solution.py:320
  (32 shorter events, 2.2 us)
Async XLA Ops:
  11.2 16.0 %collective-permute-start = (f32[2048,256]{1,0:T(8,128)}, f32[2048,256]{1,0:T(8,128)S(1)}, u32[]{:S(2)}, u32[]{:S(2)}) collective-permute-start(f32[2048,256]{1,0:T(8,128)} %get-tuple-element.12), channel_id=1, source_target_pairs={{0,16},{16,0},{1,17},{17,1},{2,18},{18,2},{3,19},{19,3},{4,20},{20... | collective-permute-start | bytes 6291464 | tf_op jit(solution)/shard_map/ppermute | solution.py:287
  17.1 25.5 %collective-permute-start.1 = (f32[512,512]{1,0:T(8,128)}, f32[512,512]{1,0:T(8,128)}, u32[]{:S(2)}, u32[]{:S(2)}) collective-permute-start(f32[512,512]{1,0:T(8,128)} %get-tuple-element.16), channel_id=1, source_target_pairs={{0,16},{16,0},{1,17},{17,1},{2,18},{18,2},{3,19},{19,3},{4,20},{20... | collective-permute-start | bytes 3145736 | tf_op jit(solution)/shard_map/ppermute | solution.py:274
  27.2 1.3 copy-start.2
  32.0 109.7 %all-to-all-start = ((bf16[128,16,768]{2,1,0:T(8,128)(2,1)}), bf16[128,16,768]{2,1,0:T(8,128)(2,1)S(1)}, u32[]{:S(2)}, u32[]{:S(2)}) async-start(bf16[128,16,768]{2,1,0:T(8,128)(2,1)} %bitcast.35), calls=%async_computation | async-start | bytes 6291456 | tf_op jit(solution)/shard_map/all_to_all | solution.py:300
  44.4 1.0 copy-start.1
  46.1 34.5 %collective-permute-start.4 = (bf16[128,512]{1,0:T(8,128)(2,1)}, bf16[128,512]{1,0:T(8,128)(2,1)S(1)}, u32[]{:S(2)}, u32[]{:S(2)}) collective-permute-start(bf16[128,512]{1,0:T(8,128)(2,1)} %get-tuple-element.18), channel_id=1, source_target_pairs={{0,3},{1,0},{2,1},{3,2},{4,7},{5,4},{6,5},{7,6},{8,11},{9,8},{10,9... | collective-permute-start | bytes 393224 | tf_op jit(solution)/shard_map/ppermute | solution.py:216
  48.7 33.4 %collective-permute-start.3 = (bf16[128,512]{1,0:T(8,128)(2,1)}, bf16[128,512]{1,0:T(8,128)(2,1)S(1)}, u32[]{:S(2)}, u32[]{:S(2)}) collective-permute-start(bf16[128,512]{1,0:T(8,128)(2,1)} %get-tuple-element.19), channel_id=1, source_target_pairs={{0,2},{1,3},{2,0},{3,1},{4,6},{5,7},{6,4},{7,5},{8,10},{9,11},{10,... | collective-permute-start | bytes 393224 | tf_op jit(solution)/shard_map/ppermute | solution.py:216
  49.3 35.4 %collective-permute-start.2 = (bf16[128,512]{1,0:T(8,128)(2,1)S(1)}, bf16[128,512]{1,0:T(8,128)(2,1)}, u32[]{:S(2)}, u32[]{:S(2)}) collective-permute-start(bf16[128,512]{1,0:T(8,128)(2,1)S(1)} %get-tuple-element.17), channel_id=1, source_target_pairs={{0,1},{1,2},{2,3},{3,0},{4,5},{5,6},{6,7},{7,4},{8,9},{9,10},{10,1... | collective-permute-start | bytes 393224 | tf_op jit(solution)/shard_map/ppermute | solution.py:216
  82.1 0.7 copy-start.8
  86.6 4.8 %collective-permute-start.7 = (f32[32,512]{1,0:T(8,128)}, f32[32,512]{1,0:T(8,128)S(1)}, u32[]{:S(2)}, u32[]{:S(2)}) collective-permute-start(f32[32,512]{1,0:T(8,128)} %get-tuple-element.27), channel_id=1, source_target_pairs={{0,12},{4,0},{8,4},{12,8},{1,13},{5,1},{9,5},{13,9},{2,14},{6,2},{... | collective-permute-start | bytes 196616 | tf_op jit(solution)/shard_map/ppermute | solution.py:216
  89.7 4.9 %collective-permute-start.6 = (f32[32,512]{1,0:T(8,128)}, f32[32,512]{1,0:T(8,128)S(1)}, u32[]{:S(2)}, u32[]{:S(2)}) collective-permute-start(f32[32,512]{1,0:T(8,128)} %get-tuple-element.28), channel_id=1, source_target_pairs={{0,8},{4,12},{8,0},{12,4},{1,9},{5,13},{9,1},{13,5},{2,10},{6,14},... | collective-permute-start | bytes 196616 | tf_op jit(solution)/shard_map/ppermute | solution.py:216
  89.7 5.5 %collective-permute-start.5 = (f32[32,512]{1,0:T(8,128)}, f32[32,512]{1,0:T(8,128)}, u32[]{:S(2)}, u32[]{:S(2)}) collective-permute-start(f32[32,512]{1,0:T(8,128)} %get-tuple-element.26), channel_id=1, source_target_pairs={{0,4},{4,8},{8,12},{12,0},{1,5},{5,9},{9,13},{13,1},{2,6},{6,10},{... | collective-permute-start | bytes 196616 | tf_op jit(solution)/shard_map/ppermute | solution.py:216
  94.6 0.6 copy-start.9
  96.2 4.0 %collective-permute-start.8 = (f32[32,512]{1,0:T(8,128)S(1)}, f32[32,512]{1,0:T(8,128)S(1)}, u32[]{:S(2)}, u32[]{:S(2)}) collective-permute-start(f32[32,512]{1,0:T(8,128)S(1)} %fusion.7), channel_id=1, source_target_pairs={{0,96},{32,0},{64,32},{96,64},{1,97},{33,1},{65,33},{97,65},{2,98}... | collective-permute-start | bytes 196616 | tf_op jit(solution)/shard_map/ppermute | solution.py:216
  98.8 4.7 %collective-permute-start.9 = (f32[32,512]{1,0:T(8,128)S(1)}, f32[32,512]{1,0:T(8,128)S(1)}, u32[]{:S(2)}, u32[]{:S(2)}) collective-permute-start(f32[32,512]{1,0:T(8,128)S(1)} %fusion.7), channel_id=1, source_target_pairs={{0,64},{32,96},{64,0},{96,32},{1,65},{33,97},{65,1},{97,33},{2,66}... | collective-permute-start | bytes 196616 | tf_op jit(solution)/shard_map/ppermute | solution.py:216
  99.3 4.9 %collective-permute-start.10 = (f32[32,512]{1,0:T(8,128)S(1)}, f32[32,512]{1,0:T(8,128)S(1)}, u32[]{:S(2)}, u32[]{:S(2)}) collective-permute-start(f32[32,512]{1,0:T(8,128)S(1)} %fusion.7), channel_id=1, source_target_pairs={{0,32},{32,64},{64,96},{96,0},{1,33},{33,65},{65,97},{97,1},{2,34}... | collective-permute-start | bytes 196616 | tf_op jit(solution)/shard_map/ppermute | solution.py:216
  99.9 28.4 %copy-start.10 = (s32[1,128,16]{1,2,0:T(8,128)S(1)}, s32[1,128,16]{1,2,0:T(8,128)}, u32[]{:S(2)}) copy-start(s32[1,128,16]{1,2,0:T(8,128)} %param.19) | copy-start | bytes 24580
  104.2 3.1 %collective-permute-start.11 = (bf16[32,512]{1,0:T(8,128)(2,1)S(1)}, bf16[32,512]{1,0:T(8,128)(2,1)S(1)}, u32[]{:S(2)}, u32[]{:S(2)}) collective-permute-start(bf16[32,512]{1,0:T(8,128)(2,1)S(1)} %add_convert_fusion), channel_id=1, source_target_pairs={{0,12},{4,0},{8,4},{12,8},{1,13},{5,1},{9,5},{13,9},{2,14},{6,2},{... | collective-permute-start | bytes 98312 | tf_op jit(solution)/shard_map/ppermute | solution.py:216
  104.8 4.3 %collective-permute-start.12 = (bf16[32,512]{1,0:T(8,128)(2,1)S(1)}, bf16[32,512]{1,0:T(8,128)(2,1)S(1)}, u32[]{:S(2)}, u32[]{:S(2)}) collective-permute-start(bf16[32,512]{1,0:T(8,128)(2,1)S(1)} %add_convert_fusion), channel_id=1, source_target_pairs={{0,8},{4,12},{8,0},{12,4},{1,9},{5,13},{9,1},{13,5},{2,10},{6,14},... | collective-permute-start | bytes 98312 | tf_op jit(solution)/shard_map/ppermute | solution.py:216
  105.9 4.0 %collective-permute-start.13 = (bf16[32,512]{1,0:T(8,128)(2,1)S(1)}, bf16[32,512]{1,0:T(8,128)(2,1)S(1)}, u32[]{:S(2)}, u32[]{:S(2)}) collective-permute-start(bf16[32,512]{1,0:T(8,128)(2,1)S(1)} %add_convert_fusion), channel_id=1, source_target_pairs={{0,4},{4,8},{8,12},{12,0},{1,5},{5,9},{9,13},{13,1},{2,6},{6,10},{... | collective-permute-start | bytes 98312 | tf_op jit(solution)/shard_map/ppermute | solution.py:216
  109.9 2.4 %copy-start.4 = (bf16[32,512]{1,0:T(8,128)(2,1)}, bf16[32,512]{1,0:T(8,128)(2,1)S(1)}, u32[]{:S(2)}) copy-start(bf16[32,512]{1,0:T(8,128)(2,1)S(1)} %get-tuple-element.29) | copy-start | bytes 98308
  109.9 3.6 %copy-start.5 = (bf16[32,512]{1,0:T(8,128)(2,1)}, bf16[32,512]{1,0:T(8,128)(2,1)S(1)}, u32[]{:S(2)}) copy-start(bf16[32,512]{1,0:T(8,128)(2,1)S(1)} %get-tuple-element.30) | copy-start | bytes 98308
  109.9 3.6 %copy-start.6 = (bf16[32,512]{1,0:T(8,128)(2,1)}, bf16[32,512]{1,0:T(8,128)(2,1)S(1)}, u32[]{:S(2)}) copy-start(bf16[32,512]{1,0:T(8,128)(2,1)S(1)} %get-tuple-element.31) | copy-start | bytes 98308
  109.9 3.6 %copy-start.7 = (bf16[32,512]{1,0:T(8,128)(2,1)}, bf16[32,512]{1,0:T(8,128)(2,1)S(1)}, u32[]{:S(2)}) copy-start(bf16[32,512]{1,0:T(8,128)(2,1)S(1)} %get-tuple-element.32) | copy-start | bytes 98308
  110.6 5.4 %collective-permute-start.14 = (bf16[128,512]{1,0:T(8,128)(2,1)}, bf16[128,512]{1,0:T(8,128)(2,1)S(1)}, u32[]{:S(2)}, u32[]{:S(2)}) collective-permute-start(bf16[128,512]{1,0:T(8,128)(2,1)} %pad_maximum_fusion.1), channel_id=1, source_target_pairs={{0,3},{1,0},{2,1},{3,2},{4,7},{5,4},{6,5},{7,6},{8,11},{9,8},{10,9... | collective-permute-start | bytes 393224 | tf_op jit(solution)/shard_map/ppermute | solution.py:216
  112.3 5.6 %collective-permute-start.15 = (bf16[128,512]{1,0:T(8,128)(2,1)}, bf16[128,512]{1,0:T(8,128)(2,1)S(1)}, u32[]{:S(2)}, u32[]{:S(2)}) collective-permute-start(bf16[128,512]{1,0:T(8,128)(2,1)} %pad_maximum_fusion.1), channel_id=1, source_target_pairs={{0,2},{1,3},{2,0},{3,1},{4,6},{5,7},{6,4},{7,5},{8,10},{9,11},{10,... | collective-permute-start | bytes 393224 | tf_op jit(solution)/shard_map/ppermute | solution.py:216
  113.5 5.7 %collective-permute-start.16 = (bf16[128,512]{1,0:T(8,128)(2,1)}, bf16[128,512]{1,0:T(8,128)(2,1)S(1)}, u32[]{:S(2)}, u32[]{:S(2)}) collective-permute-start(bf16[128,512]{1,0:T(8,128)(2,1)} %pad_maximum_fusion.1), channel_id=1, source_target_pairs={{0,1},{1,2},{2,3},{3,0},{4,5},{5,6},{6,7},{7,4},{8,9},{9,10},{10,1... | collective-permute-start | bytes 393224 | tf_op jit(solution)/shard_map/ppermute | solution.py:216
  122.1 16.7 %collective-permute-start.17 = (bf16[512,512]{1,0:T(8,128)(2,1)}, bf16[512,512]{1,0:T(8,128)(2,1)}, u32[]{:S(2)}, u32[]{:S(2)}) collective-permute-start(bf16[512,512]{1,0:T(8,128)(2,1)} %get-tuple-element.21), channel_id=1, source_target_pairs={{0,16},{16,0},{1,17},{17,1},{2,18},{18,2},{3,19},{19,3},{4,20},{20... | collective-permute-start | bytes 1572872 | tf_op jit(solution)/shard_map/ppermute | solution.py:315
  129.1 9.7 %copy-start.3 = (bf16[1,512,512]{2,1,0:T(8,128)(2,1)S(1)}, bf16[1,512,512]{2,1,0:T(8,128)(2,1)}, u32[]{:S(2)}) copy-start(bf16[1,512,512]{2,1,0:T(8,128)(2,1)} %get-tuple-element.20) | copy-start | bytes 1572868
  141.7 1.6 %copy-start = (bf16[128,16,768]{2,1,0:T(8,128)(2,1)}, bf16[128,16,768]{2,1,0:T(8,128)(2,1)S(1)}, u32[]{:S(2)}) copy-start(bf16[128,16,768]{2,1,0:T(8,128)(2,1)S(1)} %all-to-all-done) | copy-start | bytes 9437188

commit v2 on v1

v2 whole, which is shorter than its diff:
```python
import functools

import jax
import jax.numpy as jnp
from jax import lax
from jax.experimental import pallas as pl
from jax.experimental.pallas import tpu as pltpu
from jax.sharding import Mesh, PartitionSpec as P

F32 = jnp.float32
BF16 = jnp.bfloat16
ALL = ("y", "core", "z", "x")
TILE = 128
REG = 128
WIDTH = 512
NODES = 1024
HUB_BLOCKS = 16
OWN_BLOCKS = 8
UNROLL = 8
PLAN = 256
VMEM = 56 << 20


def contract(a, b, da, db):
    return lax.dot_general(a, b, (((da,), (db,)), ((), ())), preferred_element_type=F32)


def write_plan(region, rows_ref, cols_ref, plan_vmem, blocks):
    cols = cols_ref[region : region + 1, :]
    rows = rows_ref[region : region + 1, :]
    hot = (lax.broadcasted_iota(jnp.int32, (16, REG), 0) == cols).astype(F32)
    before = (
        lax.broadcasted_iota(jnp.int32, (REG, REG), 0) < lax.broadcasted_iota(jnp.int32, (REG, REG), 1)
    ).astype(BF16)
    rank = jnp.sum(hot * contract(hot.astype(BF16), before, 1, 0), axis=0, keepdims=True)
    counts = jnp.sum(hot, axis=1, keepdims=True)
    groups = jnp.floor((counts + 1.0) * 0.5)
    upto = (
        lax.broadcasted_iota(jnp.int32, (16, 16), 1) <= lax.broadcasted_iota(jnp.int32, (16, 16), 0)
    ).astype(BF16)
    ends = contract(upto, jnp.broadcast_to(groups, (16, REG)).astype(BF16), 1, 0)
    starts = ends - groups
    slot = 2.0 * jnp.sum(hot * starts, axis=0, keepdims=True) + rank
    match = (lax.broadcasted_iota(jnp.int32, (PLAN, REG), 0) == slot.astype(jnp.int32)).astype(BF16)
    which = lax.broadcasted_iota(jnp.int32, (8, REG), 1).astype(F32) - REG
    line = lax.broadcasted_iota(jnp.int32, (8, REG), 0)
    values = jnp.where(line == 0, which, jnp.where(line == 1, rows.astype(F32), 0.0))
    slots = contract(values.astype(BF16), match, 1, 1)
    group = lax.broadcasted_iota(jnp.int32, (16, REG), 1).astype(F32)
    column = jnp.sum((ends <= group).astype(F32), axis=0, keepdims=True)
    column = jnp.minimum(column, blocks - 1.0)
    column = jnp.concatenate([column, column], axis=1)
    line = lax.broadcasted_iota(jnp.int32, (8, PLAN), 0)
    plan_vmem[...] = jnp.where(line == 2, column, slots).astype(jnp.int32)


def tile_products(blocks, plan, vals, msg_ref, acc):
    groups = (REG + blocks) // 2

    def one(g):
        first = plan[0, 2 * g] + REG
        second = plan[0, 2 * g + 1] + REG
        row_a = pl.multiple_of(plan[1, 2 * g] * TILE, TILE)
        row_b = pl.multiple_of(plan[1, 2 * g + 1] * TILE, TILE)
        lhs = jnp.concatenate([vals[first], vals[second]], axis=0)
        rhs = jnp.concatenate([msg_ref[pl.ds(row_a, TILE), :], msg_ref[pl.ds(row_b, TILE), :]], axis=0)
        place = pl.ds(pl.multiple_of(plan[2, g] * TILE, TILE), TILE)
        acc[place, :] += contract(lhs, rhs, 0, 0)

    def body(step, carry):
        for k in range(UNROLL):
            one(step * UNROLL + k)
        return carry

    lax.fori_loop(0, groups // UNROLL, body, 0)
    for g in range(groups // UNROLL * UNROLL, groups):
        one(g)


def load_tiles(region, vals_hbm, vals, sem):
    copy = pltpu.make_async_copy(vals_hbm.at[pl.ds(region * REG, REG)], vals.at[pl.ds(0, REG)], sem)
    copy.start()
    vals[REG] = jnp.zeros((TILE, TILE), BF16)
    return copy


def make_plan(region, rows_ref, cols_ref, plan_vmem, plan, plan_sem, blocks):
    write_plan(region, rows_ref, cols_ref, plan_vmem, blocks)
    copy = pltpu.make_async_copy(plan_vmem, plan, plan_sem)
    copy.start()
    return copy


def ghost_kernel(rows_ref, cols_ref, deg_ref, cot_ref, w_ref, vals_hbm, msg_ref, out_ref,
                 vals, acc, plan_vmem, plan, sem, plan_sem):
    tiles = load_tiles(2, vals_hbm, vals, sem)
    ready = make_plan(2, rows_ref, cols_ref, plan_vmem, plan, plan_sem, HUB_BLOCKS)
    scale = jnp.transpose(1.0 / deg_ref[...].astype(F32))
    for r in range(NODES // TILE):
        part = contract(cot_ref[r * TILE : (r + 1) * TILE, :], w_ref[...], 1, 1)
        msg_ref[r * TILE : (r + 1) * TILE, :] = (part * scale[:, r : r + 1]).astype(BF16)
    acc[...] = jnp.zeros_like(acc)
    ready.wait()
    tiles.wait()
    tile_products(HUB_BLOCKS, plan, vals, msg_ref, acc)
    out_ref[...] = acc[...].astype(BF16)


def hub_kernel(core, rows_ref, cols_ref, msg_ref, vals_hbm, keep_ref, send_ref,
               vals, acc, plan_vmem, plan, sem, plan_sem):
    tiles = load_tiles(0, vals_hbm, vals, sem)
    ready = make_plan(0, rows_ref, cols_ref, plan_vmem, plan, plan_sem, HUB_BLOCKS)
    acc[...] = jnp.zeros_like(acc)
    ready.wait()
    tiles.wait()
    tile_products(HUB_BLOCKS, plan, vals, msg_ref, acc)
    for y in range(4):
        mine = pl.multiple_of((2 * y + core[0]) * 256, 256)
        theirs = pl.multiple_of((2 * y + 1 - core[0]) * 256, 256)
        keep_ref[y * 256 : (y + 1) * 256, :] = acc[pl.ds(mine, 256), :]
        send_ref[y * 256 : (y + 1) * 256, :] = acc[pl.ds(theirs, 256), :]


def own_kernel(rows_ref, cols_ref, msg_ref, cot_ref, w_ref, vals_hbm, out_ref, vals, plan_vmem, plan, sem, plan_sem):
    tiles = load_tiles(1, vals_hbm, vals, sem)
    ready = make_plan(1, rows_ref, cols_ref, plan_vmem, plan, plan_sem, OWN_BLOCKS)
    for r in range(NODES // TILE):
        block = slice(r * TILE, (r + 1) * TILE)
        out_ref[block, :] = contract(cot_ref[block, :], w_ref[...], 1, 1)
    ready.wait()
    tiles.wait()
    tile_products(OWN_BLOCKS, plan, vals, msg_ref, out_ref)


def pack_kernel(keep_ref, came_ref, packed_hbm, out_ref):
    del packed_hbm
    out_ref[...] = (keep_ref[...] + came_ref[...]).astype(BF16)


def hub_pack_kernel(keep_ref, came_ref, out_ref):
    out_ref[...] = (keep_ref[...] + came_ref[...]).astype(BF16)


def weights_kernel(core, feat_ref, agg_ref, cot_ref, keep_ref, send_ref, acc):
    step = pl.program_id(0)
    first = contract(feat_ref[...], cot_ref[...], 0, 0)
    second = contract(agg_ref[...], cot_ref[...], 0, 0)

    @pl.when(step == 0)
    def _():
        acc[:WIDTH] = first
        acc[WIDTH:] = second

    @pl.when(step != 0)
    def _():
        acc[:WIDTH] += first
        acc[WIDTH:] += second

    def put(ref, column):
        for k in range(2):
            ref[k * 2 * WIDTH : (k + 1) * 2 * WIDTH, :] = acc[:, column + k * TILE : column + (k + 1) * TILE]

    last = step == pl.num_programs(0) - 1

    @pl.when(last & (core[0] == 0))
    def _():
        put(keep_ref, 0)
        put(send_ref, 2 * TILE)

    @pl.when(last & (core[0] != 0))
    def _():
        put(keep_ref, 2 * TILE)
        put(send_ref, 0)


def spread_kernel(arrived_ref, packed_hbm, out_ref):
    del packed_hbm
    for c in range(2):
        total = jnp.zeros((16, TILE), F32)
        for y in range(4):
            for m in range(16):
                start = (2 * y + c) * 256 + 16 * m
                total += arrived_ref[start : start + 16, :].astype(F32)
        total = total.astype(BF16)
        for peer in range(64):
            out_ref[16 * peer : 16 * peer + 16, c * TILE : (c + 1) * TILE] = total


def landing_kernel(targets_ref, own_ref, arrived_ref, nodes_ref):
    chunk = 256
    slots = arrived_ref.shape[0]
    for s in range(slots // chunk):
        goal = targets_ref[s : s + 1, :]
        place = (lax.broadcasted_iota(jnp.int32, (NODES, chunk), 0) == goal).astype(BF16)
        part = contract(place, arrived_ref[s * chunk : (s + 1) * chunk, :], 1, 0)
        if s == 0:
            nodes_ref[...] = own_ref[...] + part
        else:
            nodes_ref[...] += part


def hub_sum_kernel(arrived_ref, hubs_ref):
    total = jnp.zeros((16, WIDTH), F32)
    for p in range(64):
        total += arrived_ref[16 * p : 16 * p + 16, :].astype(F32)
    hubs_ref[...] = total


def join_kernel(core, mine_ref, came_ref, out_ref):
    for ref, part in ((mine_ref, core[0]), (came_ref, 1 - core[0])):
        place = pl.ds(pl.multiple_of(part * 256, 256), 256)
        for y in range(4):
            for c in range(2):
                column = (2 * c + y // 2) * TILE
                block = ref[y * 256 : (y + 1) * 256, c * TILE : (c + 1) * TILE]
                out_ref[y % 2, place, column : column + TILE] = block.astype(F32)


def whole(*shape):
    return pl.BlockSpec(shape, lambda i, *_: (0,) * len(shape))


ANY = pl.BlockSpec(memory_space=pl.ANY)


def call(kernel, name, scalars, ins, outs, shapes, scratch, flops, moved, grid=(1,), **more):
    return pl.pallas_call(
        kernel,
        grid_spec=pltpu.PrefetchScalarGridSpec(
            num_scalar_prefetch=scalars, grid=grid, in_specs=ins, out_specs=outs, scratch_shapes=scratch
        ),
        out_shape=shapes,
        compiler_params=pltpu.CompilerParams(vmem_limit_bytes=VMEM),
        cost_estimate=pl.CostEstimate(flops=flops, bytes_accessed=moved, transcendentals=0),
        name=name,
        **more,
    )


def tile_scratch(acc):
    kept = [pltpu.VMEM((REG + 1, TILE, TILE), BF16)]
    if acc:
        kept.append(pltpu.VMEM((HUB_BLOCKS * TILE, WIDTH), F32))
    return kept + [
        pltpu.VMEM((8, PLAN), jnp.int32),
        pltpu.SMEM((8, PLAN), jnp.int32),
        pltpu.SemaphoreType.DMA,
        pltpu.SemaphoreType.DMA,
    ]


def shift(k, n):
    return [(i, (i + k) % n) for i in range(n)]


def local(features, aggregated, cotangent, w_self, w_neigh, degrees, tile_rows, tile_cols, tile_vals, recv_rows):
    core_arg = lax.axis_index("core").reshape(1).astype(jnp.int32)
    rows = tile_rows.reshape(3, REG)
    cols = tile_cols.reshape(3, REG)
    deg = degrees.reshape(NODES // TILE, TILE)
    targets = recv_rows.reshape(8, 256)
    spec_rc = whole(3, REG)
    spec_nodes = whole(NODES, WIDTH)
    spec_w = whole(WIDTH, WIDTH)
    slots = HUB_BLOCKS * TILE
    region_flops = 2 * REG * TILE * TILE * WIDTH
    region_bytes = REG * TILE * TILE * 2 + NODES * WIDTH * 2 + slots * WIDTH * 2
    swap = shift(1, 2)

    steps = 4
    spec_rows = pl.BlockSpec((NODES // steps, WIDTH), lambda i, *_: (i, 0))
    w_keep, w_send = call(
        weights_kernel, "weights", 1, [spec_rows] * 3, [whole(slots, TILE)] * 2,
        [jax.ShapeDtypeStruct((slots, TILE), F32)] * 2, [pltpu.VMEM((2 * WIDTH, WIDTH), F32)],
        4 * NODES * WIDTH * WIDTH, 5 << 20, grid=(steps,),
    )(core_arg, features, aggregated, cotangent)
    w_came = lax.ppermute(w_send, "core", swap)

    wide = WIDTH + TILE
    msg, packed = call(
        ghost_kernel, "ghost", 0,
        [spec_rc, spec_rc, whole(8, TILE), spec_nodes, spec_w, ANY],
        [spec_nodes, whole(slots, WIDTH)],
        [jax.ShapeDtypeStruct((NODES, WIDTH), BF16), jax.ShapeDtypeStruct((slots, wide), BF16)],
        tile_scratch(True), region_flops + 2 * NODES * WIDTH * WIDTH, region_bytes + (2 << 20),
    )(rows, cols, deg, cotangent, w_neigh, tile_vals)
    spec_part = pl.BlockSpec((slots // steps, TILE), lambda i: (i, 0))
    packed = call(
        pack_kernel, "pack", 0, [spec_part, spec_part, ANY],
        pl.BlockSpec((slots // steps, TILE), lambda i: (i, WIDTH // TILE)),
        jax.ShapeDtypeStruct((slots, wide), BF16),
        [], slots * TILE, 3 << 20, grid=(steps,), input_output_aliases={2: 0},
    )(w_keep, w_came, packed)
    arrived = lax.all_to_all(
        packed.reshape(128, 16, wide), ALL, split_axis=0, concat_axis=0, tiled=True
    ).reshape(slots, wide)

    hub_keep, hub_send = call(
        hub_kernel, "hub", 1, [spec_rc, spec_rc, spec_nodes, ANY], [spec_nodes, spec_nodes],
        [jax.ShapeDtypeStruct((NODES, WIDTH), F32)] * 2,
        tile_scratch(True), region_flops, region_bytes + (2 << 20),
    )(core_arg, rows, cols, msg, tile_vals)
    hub_came = lax.ppermute(hub_send, "core", swap)
    own = call(
        own_kernel, "own", 0, [spec_rc, spec_rc, spec_nodes, spec_nodes, spec_w, ANY], spec_nodes,
        jax.ShapeDtypeStruct((NODES, WIDTH), F32),
        tile_scratch(False), region_flops + 2 * NODES * WIDTH * WIDTH, region_bytes,
    )(rows, cols, msg, cotangent, w_self, tile_vals)

    wider = WIDTH + 2 * TILE
    spec_hub = pl.BlockSpec((NODES // steps, WIDTH), lambda i: (i, 0))
    packed = call(
        hub_pack_kernel, "hub_pack", 0, [spec_hub, spec_hub], spec_hub,
        jax.ShapeDtypeStruct((NODES, wider), BF16), [], NODES * WIDTH, 5 << 20, grid=(steps,),
    )(hub_keep, hub_came)
    packed = call(
        spread_kernel, "spread", 0, [pl.BlockSpec((slots, TILE), lambda i: (0, WIDTH // TILE)), ANY],
        pl.BlockSpec((NODES, 2 * TILE), lambda i: (0, WIDTH // (2 * TILE))),
        jax.ShapeDtypeStruct((NODES, wider), BF16), [], slots * TILE, 1 << 20, input_output_aliases={1: 0},
    )(arrived, packed)
    shared = lax.all_to_all(
        packed.reshape(64, 16, wider), ("y", "z", "x"), split_axis=0, concat_axis=0, tiled=True
    ).reshape(NODES, wider)

    grad_nodes = call(
        landing_kernel, "landing", 0, [whole(8, 256), spec_nodes, whole(slots, WIDTH)], spec_nodes,
        jax.ShapeDtypeStruct((NODES, WIDTH), F32), [], 2 * slots * NODES * WIDTH, 7 << 20,
    )(targets, own, arrived)

    w_mine = shared[:, WIDTH:]
    w_theirs = lax.ppermute(w_mine, "core", swap)
    grad_hubs = call(
        hub_sum_kernel, "hub_sum", 0, [spec_nodes], whole(16, WIDTH),
        jax.ShapeDtypeStruct((16, WIDTH), F32), [], NODES * WIDTH, 1 << 20,
    )(shared)
    grad_weights = call(
        join_kernel, "join", 1, [whole(NODES, 2 * TILE)] * 2, whole(2, WIDTH, WIDTH),
        jax.ShapeDtypeStruct((2, WIDTH, WIDTH), F32), [], NODES * WIDTH, 3 << 20,
    )(core_arg, w_mine, w_theirs)
    return (grad_nodes, grad_hubs, grad_weights)


def solution(mesh):
    fine = Mesh(mesh.devices.reshape(4, 2, 4, 4), ALL)
    rows = P(ALL, None)
    in_specs = (
        rows, rows, rows, P(), P(), P(ALL), P(ALL), P(ALL), P(ALL, None, None), P(ALL, None, None),
    )
    out_specs = (rows, rows, P())
    return jax.shard_map(local, mesh=fine, in_specs=in_specs, out_specs=out_specs, check_vma=False)
```

time: 150 us -> 124 us (0.83)
  waiting for transfers between devices: 51.3 us -> 17.8 us
  blocking collectives: 0 us -> 28.7 us
  starting transfers between devices: 35.3 us -> 15.2 us
  Pallas kernels: 44.4 us -> 55.7 us
  other arithmetic: 10.2 us -> 0 us
  local copies, waits for them, and re-layouts: 7.43 us -> 5.41 us
    ppermute x18 -> x3, waiting for transfers between devices: 51.3 us -> 4 us  [the longest x1 4 us: local(): hub_came = lax.ppermute(hub_send, 'core', swap)]
    all_to_all x0 -> x1, blocking collectives: none -> 28.7 us  [local(): lax.all_to_all(packed.reshape(64, 16, wider), ('y', 'z', 'x'), split_axis...]
    ppermute x18 -> x3, starting transfers between devices: 24.7 us -> 5.07 us  [the longest x1 2.51 us: local(): w_theirs = lax.ppermute(w_mine, 'core', swap)]
    all_to_all x1, waiting for transfers between devices: 0.01 us -> 13.8 us  [local(): lax.all_to_all(packed.reshape(128, 16, wide), ALL, split_axis=0, concat_a...]
    pallas_call x4 -> x8, Pallas kernels: 28.5 us -> 40.2 us  [the longest x1 10.7 us: local(): call(hub_kernel, 'hub', 1, [spec_rc, spec_rc, spec_nodes, ANY], [spec_nod...]
    add x3 -> x0, other arithmetic: 3.78 us -> none  [the longest x2 2.03 us: scatter_sum(): total = total + part.astype(F32)]
    convert_element_type x2 -> x0, other arithmetic: 2.87 us -> none  [the longest x1 2.83 us: local(): grad_weights = jnp.where(core == 0, jnp.stack([mine, other]), jnp.stack([...]
    select_n x3 -> x0, other arithmetic: 1.84 us -> none  [by_index(): pick = jnp.where(back == k, held[k], pick)]
  transfers between devices with their start and end apart: 19 -> 4, of which waited for: 14 -> 2; matrix products, arithmetic and copies ran while one was open for 8% -> 1% of each run, Pallas kernels for 19% -> 34%
where the time goes in v2:
time: 124 us
  Pallas kernels  55.7 us (45%)
  blocking collectives  28.7 us (23%)
  waiting for transfers between devices  17.8 us (14%)
  starting transfers between devices  15.2 us (12%)
  local copies, waits for them, and re-layouts  5.41 us (4%)
    all_to_all x1, blocking collectives, local(): lax.all_to_all(packed.reshape(64, 16, wider), ('y', 'z', 'x'), split_axis...  28.7 us
    all_to_all x1, waiting for transfers between devices, local(): lax.all_to_all(packed.reshape(128, 16, wide), ALL, split_axis=0, concat_a...  13.8 us
    pallas_call x1, Pallas kernels, local(): call(hub_kernel, 'hub', 1, [spec_rc, spec_rc, spec_nodes, ANY], [spec_nod...  10.7 us
    all_to_all x1, starting transfers between devices, local(): lax.all_to_all(packed.reshape(128, 16, wide), ALL, split_axis=0, concat_a...  10.1 us
    pallas_call x1, Pallas kernels, local(): call(own_kernel, 'own', 0, [spec_rc, spec_rc, spec_nodes, spec_nodes, spe...  9.64 us
    pallas_call x1, Pallas kernels, local(): call(ghost_kernel, 'ghost', 0, [spec_rc, spec_rc, whole(8, TILE), spec_no...  9.48 us
    pallas_call x1, Pallas kernels, local(): call(landing_kernel, 'landing', 0, [whole(8, 256), spec_nodes, whole(slot...  5.89 us
    pallas_call x1, Pallas kernels, local(): call(weights_kernel, 'weights', 1, [spec_rows] * 3, [whole(slots, TILE)]...  5.74 us
  transfers between devices with their start and end apart: 4, of which 2 were waited for; matrix products, arithmetic and copies ran while one was open for 1% of the time, Pallas kernels for 34%

profile of v2, /device:TPU:1, one launch (start us, length us, event | category | flops | bytes accessed | tf_op | source)
XLA Modules:
  0.0 123.5 jit_solution(8569211040532188832)
XLA Ops:
  0.6 5.7 %weights.1 = (f32[2048,128]{1,0:T(8,128)}, f32[2048,128]{1,0:T(8,128)}) custom-call(s32[1]{0:T(128)} %bitcast.3.core, bf16[1024,512]{1,0:T(8,128)(2,1)} %feat_ref.1, bf16[1024,512]{1,0:T(8,128)(2,1)} %agg_ref.1, bf16[1024,512]{1,0:T(8,128)(2,1)} %cot_ref.5), custom_call_target="tpu_custom_call" | custom-call | flops 1073741824 | bytes 5242880 | tf_op jit(solution)/shard_map/weights/pallas_call | solution.py:272
  6.4 1.4 %collective-permute-start = (f32[2048,128]{1,0:T(8,128)}, f32[2048,128]{1,0:T(8,128)S(1)}, u32[]{:S(2)}, u32[]{:S(2)}) collective-permute-start(f32[2048,128]{1,0:T(8,128)} %get-tuple-element.11), channel_id=1, source_target_pairs={{0,16},{16,0},{1,17},{17,1},{2,18},{18,2},{3,19},{19,3},{4,20},{20... | collective-permute-start | bytes 3145736 | tf_op jit(solution)/shard_map/ppermute | solution.py:277
  7.8 9.5 %ghost.1 = (bf16[1024,512]{1,0:T(8,128)(2,1)}, bf16[2048,640]{1,0:T(8,128)(2,1)}) custom-call(s32[3,128]{1,0:T(4,128)} %bitcast.14, s32[3,128]{1,0:T(4,128)} %bitcast.17, s32[8,128]{1,0:T(8,128)} %bitcast.20, bf16[1024,512]{1,0:T(8,128)(2,1)} %cot_ref.5, bf16[512,512]{1,0:T(8,128)(2,1)} %w_ref.2, bf16[384,128,128]{2,1,0:T(8,128)(2,1)} %vals_hbm.5), custom_call_target="tpu_custom_call" | custom-call | flops 2684354560 | bytes 9437184 | tf_op jit(solution)/shard_map/ghost/pallas_call | solution.py:280
  17.3 0.0 collective-permute-done.came_ref
  17.3 0.0 copy-start.4
  17.3 1.0 copy-done.4
  18.3 3.5 %pack.1 = bf16[2048,640]{1,0:T(8,128)(2,1)} custom-call(f32[2048,128]{1,0:T(8,128)} %get-tuple-element.10.keep_ref, f32[2048,128]{1,0:T(8,128)} %copy-done.4, bf16[2048,640]{1,0:T(8,128)(2,1)} %get-tuple-element.12.packed_hbm), custom_call_target="tpu_custom_call", output_to_operand_aliasing={{}: (2, {})} | custom-call | flops 262144 | bytes 3145728 | tf_op jit(solution)/shard_map/pack/pallas_call | solution.py:288
  21.8 10.1 %all-to-all-start = ((bf16[128,16,640]{2,1,0:T(8,128)(2,1)}), bf16[128,16,640]{2,1,0:T(8,128)(2,1)S(1)}, u32[]{:S(2)}, u32[]{:S(2)}) async-start(bf16[128,16,640]{2,1,0:T(8,128)(2,1)} %bitcast.9), calls=%async_computation | async-start | bytes 5242880 | tf_op jit(solution)/shard_map/all_to_all | solution.py:294
  31.9 10.7 %hub.1 = (f32[1024,512]{1,0:T(8,128)}, f32[1024,512]{1,0:T(8,128)}) custom-call(s32[1]{0:T(128)} %bitcast.3.core, s32[3,128]{1,0:T(4,128)} %bitcast.15, s32[3,128]{1,0:T(4,128)} %bitcast.18, bf16[1024,512]{1,0:T(8,128)(2,1)} %get-tuple-element.9.msg_ref, bf16[384,128,128]{2,1,0:T(8,128)(2,1)} %vals_hbm.5), custom_call_target="tpu_custom_call" | custom-call | flops 2147483648 | bytes 9437184 | tf_op jit(solution)/shard_map/hub/pallas_call | solution.py:298
  42.6 1.1 collective-permute-start.1
  43.7 4.0 %collective-permute-done.1.came_ref = f32[1024,512]{1,0:T(8,128)S(1)} collective-permute-done((f32[1024,512]{1,0:T(8,128)}, f32[1024,512]{1,0:T(8,128)S(1)}, u32[]{:S(2)}, u32[]{:S(2)}) %collective-permute-start.1) | collective-permute-done | bytes 2097184 | tf_op jit(solution)/shard_map/ppermute | solution.py:303
  47.7 0.0 copy-start.3
  47.7 1.3 %copy-done.3 = f32[1024,512]{1,0:T(8,128)} copy-done((f32[1024,512]{1,0:T(8,128)}, f32[1024,512]{1,0:T(8,128)S(1)}, u32[]{:S(2)}) %copy-start.3) | copy-done | bytes 2097176
  49.1 4.0 %hub_pack.1.packed_hbm = bf16[1024,768]{1,0:T(8,128)(2,1)} custom-call(f32[1024,512]{1,0:T(8,128)} %get-tuple-element.13.keep_ref, f32[1024,512]{1,0:T(8,128)} %copy-done.3), custom_call_target="tpu_custom_call" | custom-call | flops 524288 | bytes 5242880 | tf_op jit(solution)/shard_map/hub_pack/pallas_call | solution.py:312
  53.1 13.8 %all-to-all-done = bf16[128,16,640]{2,1,0:T(8,128)(2,1)S(1)} async-done(((bf16[128,16,640]{2,1,0:T(8,128)(2,1)}), bf16[128,16,640]{2,1,0:T(8,128)(2,1)S(1)}, u32[]{:S(2)}, u32[]{:S(2)}) %all-to-all-start) | async-done | bytes 2621472 | tf_op jit(solution)/shard_map/all_to_all | solution.py:294
  66.9 0.0 copy-start
  66.9 1.5 %copy-done = bf16[128,16,640]{2,1,0:T(8,128)(2,1)} copy-done((bf16[128,16,640]{2,1,0:T(8,128)(2,1)}, bf16[128,16,640]{2,1,0:T(8,128)(2,1)S(1)}, u32[]{:S(2)}) %copy-start) | copy-done | bytes 2621464
  68.4 2.0 %spread.1 = bf16[1024,768]{1,0:T(8,128)(2,1)} custom-call(bf16[2048,640]{1,0:T(8,128)(2,1)} %bitcast.10, bf16[1024,768]{1,0:T(8,128)(2,1)} %hub_pack.1.packed_hbm), custom_call_target="tpu_custom_call", output_to_operand_aliasing={{}: (1, {})} | custom-call | flops 262144 | bytes 1048576 | tf_op jit(solution)/shard_map/spread/pallas_call | solution.py:316
  70.4 0.0 copy-start.6
  70.4 28.7 %all_to_all.10 = bf16[64,16,768]{2,1,0:T(8,128)(2,1)S(1)} all-to-all(bf16[64,16,768]{2,1,0:T(8,128)(2,1)} %bitcast.8), channel_id=1, replica_groups=mesh['y'=4,'core'=2,'z'=4,'x'=4] {'y','z','x'}, dimensions={0} | all-to-all | bytes 3145728 | tf_op jit(solution)/shard_map/all_to_all | solution.py:321
  99.0 0.0 copy-start.1
  99.1 0.0 copy-start.2
  99.1 2.5 %collective-permute-start.2 = (bf16[1024,256]{1,0:T(8,128)(2,1)S(1)}, bf16[1024,256]{1,0:T(8,128)(2,1)S(1)}, u32[]{:S(2)}, u32[]{:S(2)}) collective-permute-start(bf16[1024,256]{1,0:T(8,128)(2,1)S(1)} %slice.4.mine_ref), channel_id=1, source_target_pairs={{0,16},{16,0},{1,17},{17,1},{2,18},{18,2},{3,19},{19,3},{4,20},{20... | collective-permute-start | bytes 1572872 | tf_op jit(solution)/shard_map/ppermute | solution.py:331
  101.6 0.0 copy-done.6
  101.6 0.1 copy.16
  101.7 0.7 reshape.33.targets_ref
  102.4 9.6 %own.1.own_ref = f32[1024,512]{1,0:T(8,128)} custom-call(s32[3,128]{1,0:T(4,128)} %bitcast.16, s32[3,128]{1,0:T(4,128)} %bitcast.19, bf16[1024,512]{1,0:T(8,128)(2,1)} %get-tuple-element.9.msg_ref, bf16[1024,512]{1,0:T(8,128)(2,1)} %cot_ref.5, bf16[512,512]{1,0:T(8,128)(2,1)} %w_ref.3, bf16[384,128,128]{2,1,0:T(8,128)(2,1)} %vals_hbm.5), custom_call_target="tpu_custom_call" | custom-call | flops 2684354560 | bytes 7340032 | tf_op jit(solution)/shard_map/own/pallas_call | solution.py:304
  112.0 0.0 copy-done.1
  112.1 0.0 copy-done.2
  112.1 5.9 %landing.1 = f32[1024,512]{1,0:T(8,128)} custom-call(s32[8,256]{1,0:T(8,128)} %reshape.33.targets_ref, f32[1024,512]{1,0:T(8,128)} %own.1.own_ref, bf16[2048,640]{1,0:T(8,128)(2,1)} %bitcast.11), custom_call_target="tpu_custom_call" | custom-call | flops 2147483648 | bytes 7340032 | tf_op jit(solution)/shard_map/landing/pallas_call | solution.py:325
  118.0 2.0 %hub_sum.1 = f32[16,512]{1,0:T(8,128)} custom-call(bf16[1024,768]{1,0:T(8,128)(2,1)} %bitcast.13), custom_call_target="tpu_custom_call" | custom-call | flops 524288 | bytes 1048576 | tf_op jit(solution)/shard_map/hub_sum/pallas_call | solution.py:332
  120.0 0.0 collective-permute-done.2.came_ref
  120.0 0.0 copy-start.5
  120.0 0.8 copy-done.5
  120.8 2.8 %join.1 = f32[2,512,512]{2,1,0:T(8,128)} custom-call(s32[1]{0:T(128)} %bitcast.3.core, bf16[1024,256]{1,0:T(8,128)(2,1)} %copy-done.2, bf16[1024,256]{1,0:T(8,128)(2,1)} %copy-done.5), custom_call_target="tpu_custom_call" | custom-call | flops 524288 | bytes 3145728 | tf_op jit(solution)/shard_map/join/pallas_call | solution.py:336
  (1 shorter events, 0.0 us)
Async XLA Ops:
  6.4 10.9 %collective-permute-start = (f32[2048,128]{1,0:T(8,128)}, f32[2048,128]{1,0:T(8,128)S(1)}, u32[]{:S(2)}, u32[]{:S(2)}) collective-permute-start(f32[2048,128]{1,0:T(8,128)} %get-tuple-element.11), channel_id=1, source_target_pairs={{0,16},{16,0},{1,17},{17,1},{2,18},{18,2},{3,19},{19,3},{4,20},{20... | collective-permute-start | bytes 3145736 | tf_op jit(solution)/shard_map/ppermute | solution.py:277
  17.3 1.0 copy-start.4
  21.8 45.1 %all-to-all-start = ((bf16[128,16,640]{2,1,0:T(8,128)(2,1)}), bf16[128,16,640]{2,1,0:T(8,128)(2,1)S(1)}, u32[]{:S(2)}, u32[]{:S(2)}) async-start(bf16[128,16,640]{2,1,0:T(8,128)(2,1)} %bitcast.9), calls=%async_computation | async-start | bytes 5242880 | tf_op jit(solution)/shard_map/all_to_all | solution.py:294
  42.6 5.1 %collective-permute-start.1 = (f32[1024,512]{1,0:T(8,128)}, f32[1024,512]{1,0:T(8,128)S(1)}, u32[]{:S(2)}, u32[]{:S(2)}) collective-permute-start(f32[1024,512]{1,0:T(8,128)} %get-tuple-element.14), channel_id=1, source_target_pairs={{0,16},{16,0},{1,17},{17,1},{2,18},{18,2},{3,19},{19,3},{4,20},{20... | collective-permute-start | bytes 6291464 | tf_op jit(solution)/shard_map/ppermute | solution.py:303
  47.7 1.3 %copy-start.3 = (f32[1024,512]{1,0:T(8,128)}, f32[1024,512]{1,0:T(8,128)S(1)}, u32[]{:S(2)}) copy-start(f32[1024,512]{1,0:T(8,128)S(1)} %collective-permute-done.1.came_ref) | copy-start | bytes 6291460
  66.9 1.5 %copy-start = (bf16[128,16,640]{2,1,0:T(8,128)(2,1)}, bf16[128,16,640]{2,1,0:T(8,128)(2,1)S(1)}, u32[]{:S(2)}) copy-start(bf16[128,16,640]{2,1,0:T(8,128)(2,1)S(1)} %all-to-all-done) | copy-start | bytes 7864324
  70.4 31.2 %copy-start.6 = (s32[1,128,16]{1,2,0:T(8,128)S(1)}, s32[1,128,16]{1,2,0:T(8,128)}, u32[]{:S(2)}) copy-start(s32[1,128,16]{1,2,0:T(8,128)} %param.19) | copy-start | bytes 24580
  99.0 13.0 %copy-start.1 = (bf16[64,16,768]{2,1,0:T(8,128)(2,1)}, bf16[64,16,768]{2,1,0:T(8,128)(2,1)S(1)}, u32[]{:S(2)}) copy-start(bf16[64,16,768]{2,1,0:T(8,128)(2,1)S(1)} %all_to_all.10) | copy-start | bytes 4718596
  99.1 13.0 %copy-start.2 = (bf16[1024,256]{1,0:T(8,128)(2,1)}, bf16[1024,256]{1,0:T(8,128)(2,1)S(1)}, u32[]{:S(2)}) copy-start(bf16[1024,256]{1,0:T(8,128)(2,1)S(1)} %slice.4.mine_ref) | copy-start | bytes 1572868
  99.1 20.9 %collective-permute-start.2 = (bf16[1024,256]{1,0:T(8,128)(2,1)S(1)}, bf16[1024,256]{1,0:T(8,128)(2,1)S(1)}, u32[]{:S(2)}, u32[]{:S(2)}) collective-permute-start(bf16[1024,256]{1,0:T(8,128)(2,1)S(1)} %slice.4.mine_ref), channel_id=1, source_target_pairs={{0,16},{16,0},{1,17},{17,1},{2,18},{18,2},{3,19},{19,3},{4,20},{20... | collective-permute-start | bytes 1572872 | tf_op jit(solution)/shard_map/ppermute | solution.py:331
  120.0 0.8 copy-start.5

commit v3 on v2

--- a/solution.py
+++ b/solution.py
@@ -313,6 +313,7 @@
         hub_pack_kernel, "hub_pack", 0, [spec_hub, spec_hub], spec_hub,
         jax.ShapeDtypeStruct((NODES, wider), BF16), [], NODES * WIDTH, 5 << 20, grid=(steps,),
     )(hub_keep, hub_came)
+    packed, own = lax.optimization_barrier((packed, own))
     packed = call(
         spread_kernel, "spread", 0, [pl.BlockSpec((slots, TILE), lambda i: (0, WIDTH // TILE)), ANY],
         pl.BlockSpec((NODES, 2 * TILE), lambda i: (0, WIDTH // (2 * TILE))),
@@ -327,6 +328,7 @@
         jax.ShapeDtypeStruct((NODES, WIDTH), F32), [], 2 * slots * NODES * WIDTH, 7 << 20,
     )(targets, own, arrived)
 
+    shared, grad_nodes = lax.optimization_barrier((shared, grad_nodes))
     w_mine = shared[:, WIDTH:]
     w_theirs = lax.ppermute(w_mine, "core", swap)
     grad_hubs = call(

time: 124 us -> 108 us (0.87)
  blocking collectives: 28.7 us -> 0 us
  waiting for transfers between devices: 17.8 us -> 24.6 us
  starting transfers between devices: 15.2 us -> 20.8 us
    all_to_all x1 -> x0, blocking collectives: 28.7 us -> none  [local(): lax.all_to_all(packed.reshape(64, 16, wider), ('y', 'z', 'x'), split_axis...]
    all_to_all x0 -> x1, waiting for transfers between devices: none -> 16.4 us  [local(): lax.all_to_all(packed.reshape(64, 16, wider), ('y', 'z', 'x'), split_axis...]
    all_to_all x1, waiting for transfers between devices: 13.8 us -> 8.12 us  [local(): lax.all_to_all(packed.reshape(128, 16, wide), ALL, split_axis=0, concat_a...]
    all_to_all x0 -> x1, starting transfers between devices: none -> 5.58 us  [local(): lax.all_to_all(packed.reshape(64, 16, wider), ('y', 'z', 'x'), split_axis...]
    ppermute x1, waiting for transfers between devices: 4 us -> 0.01 us  [local(): hub_came = lax.ppermute(hub_send, 'core', swap)]
  transfers between devices with their start and end apart: 4 -> 5, of which waited for: 2 -> 2; matrix products, arithmetic and copies ran while one was open for 1% -> 1% of each run, Pallas kernels for 34% -> 39%
where the time goes in v3:
time: 108 us; the launch traced here: 107 us
  Pallas kernels  55.7 us (52%)
  waiting for transfers between devices  24.6 us (23%)
  starting transfers between devices  20.8 us (19%)
  local copies, waits for them, and re-layouts  5.42 us (5%)
    all_to_all x1, waiting for transfers between devices, local(): lax.all_to_all(packed.reshape(64, 16, wider), ('y', 'z', 'x'), split_axis...  16.4 us
    pallas_call x1, Pallas kernels, local(): call(hub_kernel, 'hub', 1, [spec_rc, spec_rc, spec_nodes, ANY], [spec_nod...  10.7 us
    all_to_all x1, starting transfers between devices, local(): lax.all_to_all(packed.reshape(128, 16, wide), ALL, split_axis=0, concat_a...  10.1 us
    pallas_call x1, Pallas kernels, local(): call(own_kernel, 'own', 0, [spec_rc, spec_rc, spec_nodes, spec_nodes, spe...  9.63 us
    pallas_call x1, Pallas kernels, local(): call(ghost_kernel, 'ghost', 0, [spec_rc, spec_rc, whole(8, TILE), spec_no...  9.46 us
    all_to_all x1, waiting for transfers between devices, local(): lax.all_to_all(packed.reshape(128, 16, wide), ALL, split_axis=0, concat_a...  8.12 us
    pallas_call x1, Pallas kernels, local(): call(landing_kernel, 'landing', 0, [whole(8, 256), spec_nodes, whole(slot...  5.88 us
    pallas_call x1, Pallas kernels, local(): call(weights_kernel, 'weights', 1, [spec_rows] * 3, [whole(slots, TILE)]...  5.74 us
  transfers between devices with their start and end apart: 5, of which 2 were waited for; matrix products, arithmetic and copies ran while one was open for 1% of the time, Pallas kernels for 39%

profile of v3, /device:TPU:1, one launch (start us, length us, event | category | flops | bytes accessed | tf_op | source)
XLA Modules:
  0.0 107.2 jit_solution(17887039260931940490)
XLA Ops:
  0.6 5.7 %weights.1 = (f32[2048,128]{1,0:T(8,128)}, f32[2048,128]{1,0:T(8,128)}) custom-call(s32[1]{0:T(128)} %bitcast.core, bf16[1024,512]{1,0:T(8,128)(2,1)} %feat_ref.1, bf16[1024,512]{1,0:T(8,128)(2,1)} %agg_ref.1, bf16[1024,512]{1,0:T(8,128)(2,1)} %cot_ref.5), custom_call_target="tpu_custom_call" | custom-call | flops 1073741824 | bytes 5242880 | tf_op jit(solution)/shard_map/weights/pallas_call | solution.py:272
  6.4 1.4 %collective-permute-start = (f32[2048,128]{1,0:T(8,128)}, f32[2048,128]{1,0:T(8,128)S(1)}, u32[]{:S(2)}, u32[]{:S(2)}) collective-permute-start(f32[2048,128]{1,0:T(8,128)} %get-tuple-element.14), channel_id=1, source_target_pairs={{0,16},{16,0},{1,17},{17,1},{2,18},{18,2},{3,19},{19,3},{4,20},{20... | collective-permute-start | bytes 3145736 | tf_op jit(solution)/shard_map/ppermute | solution.py:277
  7.8 9.5 %ghost.1 = (bf16[1024,512]{1,0:T(8,128)(2,1)}, bf16[2048,640]{1,0:T(8,128)(2,1)}) custom-call(s32[3,128]{1,0:T(4,128)} %bitcast.14, s32[3,128]{1,0:T(4,128)} %bitcast.17, s32[8,128]{1,0:T(8,128)} %bitcast.20, bf16[1024,512]{1,0:T(8,128)(2,1)} %cot_ref.5, bf16[512,512]{1,0:T(8,128)(2,1)} %w_ref.2, bf16[384,128,128]{2,1,0:T(8,128)(2,1)} %vals_hbm.5), custom_call_target="tpu_custom_call" | custom-call | flops 2684354560 | bytes 9437184 | tf_op jit(solution)/shard_map/ghost/pallas_call | solution.py:280
  17.3 0.0 collective-permute-done.came_ref
  17.3 0.0 copy-start.4
  17.3 1.0 copy-done.4
  18.2 3.5 %pack.1 = bf16[2048,640]{1,0:T(8,128)(2,1)} custom-call(f32[2048,128]{1,0:T(8,128)} %get-tuple-element.13.keep_ref, f32[2048,128]{1,0:T(8,128)} %copy-done.4, bf16[2048,640]{1,0:T(8,128)(2,1)} %get-tuple-element.15.packed_hbm), custom_call_target="tpu_custom_call", output_to_operand_aliasing={{}: (2, {})} | custom-call | flops 262144 | bytes 3145728 | tf_op jit(solution)/shard_map/pack/pallas_call | solution.py:288
  21.7 10.1 %all-to-all-start = ((bf16[128,16,640]{2,1,0:T(8,128)(2,1)}), bf16[128,16,640]{2,1,0:T(8,128)(2,1)S(1)}, u32[]{:S(2)}, u32[]{:S(2)}) async-start(bf16[128,16,640]{2,1,0:T(8,128)(2,1)} %bitcast.9), calls=%async_computation | async-start | bytes 5242880 | tf_op jit(solution)/shard_map/all_to_all | solution.py:294
  31.9 10.7 %hub.1 = (f32[1024,512]{1,0:T(8,128)}, f32[1024,512]{1,0:T(8,128)}) custom-call(s32[1]{0:T(128)} %bitcast.core, s32[3,128]{1,0:T(4,128)} %bitcast.15, s32[3,128]{1,0:T(4,128)} %bitcast.18, bf16[1024,512]{1,0:T(8,128)(2,1)} %get-tuple-element.16.msg_ref, bf16[384,128,128]{2,1,0:T(8,128)(2,1)} %vals_hbm.5), custom_call_target="tpu_custom_call" | custom-call | flops 2147483648 | bytes 9437184 | tf_op jit(solution)/shard_map/hub/pallas_call | solution.py:298
  42.6 1.1 %collective-permute-start.1 = (f32[1024,512]{1,0:T(8,128)}, f32[1024,512]{1,0:T(8,128)S(1)}, u32[]{:S(2)}, u32[]{:S(2)}) collective-permute-start(f32[1024,512]{1,0:T(8,128)} %get-tuple-element.18), channel_id=1, source_target_pairs={{0,16},{16,0},{1,17},{17,1},{2,18},{18,2},{3,19},{19,3},{4,20},{20... | collective-permute-start | bytes 6291464 | tf_op jit(solution)/shard_map/ppermute | solution.py:303
  43.7 9.6 %own.1.own_ref = f32[1024,512]{1,0:T(8,128)} custom-call(s32[3,128]{1,0:T(4,128)} %bitcast.16, s32[3,128]{1,0:T(4,128)} %bitcast.19, bf16[1024,512]{1,0:T(8,128)(2,1)} %get-tuple-element.16.msg_ref, bf16[1024,512]{1,0:T(8,128)(2,1)} %cot_ref.5, bf16[512,512]{1,0:T(8,128)(2,1)} %w_ref.3, bf16[384,128,128]{2,1,0:T(8,128)(2,1)} %vals_hbm.5), custom_call_target="tpu_custom_call" | custom-call | flops 2684354560 | bytes 7340032 | tf_op jit(solution)/shard_map/own/pallas_call | solution.py:304
  53.4 0.0 collective-permute-done.1.came_ref
  53.4 0.0 copy-start.3
  53.4 1.3 %copy-done.3 = f32[1024,512]{1,0:T(8,128)} copy-done((f32[1024,512]{1,0:T(8,128)}, f32[1024,512]{1,0:T(8,128)S(1)}, u32[]{:S(2)}) %copy-start.3) | copy-done | bytes 2097176
  54.7 4.0 %hub_pack.1.packed_hbm = bf16[1024,768]{1,0:T(8,128)(2,1)} custom-call(f32[1024,512]{1,0:T(8,128)} %get-tuple-element.17.keep_ref, f32[1024,512]{1,0:T(8,128)} %copy-done.3), custom_call_target="tpu_custom_call" | custom-call | flops 524288 | bytes 5242880 | tf_op jit(solution)/shard_map/hub_pack/pallas_call | solution.py:312
  58.7 8.1 %all-to-all-done = bf16[128,16,640]{2,1,0:T(8,128)(2,1)S(1)} async-done(((bf16[128,16,640]{2,1,0:T(8,128)(2,1)}), bf16[128,16,640]{2,1,0:T(8,128)(2,1)S(1)}, u32[]{:S(2)}, u32[]{:S(2)}) %all-to-all-start) | async-done | bytes 2621472 | tf_op jit(solution)/shard_map/all_to_all | solution.py:294
  66.8 0.0 copy-start
  66.8 1.5 %copy-done = bf16[128,16,640]{2,1,0:T(8,128)(2,1)} copy-done((bf16[128,16,640]{2,1,0:T(8,128)(2,1)}, bf16[128,16,640]{2,1,0:T(8,128)(2,1)S(1)}, u32[]{:S(2)}) %copy-start) | copy-done | bytes 2621464
  68.3 2.0 %spread.1 = bf16[1024,768]{1,0:T(8,128)(2,1)} custom-call(bf16[2048,640]{1,0:T(8,128)(2,1)} %bitcast.10, bf16[1024,768]{1,0:T(8,128)(2,1)} %hub_pack.1.packed_hbm), custom_call_target="tpu_custom_call", output_to_operand_aliasing={{}: (1, {})} | custom-call | flops 262144 | bytes 1048576 | tf_op jit(solution)/shard_map/spread/pallas_call | solution.py:317
  70.4 0.0 copy-start.6
  70.4 5.6 %all-to-all-start.1 = ((bf16[64,16,768]{2,1,0:T(8,128)(2,1)}), bf16[64,16,768]{2,1,0:T(8,128)(2,1)S(1)}, u32[]{:S(2)}, u32[]{:S(2)}) async-start(bf16[64,16,768]{2,1,0:T(8,128)(2,1)} %bitcast.8), calls=%async_computation.1 | async-start | bytes 3145728 | tf_op jit(solution)/shard_map/all_to_all | solution.py:322
  76.0 0.0 copy-done.6
  76.0 0.1 copy.16
  76.1 0.7 reshape.41.targets_ref
  76.8 5.9 %landing.1 = f32[1024,512]{1,0:T(8,128)} custom-call(s32[8,256]{1,0:T(8,128)} %reshape.41.targets_ref, f32[1024,512]{1,0:T(8,128)} %own.1.own_ref, bf16[2048,640]{1,0:T(8,128)(2,1)} %bitcast.11), custom_call_target="tpu_custom_call" | custom-call | flops 2147483648 | bytes 7340032 | tf_op jit(solution)/shard_map/landing/pallas_call | solution.py:326
  82.6 16.4 %all-to-all-done.1 = bf16[64,16,768]{2,1,0:T(8,128)(2,1)S(1)} async-done(((bf16[64,16,768]{2,1,0:T(8,128)(2,1)}), bf16[64,16,768]{2,1,0:T(8,128)(2,1)S(1)}, u32[]{:S(2)}, u32[]{:S(2)}) %all-to-all-start.1) | async-done | bytes 1572896 | tf_op jit(solution)/shard_map/all_to_all | solution.py:322
  99.1 0.0 copy-start.1
  99.1 0.0 copy-start.2
  99.1 2.5 %collective-permute-start.2 = (bf16[1024,256]{1,0:T(8,128)(2,1)S(1)}, bf16[1024,256]{1,0:T(8,128)(2,1)S(1)}, u32[]{:S(2)}, u32[]{:S(2)}) collective-permute-start(bf16[1024,256]{1,0:T(8,128)(2,1)S(1)} %slice.3.mine_ref), channel_id=1, source_target_pairs={{0,16},{16,0},{1,17},{17,1},{2,18},{18,2},{3,19},{19,3},{4,20},{20... | collective-permute-start | bytes 1572872 | tf_op jit(solution)/shard_map/ppermute | solution.py:333
  101.6 0.0 copy-done.1
  101.6 2.0 %hub_sum.1 = f32[16,512]{1,0:T(8,128)} custom-call(bf16[1024,768]{1,0:T(8,128)(2,1)} %bitcast.13), custom_call_target="tpu_custom_call" | custom-call | flops 524288 | bytes 1048576 | tf_op jit(solution)/shard_map/hub_sum/pallas_call | solution.py:334
  103.6 0.0 collective-permute-done.2.came_ref
  103.6 0.0 copy-done.2
  103.6 0.0 copy-start.5
  103.6 0.8 copy-done.5
  104.4 2.8 %join.1 = f32[2,512,512]{2,1,0:T(8,128)} custom-call(s32[1]{0:T(128)} %bitcast.core, bf16[1024,256]{1,0:T(8,128)(2,1)} %copy-done.2, bf16[1024,256]{1,0:T(8,128)(2,1)} %copy-done.5), custom_call_target="tpu_custom_call" | custom-call | flops 524288 | bytes 3145728 | tf_op jit(solution)/shard_map/join/pallas_call | solution.py:338
  (1 shorter events, 0.0 us)
Async XLA Ops:
  6.4 10.9 %collective-permute-start = (f32[2048,128]{1,0:T(8,128)}, f32[2048,128]{1,0:T(8,128)S(1)}, u32[]{:S(2)}, u32[]{:S(2)}) collective-permute-start(f32[2048,128]{1,0:T(8,128)} %get-tuple-element.14), channel_id=1, source_target_pairs={{0,16},{16,0},{1,17},{17,1},{2,18},{18,2},{3,19},{19,3},{4,20},{20... | collective-permute-start | bytes 3145736 | tf_op jit(solution)/shard_map/ppermute | solution.py:277
  17.3 1.0 copy-start.4
  21.7 45.1 %all-to-all-start = ((bf16[128,16,640]{2,1,0:T(8,128)(2,1)}), bf16[128,16,640]{2,1,0:T(8,128)(2,1)S(1)}, u32[]{:S(2)}, u32[]{:S(2)}) async-start(bf16[128,16,640]{2,1,0:T(8,128)(2,1)} %bitcast.9), calls=%async_computation | async-start | bytes 5242880 | tf_op jit(solution)/shard_map/all_to_all | solution.py:294
  42.6 10.8 %collective-permute-start.1 = (f32[1024,512]{1,0:T(8,128)}, f32[1024,512]{1,0:T(8,128)S(1)}, u32[]{:S(2)}, u32[]{:S(2)}) collective-permute-start(f32[1024,512]{1,0:T(8,128)} %get-tuple-element.18), channel_id=1, source_target_pairs={{0,16},{16,0},{1,17},{17,1},{2,18},{18,2},{3,19},{19,3},{4,20},{20... | collective-permute-start | bytes 6291464 | tf_op jit(solution)/shard_map/ppermute | solution.py:303
  53.4 1.3 %copy-start.3 = (f32[1024,512]{1,0:T(8,128)}, f32[1024,512]{1,0:T(8,128)S(1)}, u32[]{:S(2)}) copy-start(f32[1024,512]{1,0:T(8,128)S(1)} %collective-permute-done.1.came_ref) | copy-start | bytes 6291460
  66.8 1.5 %copy-start = (bf16[128,16,640]{2,1,0:T(8,128)(2,1)}, bf16[128,16,640]{2,1,0:T(8,128)(2,1)S(1)}, u32[]{:S(2)}) copy-start(bf16[128,16,640]{2,1,0:T(8,128)(2,1)S(1)} %all-to-all-done) | copy-start | bytes 7864324
  70.4 5.6 %copy-start.6 = (s32[1,128,16]{1,2,0:T(8,128)S(1)}, s32[1,128,16]{1,2,0:T(8,128)}, u32[]{:S(2)}) copy-start(s32[1,128,16]{1,2,0:T(8,128)} %param.19) | copy-start | bytes 24580
  70.4 28.7 %all-to-all-start.1 = ((bf16[64,16,768]{2,1,0:T(8,128)(2,1)}), bf16[64,16,768]{2,1,0:T(8,128)(2,1)S(1)}, u32[]{:S(2)}, u32[]{:S(2)}) async-start(bf16[64,16,768]{2,1,0:T(8,128)(2,1)} %bitcast.8), calls=%async_computation.1 | async-start | bytes 3145728 | tf_op jit(solution)/shard_map/all_to_all | solution.py:322
  99.1 2.6 %copy-start.1 = (bf16[64,16,768]{2,1,0:T(8,128)(2,1)}, bf16[64,16,768]{2,1,0:T(8,128)(2,1)S(1)}, u32[]{:S(2)}) copy-start(bf16[64,16,768]{2,1,0:T(8,128)(2,1)S(1)} %all-to-all-done.1) | copy-start | bytes 4718596
  99.1 4.5 %copy-start.2 = (bf16[1024,256]{1,0:T(8,128)(2,1)}, bf16[1024,256]{1,0:T(8,128)(2,1)S(1)}, u32[]{:S(2)}) copy-start(bf16[1024,256]{1,0:T(8,128)(2,1)S(1)} %slice.3.mine_ref) | copy-start | bytes 1572868
  99.1 4.5 %collective-permute-start.2 = (bf16[1024,256]{1,0:T(8,128)(2,1)S(1)}, bf16[1024,256]{1,0:T(8,128)(2,1)S(1)}, u32[]{:S(2)}, u32[]{:S(2)}) collective-permute-start(bf16[1024,256]{1,0:T(8,128)(2,1)S(1)} %slice.3.mine_ref), channel_id=1, source_target_pairs={{0,16},{16,0},{1,17},{17,1},{2,18},{18,2},{3,19},{19,3},{4,20},{20... | collective-permute-start | bytes 1572872 | tf_op jit(solution)/shard_map/ppermute | solution.py:333
  103.6 0.8 copy-start.5

commit v4 on v3

--- a/solution.py
+++ b/solution.py
@@ -18,6 +18,7 @@
 OWN_BLOCKS = 8
 UNROLL = 8
 PLAN = 256
+LAYERS = 3
 VMEM = 56 << 20
 
 
@@ -91,19 +92,83 @@
     return copy
 
 
-def ghost_kernel(rows_ref, cols_ref, deg_ref, cot_ref, w_ref, vals_hbm, msg_ref, out_ref,
-                 vals, acc, plan_vmem, plan, sem, plan_sem):
-    tiles = load_tiles(2, vals_hbm, vals, sem)
-    ready = make_plan(2, rows_ref, cols_ref, plan_vmem, plan, plan_sem, HUB_BLOCKS)
-    scale = jnp.transpose(1.0 / deg_ref[...].astype(F32))
-    for r in range(NODES // TILE):
-        part = contract(cot_ref[r * TILE : (r + 1) * TILE, :], w_ref[...], 1, 1)
-        msg_ref[r * TILE : (r + 1) * TILE, :] = (part * scale[:, r : r + 1]).astype(BF16)
-    acc[...] = jnp.zeros_like(acc)
+def write_cells(region, rows_ref, cols_ref, plan_vmem):
+    cols = cols_ref[region : region + 1, :]
+    rows = rows_ref[region : region + 1, :]
+    cell = cols * (NODES // TILE) + rows
+    hot = (lax.broadcasted_iota(jnp.int32, (REG, REG), 0) == cell).astype(F32)
+    before = (
+        lax.broadcasted_iota(jnp.int32, (REG, REG), 0) < lax.broadcasted_iota(jnp.int32, (REG, REG), 1)
+    ).astype(BF16)
+    rank = jnp.sum(hot * contract(hot.astype(BF16), before, 1, 0), axis=0, keepdims=True)
+    line = lax.broadcasted_iota(jnp.int32, (8, REG), 0)
+    which = lax.broadcasted_iota(jnp.int32, (8, REG), 1).astype(F32) - REG
+    tables = jnp.zeros((8, REG), F32)
+    for layer in range(LAYERS):
+        value = jnp.where((line == layer) & (rank == layer), which, 0.0).astype(BF16)
+        tables += contract(value, hot.astype(BF16), 1, 1)
+    late = (rank >= LAYERS).astype(F32)
+    place = contract(jnp.broadcast_to(late, (8, REG)).astype(BF16), before, 1, 0)[0:1, :]
+    match = ((lax.broadcasted_iota(jnp.int32, (REG, REG), 0).astype(F32) == place) & (late > 0.0)).astype(BF16)
+    value = jnp.where(line == 3, which, jnp.where(line == 4, rows.astype(F32), jnp.where(line == 5, cols.astype(F32), 0.0)))
+    tables += contract(value.astype(BF16), match, 1, 1)
+    tables = jnp.where(line == 6, jnp.sum(late, axis=1, keepdims=True), tables)
+    plan_vmem[:, :REG] = tables.astype(jnp.int32)
+
+
+def ghost_kernel(rows_ref, cols_ref, msg_hbm, keep_hbm, came_hbm, vals_hbm, out_hbm,
+                 vals, msg, keep, came, dense, acc, out, plan_vmem, plan, sems, out_sems, plan_sem):
+    copies = [
+        pltpu.make_async_copy(
+            vals_hbm.at[pl.ds(2 * REG + k * 32, 32)], vals.at[pl.ds(k * 32, 32)], sems.at[k]
+        )
+        for k in range(4)
+    ]
+    copies.append(pltpu.make_async_copy(msg_hbm, msg, sems.at[4]))
+    copies.append(pltpu.make_async_copy(keep_hbm, keep, sems.at[5]))
+    copies.append(pltpu.make_async_copy(came_hbm, came, sems.at[6]))
+    for copy in copies:
+        copy.start()
+    vals[REG] = jnp.zeros((TILE, TILE), BF16)
+    write_cells(2, rows_ref, cols_ref, plan_vmem)
+    ready = pltpu.make_async_copy(plan_vmem, plan, plan_sem)
+    ready.start()
     ready.wait()
-    tiles.wait()
-    tile_products(HUB_BLOCKS, plan, vals, msg_ref, acc)
-    out_ref[...] = acc[...].astype(BF16)
+    for copy in copies[:4]:
+        copy.wait()
+    per = NODES // TILE
+    for c in range(HUB_BLOCKS):
+        for r in range(per):
+            total = vals[plan[0, c * per + r] + REG].astype(F32)
+            for layer in range(1, LAYERS):
+                total += vals[plan[layer, c * per + r] + REG].astype(F32)
+            dense[c, r * TILE : (r + 1) * TILE, :] = total.astype(BF16)
+    copies[4].wait()
+    copies[5].wait()
+    copies[6].wait()
+    for b in range(4):
+        lanes = slice(b * TILE, (b + 1) * TILE)
+        out[b * WIDTH : (b + 1) * WIDTH, WIDTH:] = (keep[:, lanes] + came[:, lanes]).astype(BF16)
+    for c in range(0, HUB_BLOCKS, 4):
+        lhs = jnp.concatenate([dense[c + k] for k in range(4)], axis=1)
+        acc[c * TILE : (c + 4) * TILE, :] = contract(lhs, msg[...], 0, 0)
+
+    def late(k, carry):
+        row = pl.multiple_of(plan[4, k] * TILE, TILE)
+        place = pl.ds(pl.multiple_of(plan[5, k] * TILE, TILE), TILE)
+        acc[place, :] += contract(vals[plan[3, k] + REG], msg[pl.ds(row, TILE), :], 0, 0)
+        return carry
+
+    lax.fori_loop(0, plan[6, 0], late, 0)
+    sent = []
+    piece = 4 * TILE
+    for k in range(4):
+        part = pl.ds(k * piece, piece)
+        out[part, :WIDTH] = acc[part, :].astype(BF16)
+        sent.append(pltpu.make_async_copy(out.at[part], out_hbm.at[part], out_sems.at[k]))
+        sent[-1].start()
+    for copy in sent:
+        copy.wait()
 
 
 def hub_kernel(core, rows_ref, cols_ref, msg_ref, vals_hbm, keep_ref, send_ref,
@@ -132,45 +197,8 @@
     tile_products(OWN_BLOCKS, plan, vals, msg_ref, out_ref)
 
 
-def pack_kernel(keep_ref, came_ref, packed_hbm, out_ref):
-    del packed_hbm
-    out_ref[...] = (keep_ref[...] + came_ref[...]).astype(BF16)
-
-
 def hub_pack_kernel(keep_ref, came_ref, out_ref):
     out_ref[...] = (keep_ref[...] + came_ref[...]).astype(BF16)
-
-
-def weights_kernel(core, feat_ref, agg_ref, cot_ref, keep_ref, send_ref, acc):
-    step = pl.program_id(0)
-    first = contract(feat_ref[...], cot_ref[...], 0, 0)
-    second = contract(agg_ref[...], cot_ref[...], 0, 0)
-
-    @pl.when(step == 0)
-    def _():
-        acc[:WIDTH] = first
-        acc[WIDTH:] = second
-
-    @pl.when(step != 0)
-    def _():
-        acc[:WIDTH] += first
-        acc[WIDTH:] += second
-
-    def put(ref, column):
-        for k in range(2):
-            ref[k * 2 * WIDTH : (k + 1) * 2 * WIDTH, :] = acc[:, column + k * TILE : column + (k + 1) * TILE]
-
-    last = step == pl.num_programs(0) - 1
-
-    @pl.when(last & (core[0] == 0))
-    def _():
-        put(keep_ref, 0)
-        put(send_ref, 2 * TILE)
-
-    @pl.when(last & (core[0] != 0))
-    def _():
-        put(keep_ref, 2 * TILE)
-        put(send_ref, 0)
 
 
 def spread_kernel(arrived_ref, packed_hbm, out_ref):
@@ -211,9 +239,8 @@
         place = pl.ds(pl.multiple_of(part * 256, 256), 256)
         for y in range(4):
             for c in range(2):
-                column = (2 * c + y // 2) * TILE
                 block = ref[y * 256 : (y + 1) * 256, c * TILE : (c + 1) * TILE]
-                out_ref[y % 2, place, column : column + TILE] = block.astype(F32)
+                out_ref[c, place, y * TILE : (y + 1) * TILE] = block.astype(F32)
 
 
 def whole(*shape):
@@ -257,7 +284,6 @@
     core_arg = lax.axis_index("core").reshape(1).astype(jnp.int32)
     rows = tile_rows.reshape(3, REG)
     cols = tile_cols.reshape(3, REG)
-    deg = degrees.reshape(NODES // TILE, TILE)
     targets = recv_rows.reshape(8, 256)
     spec_rc = whole(3, REG)
     spec_nodes = whole(NODES, WIDTH)
@@ -268,29 +294,34 @@
     swap = shift(1, 2)
 
     steps = 4
-    spec_rows = pl.BlockSpec((NODES // steps, WIDTH), lambda i, *_: (i, 0))
-    w_keep, w_send = call(
-        weights_kernel, "weights", 1, [spec_rows] * 3, [whole(slots, TILE)] * 2,
-        [jax.ShapeDtypeStruct((slots, TILE), F32)] * 2, [pltpu.VMEM((2 * WIDTH, WIDTH), F32)],
-        4 * NODES * WIDTH * WIDTH, 5 << 20, grid=(steps,),
-    )(core_arg, features, aggregated, cotangent)
-    w_came = lax.ppermute(w_send, "core", swap)
+    core = lax.axis_index("core")
+    w_first = contract(features, cotangent, 0, 0)
+    w_second = contract(aggregated, cotangent, 0, 0)
+    w_keep = jnp.where(core == 0, w_first, w_second)
+    w_came = lax.ppermute(jnp.where(core == 0, w_second, w_first), "core", swap)
+    msg = (contract(cotangent, w_neigh, 1, 1) / degrees[:, None].astype(F32)).astype(BF16)
 
     wide = WIDTH + TILE
-    msg, packed = call(
+    packed = call(
         ghost_kernel, "ghost", 0,
-        [spec_rc, spec_rc, whole(8, TILE), spec_nodes, spec_w, ANY],
-        [spec_nodes, whole(slots, WIDTH)],
-        [jax.ShapeDtypeStruct((NODES, WIDTH), BF16), jax.ShapeDtypeStruct((slots, wide), BF16)],
-        tile_scratch(True), region_flops + 2 * NODES * WIDTH * WIDTH, region_bytes + (2 << 20),
-    )(rows, cols, deg, cotangent, w_neigh, tile_vals)
-    spec_part = pl.BlockSpec((slots // steps, TILE), lambda i: (i, 0))
-    packed = call(
-        pack_kernel, "pack", 0, [spec_part, spec_part, ANY],
-        pl.BlockSpec((slots // steps, TILE), lambda i: (i, WIDTH // TILE)),
+        [spec_rc, spec_rc, ANY, ANY, ANY, ANY], ANY,
         jax.ShapeDtypeStruct((slots, wide), BF16),
-        [], slots * TILE, 3 << 20, grid=(steps,), input_output_aliases={2: 0},
-    )(w_keep, w_came, packed)
+        [
+            pltpu.VMEM((REG + 1, TILE, TILE), BF16),
+            pltpu.VMEM((NODES, WIDTH), BF16),
+            pltpu.VMEM((WIDTH, WIDTH), F32),
+            pltpu.VMEM((WIDTH, WIDTH), F32),
+            pltpu.VMEM((HUB_BLOCKS, NODES, TILE), BF16),
+            pltpu.VMEM((slots, WIDTH), F32),
+            pltpu.VMEM((slots, wide), BF16),
+            pltpu.VMEM((8, PLAN), jnp.int32),
+            pltpu.SMEM((8, PLAN), jnp.int32),
+            pltpu.SemaphoreType.DMA((7,)),
+            pltpu.SemaphoreType.DMA((4,)),
+            pltpu.SemaphoreType.DMA,
+        ],
+        region_flops, region_bytes + (2 << 20),
+    )(rows, cols, msg, w_keep, w_came, tile_vals)
     arrived = lax.all_to_all(
         packed.reshape(128, 16, wide), ALL, split_axis=0, concat_axis=0, tiled=True
     ).reshape(slots, wide)

time: 108 us -> 105 us (0.972)
  Pallas kernels: 55.7 us -> 46.5 us
  matrix products: 0 us -> 5.92 us
  starting transfers between devices: 20.8 us -> 22.5 us
  local copies, waits for them, and re-layouts: 5.42 us -> 3.98 us
    pallas_call x3 -> x1, Pallas kernels: 18.7 us -> 9.34 us  [local(): call(ghost_kernel, 'ghost', 0, [spec_rc, spec_rc, ANY, ANY, ANY, ANY], AN...]
    dot_general x0 -> x3, matrix products: none -> 5.92 us  [contract(): lax.dot_general(a, b, (((da,), (db,)), ((), ())), preferred_element_type=...]
    all_to_all x1, starting transfers between devices: 10.1 us -> 11.8 us  [local(): lax.all_to_all(packed.reshape(128, 16, wide), ALL, split_axis=0, concat_a...]
    unnamed x15 -> x21, local copies, waits for them, and re-layouts: 4.7 us -> 3.25 us
  transfers between devices with their start and end apart: 5 -> 5, of which waited for: 2 -> 3; matrix products, arithmetic and copies ran while one was open for 1% -> 2% of each run, Pallas kernels for 39% -> 31%
where the time goes in v4:
time: 105 us; the launch traced here: 104 us
  Pallas kernels  46.5 us (44%)
  waiting for transfers between devices  24.6 us (23%)
  starting transfers between devices  22.5 us (21%)
  matrix products  5.92 us (6%)
  local copies, waits for them, and re-layouts  3.98 us (4%)
    all_to_all x1, waiting for transfers between devices, local(): lax.all_to_all(packed.reshape(64, 16, wider), ('y', 'z', 'x'), split_axis...  16.4 us
    all_to_all x1, starting transfers between devices, local(): lax.all_to_all(packed.reshape(128, 16, wide), ALL, split_axis=0, concat_a...  11.8 us
    pallas_call x1, Pallas kernels, local(): call(hub_kernel, 'hub', 1, [spec_rc, spec_rc, spec_nodes, ANY], [spec_nod...  10.7 us
    pallas_call x1, Pallas kernels, local(): call(own_kernel, 'own', 0, [spec_rc, spec_rc, spec_nodes, spec_nodes, spe...  9.63 us
    pallas_call x1, Pallas kernels, local(): call(ghost_kernel, 'ghost', 0, [spec_rc, spec_rc, ANY, ANY, ANY, ANY], AN...  9.34 us
    all_to_all x1, waiting for transfers between devices, local(): lax.all_to_all(packed.reshape(128, 16, wide), ALL, split_axis=0, concat_a...  7.67 us
    dot_general x3, matrix products, contract(): lax.dot_general(a, b, (((da,), (db,)), ((), ())), preferred_element_type=...  5.92 us
    pallas_call x1, Pallas kernels, local(): call(landing_kernel, 'landing', 0, [whole(8, 256), spec_nodes, whole(slot...  5.88 us
  transfers between devices with their start and end apart: 5, of which 3 were waited for; matrix products, arithmetic and copies ran while one was open for 2% of the time, Pallas kernels for 31%

profile of v4, /device:TPU:1, one launch (start us, length us, event | category | flops | bytes accessed | tf_op | source)
XLA Modules:
  0.0 104.2 jit_solution(15468079694372844909)
XLA Ops:
  0.6 0.0 copy-start
  0.7 0.0 copy-start.2
  0.7 2.4 %fusion = f32[512,512]{1,0:T(8,128)S(1)} fusion(bf16[1024,512]{1,0:T(8,128)(2,1)} %param.10, bf16[1024,512]{1,0:T(8,128)(2,1)} %cot_ref.1), kind=kOutput, calls=%fused_computation.3 | convolution fusion | flops 536870912 | bytes 3145728 | tf_op jit(solution)/shard_map/dot_general | solution.py:26
  3.1 0.0 copy-done
  3.1 0.0 copy-done.2
  3.1 0.0 copy-start.8
  3.1 0.0 copy-start.9
  3.1 1.7 %broadcast_select_fusion = (f32[512,512]{1,0:T(8,128)S(1)}, f32[512,512]{1,0:T(8,128)}) fusion(f32[512,512]{1,0:T(8,128)S(1)} %fusion, pred[]{:T(512)S(6)} %eq.4, bf16[1024,512]{1,0:T(8,128)(2,1)S(1)} %copy-done, bf16[1024,512]{1,0:T(8,128)(2,1)S(1)} %copy-done.2), kind=kOutput, calls=%fused_computation.1 | convolution fusion | flops 537395200 | bytes 5242881 | tf_op jit(solution)/shard_map/dot_general | solution.py:26
  4.8 1.4 %collective-permute-start = (f32[512,512]{1,0:T(8,128)S(1)}, f32[512,512]{1,0:T(8,128)S(1)}, u32[]{:S(2)}, u32[]{:S(2)}) collective-permute-start(f32[512,512]{1,0:T(8,128)S(1)} %get-tuple-element.15), channel_id=1, source_target_pairs={{0,16},{16,0},{1,17},{17,1},{2,18},{18,2},{3,19},{19,3},{4,20},{20... | collective-permute-start | bytes 3145736 | tf_op jit(solution)/shard_map/ppermute | solution.py:301
  6.3 0.0 copy-done.8
  6.3 0.0 copy-done.9
  6.3 1.8 %divide_convert_fusion.msg_hbm.msg_ref = bf16[1024,512]{1,0:T(8,128)(2,1)} fusion(bf16[1024,512]{1,0:T(8,128)(2,1)S(1)} %copy-done.2, bf16[512,512]{1,0:T(8,128)(2,1)S(1)} %copy-done.9, f32[1024]{0:T(1024)S(1)} %convert_element_type.7), kind=kOutput, calls=%fused_computation | convolution fusion | flops 537919488 | bytes 2625536 | tf_op jit(solution)/shard_map/dot_general | solution.py:26
  8.1 0.5 collective-permute-done.came_hbm
  8.5 0.0 copy-start.5
  8.5 1.0 copy-done.5
  9.5 9.3 %ghost.1 = bf16[2048,640]{1,0:T(8,128)(2,1)} custom-call(s32[3,128]{1,0:T(4,128)} %bitcast.17, s32[3,128]{1,0:T(4,128)} %bitcast.20, bf16[1024,512]{1,0:T(8,128)(2,1)} %divide_convert_fusion.msg_hbm.msg_ref, f32[512,512]{1,0:T(8,128)} %get-tuple-element.16.keep_hbm, f32[512,512]{1,0:T(8,128)} %copy-done.5, bf16[384,128,128]{2,1,0:T(8,128)(2,1)} %vals_hbm.5), custom_call_target="tpu_custom_call" | custom-call | flops 2147483648 | bytes 9437184 | tf_op jit(solution)/shard_map/ghost/pallas_call | solution.py:305
  18.9 11.8 %all-to-all-start = ((bf16[128,16,640]{2,1,0:T(8,128)(2,1)}), bf16[128,16,640]{2,1,0:T(8,128)(2,1)}, u32[]{:S(2)}, u32[]{:S(2)}) async-start(bf16[128,16,640]{2,1,0:T(8,128)(2,1)} %bitcast.14), calls=%async_computation | async-start | bytes 5242880 | tf_op jit(solution)/shard_map/all_to_all | solution.py:325
  30.7 10.7 %hub.1 = (f32[1024,512]{1,0:T(8,128)}, f32[1024,512]{1,0:T(8,128)}) custom-call(s32[1]{0:T(128)} %bitcast.4.core, s32[3,128]{1,0:T(4,128)} %bitcast.18, s32[3,128]{1,0:T(4,128)} %bitcast.21, bf16[1024,512]{1,0:T(8,128)(2,1)} %divide_convert_fusion.msg_hbm.msg_ref, bf16[384,128,128]{2,1,0:T(8,128)(2,1)} %vals_hbm.5), custom_call_target="tpu_custom_call" | custom-call | flops 2147483648 | bytes 9437184 | tf_op jit(solution)/shard_map/hub/pallas_call | solution.py:329
  41.4 1.2 %collective-permute-start.1 = (f32[1024,512]{1,0:T(8,128)}, f32[1024,512]{1,0:T(8,128)S(1)}, u32[]{:S(2)}, u32[]{:S(2)}) collective-permute-start(f32[1024,512]{1,0:T(8,128)} %get-tuple-element.10), channel_id=1, source_target_pairs={{0,16},{16,0},{1,17},{17,1},{2,18},{18,2},{3,19},{19,3},{4,20},{20... | collective-permute-start | bytes 6291464 | tf_op jit(solution)/shard_map/ppermute | solution.py:334
  42.6 9.6 %own.1.own_ref = f32[1024,512]{1,0:T(8,128)} custom-call(s32[3,128]{1,0:T(4,128)} %bitcast.19, s32[3,128]{1,0:T(4,128)} %bitcast.22, bf16[1024,512]{1,0:T(8,128)(2,1)} %divide_convert_fusion.msg_hbm.msg_ref, bf16[1024,512]{1,0:T(8,128)(2,1)} %cot_ref.1, bf16[512,512]{1,0:T(8,128)(2,1)} %w_ref.1, bf16[384,128,128]{2,1,0:T(8,128)(2,1)} %vals_hbm.5), custom_call_target="tpu_custom_call" | custom-call | flops 2684354560 | bytes 7340032 | tf_op jit(solution)/shard_map/own/pallas_call | solution.py:335
  52.2 0.0 collective-permute-done.1.came_ref
  52.2 0.0 copy-start.4
  52.2 1.3 %copy-done.4 = f32[1024,512]{1,0:T(8,128)} copy-done((f32[1024,512]{1,0:T(8,128)}, f32[1024,512]{1,0:T(8,128)S(1)}, u32[]{:S(2)}) %copy-start.4) | copy-done | bytes 2097176
  53.6 4.1 %hub_pack.1.packed_hbm = bf16[1024,768]{1,0:T(8,128)(2,1)} custom-call(f32[1024,512]{1,0:T(8,128)} %get-tuple-element.9.keep_ref, f32[1024,512]{1,0:T(8,128)} %copy-done.4), custom_call_target="tpu_custom_call" | custom-call | flops 524288 | bytes 5242880 | tf_op jit(solution)/shard_map/hub_pack/pallas_call | solution.py:343
  57.6 7.7 %all-to-all-done = bf16[128,16,640]{2,1,0:T(8,128)(2,1)} async-done(((bf16[128,16,640]{2,1,0:T(8,128)(2,1)}), bf16[128,16,640]{2,1,0:T(8,128)(2,1)}, u32[]{:S(2)}, u32[]{:S(2)}) %all-to-all-start) | async-done | bytes 2621472 | tf_op jit(solution)/shard_map/all_to_all | solution.py:325
  65.3 2.1 %spread.1 = bf16[1024,768]{1,0:T(8,128)(2,1)} custom-call(bf16[2048,640]{1,0:T(8,128)(2,1)} %bitcast.3.arrived_ref, bf16[1024,768]{1,0:T(8,128)(2,1)} %hub_pack.1.packed_hbm), custom_call_target="tpu_custom_call", output_to_operand_aliasing={{}: (1, {})} | custom-call | flops 262144 | bytes 1048576 | tf_op jit(solution)/shard_map/spread/pallas_call | solution.py:348
  67.4 0.0 copy-start.7
  67.4 5.6 %all-to-all-start.1 = ((bf16[64,16,768]{2,1,0:T(8,128)(2,1)}), bf16[64,16,768]{2,1,0:T(8,128)(2,1)S(1)}, u32[]{:S(2)}, u32[]{:S(2)}) async-start(bf16[64,16,768]{2,1,0:T(8,128)(2,1)} %bitcast.13), calls=%async_computation.1 | async-start | bytes 3145728 | tf_op jit(solution)/shard_map/all_to_all | solution.py:353
  73.0 0.0 copy-done.7
  73.0 0.1 copy.15
  73.1 0.7 reshape.39.targets_ref
  73.8 5.9 %landing.1 = f32[1024,512]{1,0:T(8,128)} custom-call(s32[8,256]{1,0:T(8,128)} %reshape.39.targets_ref, f32[1024,512]{1,0:T(8,128)} %own.1.own_ref, bf16[2048,640]{1,0:T(8,128)(2,1)} %bitcast.3.arrived_ref), custom_call_target="tpu_custom_call" | custom-call | flops 2147483648 | bytes 7340032 | tf_op jit(solution)/shard_map/landing/pallas_call | solution.py:357
  79.6 16.4 %all-to-all-done.1 = bf16[64,16,768]{2,1,0:T(8,128)(2,1)S(1)} async-done(((bf16[64,16,768]{2,1,0:T(8,128)(2,1)}), bf16[64,16,768]{2,1,0:T(8,128)(2,1)S(1)}, u32[]{:S(2)}, u32[]{:S(2)}) %all-to-all-start.1) | async-done | bytes 1572896 | tf_op jit(solution)/shard_map/all_to_all | solution.py:353
  96.1 0.0 copy-start.1
  96.1 0.0 copy-start.3
  96.1 2.5 %collective-permute-start.2 = (bf16[1024,256]{1,0:T(8,128)(2,1)S(1)}, bf16[1024,256]{1,0:T(8,128)(2,1)S(1)}, u32[]{:S(2)}, u32[]{:S(2)}) collective-permute-start(bf16[1024,256]{1,0:T(8,128)(2,1)S(1)} %slice.3.mine_ref), channel_id=1, source_target_pairs={{0,16},{16,0},{1,17},{17,1},{2,18},{18,2},{3,19},{19,3},{4,20},{20... | collective-permute-start | bytes 1572872 | tf_op jit(solution)/shard_map/ppermute | solution.py:364
  98.6 0.0 copy-done.1
  98.6 2.0 %hub_sum.1 = f32[16,512]{1,0:T(8,128)} custom-call(bf16[1024,768]{1,0:T(8,128)(2,1)} %bitcast.16), custom_call_target="tpu_custom_call" | custom-call | flops 524288 | bytes 1048576 | tf_op jit(solution)/shard_map/hub_sum/pallas_call | solution.py:365
  100.6 0.0 collective-permute-done.2.came_ref
  100.6 0.0 copy-done.3
  100.6 0.0 copy-start.6
  100.7 0.8 copy-done.6
  101.5 2.8 %join.1 = f32[2,512,512]{2,1,0:T(8,128)} custom-call(s32[1]{0:T(128)} %bitcast.4.core, bf16[1024,256]{1,0:T(8,128)(2,1)} %copy-done.3, bf16[1024,256]{1,0:T(8,128)(2,1)} %copy-done.6), custom_call_target="tpu_custom_call" | custom-call | flops 524288 | bytes 3145728 | tf_op jit(solution)/shard_map/join/pallas_call | solution.py:369
  (2 shorter events, 0.0 us)
Async XLA Ops:
  0.6 2.5 %copy-start = (bf16[1024,512]{1,0:T(8,128)(2,1)S(1)}, bf16[1024,512]{1,0:T(8,128)(2,1)}, u32[]{:S(2)}) copy-start(bf16[1024,512]{1,0:T(8,128)(2,1)} %param.11) | copy-start | bytes 3145732
  0.7 2.4 %copy-start.2 = (bf16[1024,512]{1,0:T(8,128)(2,1)S(1)}, bf16[1024,512]{1,0:T(8,128)(2,1)}, u32[]{:S(2)}) copy-start(bf16[1024,512]{1,0:T(8,128)(2,1)} %cot_ref.1) | copy-start | bytes 3145732
  3.1 3.2 %copy-start.8 = (s32[1024]{0:T(1024)S(1)}, s32[1024]{0:T(1024)}, u32[]{:S(2)}) copy-start(s32[1024]{0:T(1024)} %param.15) | copy-start | bytes 12292
  3.1 3.2 %copy-start.9 = (bf16[512,512]{1,0:T(8,128)(2,1)S(1)}, bf16[512,512]{1,0:T(8,128)(2,1)}, u32[]{:S(2)}) copy-start(bf16[512,512]{1,0:T(8,128)(2,1)} %param.14) | copy-start | bytes 1572868
  4.8 3.7 %collective-permute-start = (f32[512,512]{1,0:T(8,128)S(1)}, f32[512,512]{1,0:T(8,128)S(1)}, u32[]{:S(2)}, u32[]{:S(2)}) collective-permute-start(f32[512,512]{1,0:T(8,128)S(1)} %get-tuple-element.15), channel_id=1, source_target_pairs={{0,16},{16,0},{1,17},{17,1},{2,18},{18,2},{3,19},{19,3},{4,20},{20... | collective-permute-start | bytes 3145736 | tf_op jit(solution)/shard_map/ppermute | solution.py:301
  8.5 1.0 copy-start.5
  18.9 46.4 %all-to-all-start = ((bf16[128,16,640]{2,1,0:T(8,128)(2,1)}), bf16[128,16,640]{2,1,0:T(8,128)(2,1)}, u32[]{:S(2)}, u32[]{:S(2)}) async-start(bf16[128,16,640]{2,1,0:T(8,128)(2,1)} %bitcast.14), calls=%async_computation | async-start | bytes 5242880 | tf_op jit(solution)/shard_map/all_to_all | solution.py:325
  41.4 10.8 %collective-permute-start.1 = (f32[1024,512]{1,0:T(8,128)}, f32[1024,512]{1,0:T(8,128)S(1)}, u32[]{:S(2)}, u32[]{:S(2)}) collective-permute-start(f32[1024,512]{1,0:T(8,128)} %get-tuple-element.10), channel_id=1, source_target_pairs={{0,16},{16,0},{1,17},{17,1},{2,18},{18,2},{3,19},{19,3},{4,20},{20... | collective-permute-start | bytes 6291464 | tf_op jit(solution)/shard_map/ppermute | solution.py:334
  52.2 1.4 %copy-start.4 = (f32[1024,512]{1,0:T(8,128)}, f32[1024,512]{1,0:T(8,128)S(1)}, u32[]{:S(2)}) copy-start(f32[1024,512]{1,0:T(8,128)S(1)} %collective-permute-done.1.came_ref) | copy-start | bytes 6291460
  67.4 5.6 %copy-start.7 = (s32[1,128,16]{1,2,0:T(8,128)S(1)}, s32[1,128,16]{1,2,0:T(8,128)}, u32[]{:S(2)}) copy-start(s32[1,128,16]{1,2,0:T(8,128)} %param.19) | copy-start | bytes 24580
  67.4 28.7 %all-to-all-start.1 = ((bf16[64,16,768]{2,1,0:T(8,128)(2,1)}), bf16[64,16,768]{2,1,0:T(8,128)(2,1)S(1)}, u32[]{:S(2)}, u32[]{:S(2)}) async-start(bf16[64,16,768]{2,1,0:T(8,128)(2,1)} %bitcast.13), calls=%async_computation.1 | async-start | bytes 3145728 | tf_op jit(solution)/shard_map/all_to_all | solution.py:353
  96.1 2.6 %copy-start.1 = (bf16[64,16,768]{2,1,0:T(8,128)(2,1)}, bf16[64,16,768]{2,1,0:T(8,128)(2,1)S(1)}, u32[]{:S(2)}) copy-start(bf16[64,16,768]{2,1,0:T(8,128)(2,1)S(1)} %all-to-all-done.1) | copy-start | bytes 4718596
  96.1 4.5 %copy-start.3 = (bf16[1024,256]{1,0:T(8,128)(2,1)}, bf16[1024,256]{1,0:T(8,128)(2,1)S(1)}, u32[]{:S(2)}) copy-start(bf16[1024,256]{1,0:T(8,128)(2,1)S(1)} %slice.3.mine_ref) | copy-start | bytes 1572868
  96.1 4.5 %collective-permute-start.2 = (bf16[1024,256]{1,0:T(8,128)(2,1)S(1)}, bf16[1024,256]{1,0:T(8,128)(2,1)S(1)}, u32[]{:S(2)}, u32[]{:S(2)}) collective-permute-start(bf16[1024,256]{1,0:T(8,128)(2,1)S(1)} %slice.3.mine_ref), channel_id=1, source_target_pairs={{0,16},{16,0},{1,17},{17,1},{2,18},{18,2},{3,19},{19,3},{4,20},{20... | collective-permute-start | bytes 1572872 | tf_op jit(solution)/shard_map/ppermute | solution.py:364
  100.6 0.8 copy-start.6

commit v5 on v4

--- a/solution.py
+++ b/solution.py
@@ -19,7 +19,7 @@
 UNROLL = 8
 PLAN = 256
 LAYERS = 3
-VMEM = 56 << 20
+VMEM = 28 << 20
 
 
 def contract(a, b, da, db):
@@ -116,26 +116,17 @@
     plan_vmem[:, :REG] = tables.astype(jnp.int32)
 
 
-def ghost_kernel(rows_ref, cols_ref, msg_hbm, keep_hbm, came_hbm, vals_hbm, out_hbm,
-                 vals, msg, keep, came, dense, acc, out, plan_vmem, plan, sems, out_sems, plan_sem):
-    copies = [
-        pltpu.make_async_copy(
-            vals_hbm.at[pl.ds(2 * REG + k * 32, 32)], vals.at[pl.ds(k * 32, 32)], sems.at[k]
-        )
-        for k in range(4)
-    ]
-    copies.append(pltpu.make_async_copy(msg_hbm, msg, sems.at[4]))
-    copies.append(pltpu.make_async_copy(keep_hbm, keep, sems.at[5]))
-    copies.append(pltpu.make_async_copy(came_hbm, came, sems.at[6]))
-    for copy in copies:
-        copy.start()
-    vals[REG] = jnp.zeros((TILE, TILE), BF16)
+def ghost_kernel(rows_ref, cols_ref, msg, keep, came, vals_hbm, out_hbm,
+                 vals, dense, acc, out, plan_vmem, plan, sem, out_sems, plan_sem):
+    tiles = load_tiles(2, vals_hbm, vals, sem)
     write_cells(2, rows_ref, cols_ref, plan_vmem)
     ready = pltpu.make_async_copy(plan_vmem, plan, plan_sem)
     ready.start()
+    for b in range(4):
+        lanes = slice(b * TILE, (b + 1) * TILE)
+        out[b * WIDTH : (b + 1) * WIDTH, WIDTH:] = (keep[:, lanes] + came[:, lanes]).astype(BF16)
     ready.wait()
-    for copy in copies[:4]:
-        copy.wait()
+    tiles.wait()
     per = NODES // TILE
     for c in range(HUB_BLOCKS):
         for r in range(per):
@@ -143,12 +134,6 @@
             for layer in range(1, LAYERS):
                 total += vals[plan[layer, c * per + r] + REG].astype(F32)
             dense[c, r * TILE : (r + 1) * TILE, :] = total.astype(BF16)
-    copies[4].wait()
-    copies[5].wait()
-    copies[6].wait()
-    for b in range(4):
-        lanes = slice(b * TILE, (b + 1) * TILE)
-        out[b * WIDTH : (b + 1) * WIDTH, WIDTH:] = (keep[:, lanes] + came[:, lanes]).astype(BF16)
     for c in range(0, HUB_BLOCKS, 4):
         lhs = jnp.concatenate([dense[c + k] for k in range(4)], axis=1)
         acc[c * TILE : (c + 4) * TILE, :] = contract(lhs, msg[...], 0, 0)
@@ -248,6 +233,8 @@
 
 
 ANY = pl.BlockSpec(memory_space=pl.ANY)
+INSIDE = pl.BlockSpec(memory_space=pltpu.VMEM)
+OUTSIDE = pl.BlockSpec(memory_space=pltpu.HBM)
 
 
 def call(kernel, name, scalars, ins, outs, shapes, scratch, flops, moved, grid=(1,), **more):
@@ -292,6 +279,7 @@
     region_flops = 2 * REG * TILE * TILE * WIDTH
     region_bytes = REG * TILE * TILE * 2 + NODES * WIDTH * 2 + slots * WIDTH * 2
     swap = shift(1, 2)
+    tile_vals = pltpu.with_memory_space_constraint(tile_vals, pltpu.HBM)
 
     steps = 4
     core = lax.axis_index("core")
@@ -304,36 +292,33 @@
     wide = WIDTH + TILE
     packed = call(
         ghost_kernel, "ghost", 0,
-        [spec_rc, spec_rc, ANY, ANY, ANY, ANY], ANY,
-        jax.ShapeDtypeStruct((slots, wide), BF16),
+        [INSIDE] * 5 + [OUTSIDE], OUTSIDE,
+        pltpu.HBM((slots, wide), BF16),
         [
             pltpu.VMEM((REG + 1, TILE, TILE), BF16),
-            pltpu.VMEM((NODES, WIDTH), BF16),
-            pltpu.VMEM((WIDTH, WIDTH), F32),
-            pltpu.VMEM((WIDTH, WIDTH), F32),
             pltpu.VMEM((HUB_BLOCKS, NODES, TILE), BF16),
             pltpu.VMEM((slots, WIDTH), F32),
             pltpu.VMEM((slots, wide), BF16),
             pltpu.VMEM((8, PLAN), jnp.int32),
             pltpu.SMEM((8, PLAN), jnp.int32),
-            pltpu.SemaphoreType.DMA((7,)),
+            pltpu.SemaphoreType.DMA,
             pltpu.SemaphoreType.DMA((4,)),
             pltpu.SemaphoreType.DMA,
         ],
-        region_flops, region_bytes + (2 << 20),
+        region_flops, region_bytes + (2 << 20), grid=(),
     )(rows, cols, msg, w_keep, w_came, tile_vals)
     arrived = lax.all_to_all(
         packed.reshape(128, 16, wide), ALL, split_axis=0, concat_axis=0, tiled=True
     ).reshape(slots, wide)
 
     hub_keep, hub_send = call(
-        hub_kernel, "hub", 1, [spec_rc, spec_rc, spec_nodes, ANY], [spec_nodes, spec_nodes],
+        hub_kernel, "hub", 1, [spec_rc, spec_rc, spec_nodes, OUTSIDE], [spec_nodes, spec_nodes],
         [jax.ShapeDtypeStruct((NODES, WIDTH), F32)] * 2,
         tile_scratch(True), region_flops, region_bytes + (2 << 20),
     )(core_arg, rows, cols, msg, tile_vals)
     hub_came = lax.ppermute(hub_send, "core", swap)
     own = call(
-        own_kernel, "own", 0, [spec_rc, spec_rc, spec_nodes, spec_nodes, spec_w, ANY], spec_nodes,
+        own_kernel, "own", 0, [spec_rc, spec_rc, spec_nodes, spec_nodes, spec_w, OUTSIDE], spec_nodes,
         jax.ShapeDtypeStruct((NODES, WIDTH), F32),
         tile_scratch(False), region_flops + 2 * NODES * WIDTH * WIDTH, region_bytes,
     )(rows, cols, msg, cotangent, w_self, tile_vals)

time: 105 us -> 98.3 us (0.936)
  Pallas kernels: 46.5 us -> 31.4 us
  waiting for transfers between devices: 24.6 us -> 35.6 us
  matrix products: 5.92 us -> 3.89 us
    all_to_all x1, waiting for transfers between devices: 7.67 us -> 17.3 us  [local(): lax.all_to_all(packed.reshape(128, 16, wide), ALL, split_axis=0, concat_a...]
    pallas_call x2, Pallas kernels: 20 us -> 13.8 us  [the longest x1 7.02 us: local(): call(ghost_kernel, 'ghost', 0, [INSIDE] * 5 + [OUTSIDE], OUTSIDE, pltpu.H...]
    pallas_call x1, Pallas kernels: 9.63 us -> 6.29 us  [local(): call(own_kernel, 'own', 0, [spec_rc, spec_rc, spec_nodes, spec_nodes, spe...]
    pallas_call x1, Pallas kernels: 4.06 us -> 1.69 us  [local(): call(hub_pack_kernel, 'hub_pack', 0, [spec_hub, spec_hub], spec_hub, jax....]
    dot_general x3, matrix products: 5.92 us -> 3.89 us  [contract(): lax.dot_general(a, b, (((da,), (db,)), ((), ())), preferred_element_type=...]
    pallas_call x1, Pallas kernels: 2.01 us -> 0.79 us  [local(): call(hub_sum_kernel, 'hub_sum', 0, [spec_nodes], whole(16, WIDTH), jax.Sh...]
    pallas_call x1, Pallas kernels: 2.79 us -> 1.59 us  [local(): call(join_kernel, 'join', 1, [whole(NODES, 2 * TILE)] * 2, whole(2, WIDTH...]
  transfers between devices with their start and end apart: 5 -> 5, of which waited for: 3 -> 4; matrix products, arithmetic and copies ran while one was open for 2% -> 1% of each run, Pallas kernels for 31% -> 21%
where the time goes in v5:
time: 98.3 us; the launch traced here: 97.9 us
  waiting for transfers between devices  35.6 us (36%)
  Pallas kernels  31.4 us (32%)
  starting transfers between devices  23 us (23%)
  matrix products  3.89 us (4%)
  local copies, waits for them, and re-layouts  3.17 us (3%)
    all_to_all x1, waiting for transfers between devices, local(): lax.all_to_all(packed.reshape(128, 16, wide), ALL, split_axis=0, concat_a...  17.3 us
    all_to_all x1, waiting for transfers between devices, local(): lax.all_to_all(packed.reshape(64, 16, wider), ('y', 'z', 'x'), split_axis...  16.1 us
    all_to_all x1, starting transfers between devices, local(): lax.all_to_all(packed.reshape(128, 16, wide), ALL, split_axis=0, concat_a...  12.2 us
    pallas_call x1, Pallas kernels, local(): call(ghost_kernel, 'ghost', 0, [INSIDE] * 5 + [OUTSIDE], OUTSIDE, pltpu.H...  7.02 us
    pallas_call x1, Pallas kernels, local(): call(hub_kernel, 'hub', 1, [spec_rc, spec_rc, spec_nodes, OUTSIDE], [spec...  6.79 us
    pallas_call x1, Pallas kernels, local(): call(own_kernel, 'own', 0, [spec_rc, spec_rc, spec_nodes, spec_nodes, spe...  6.29 us
    all_to_all x1, starting transfers between devices, local(): lax.all_to_all(packed.reshape(64, 16, wider), ('y', 'z', 'x'), split_axis...  5.58 us
    pallas_call x1, Pallas kernels, local(): call(landing_kernel, 'landing', 0, [whole(8, 256), spec_nodes, whole(slot...  5.23 us
  transfers between devices with their start and end apart: 5, of which 4 were waited for; matrix products, arithmetic and copies ran while one was open for 1% of the time, Pallas kernels for 21%

profile of v5, /device:TPU:1, one launch (start us, length us, event | category | flops | bytes accessed | tf_op | source)
XLA Modules:
  0.0 97.9 jit_solution(13971362141580976576)
XLA Ops:
  0.6 0.0 copy-start
  0.7 0.0 copy-start.1
  0.7 2.4 %fusion = f32[512,512]{1,0:T(8,128)S(1)} fusion(bf16[1024,512]{1,0:T(8,128)(2,1)} %param.10, bf16[1024,512]{1,0:T(8,128)(2,1)} %cot_ref.1), kind=kOutput, calls=%fused_computation.3 | convolution fusion | flops 536870912 | bytes 3145728 | tf_op jit(solution)/shard_map/dot_general | solution.py:26
  3.1 0.0 copy-done
  3.1 0.0 copy-done.1
  3.1 0.0 copy-start.8
  3.1 0.0 copy-start.9
  3.1 0.7 broadcast_select_fusion
  3.9 1.5 %collective-permute-start = (f32[512,512]{1,0:T(8,128)S(1)}, f32[512,512]{1,0:T(8,128)S(1)}, u32[]{:S(2)}, u32[]{:S(2)}) collective-permute-start(f32[512,512]{1,0:T(8,128)S(1)} %get-tuple-element.15), channel_id=1, source_target_pairs={{0,16},{16,0},{1,17},{17,1},{2,18},{18,2},{3,19},{19,3},{4,20},{20... | collective-permute-start | bytes 3145736 | tf_op jit(solution)/shard_map/ppermute | solution.py:289
  5.4 0.0 copy-done.8
  5.4 0.0 copy-done.9
  5.4 0.0 copy-start.5
  5.4 0.0 copy-start.6
  5.4 0.7 divide_convert_fusion.msg.msg_ref
  6.2 1.5 %collective-permute-done.came = f32[512,512]{1,0:T(8,128)S(1)} collective-permute-done((f32[512,512]{1,0:T(8,128)S(1)}, f32[512,512]{1,0:T(8,128)S(1)}, u32[]{:S(2)}, u32[]{:S(2)}) %collective-permute-start) | collective-permute-done | bytes 1048608 | tf_op jit(solution)/shard_map/ppermute | solution.py:289
  7.7 0.0 copy-done.5
  7.7 0.0 copy-done.6
  7.7 7.0 %ghost.1 = bf16[2048,640]{1,0:T(8,128)(2,1)} custom-call(s32[3,128]{1,0:T(4,128)S(1)} %bitcast.15, s32[3,128]{1,0:T(4,128)S(1)} %bitcast.18, bf16[1024,512]{1,0:T(8,128)(2,1)S(1)} %divide_convert_fusion.msg.msg_ref, f32[512,512]{1,0:T(8,128)S(1)} %get-tuple-element.16.keep, f32[512,512]{1,0:T(8,128)S(1)} %collective-permute-done.came, ...), custom_call_target="tpu_custom_call" | custom-call | flops 2147483648 | bytes 9437184 | tf_op jit(solution)/shard_map/ghost/pallas_call | solution.py:293
  14.7 12.2 %all-to-all-start = ((bf16[128,16,640]{2,1,0:T(8,128)(2,1)}), bf16[128,16,640]{2,1,0:T(8,128)(2,1)}, u32[]{:S(2)}, u32[]{:S(2)}) async-start(bf16[128,16,640]{2,1,0:T(8,128)(2,1)} %bitcast.21), calls=%async_computation | async-start | bytes 5242880 | tf_op jit(solution)/shard_map/all_to_all | solution.py:310
  26.9 0.0 copy-start.4
  26.9 6.8 %hub.1 = (f32[1024,512]{1,0:T(8,128)S(1)}, f32[1024,512]{1,0:T(8,128)S(1)}) custom-call(s32[1]{0:T(128)} %bitcast.4.core, s32[3,128]{1,0:T(4,128)S(1)} %bitcast.16, s32[3,128]{1,0:T(4,128)S(1)} %bitcast.19, bf16[1024,512]{1,0:T(8,128)(2,1)S(1)} %divide_convert_fusion.msg.msg_ref, bf16[384,128,128]{2,1,0:T(8,128)(2,1)} %vals_hbm.5), custom_call_target="tpu_custom_call" | custom-call | flops 2147483648 | bytes 9437184 | tf_op jit(solution)/shard_map/hub/pallas_call | solution.py:314
  33.7 1.2 %collective-permute-start.1 = (f32[1024,512]{1,0:T(8,128)S(1)}, f32[1024,512]{1,0:T(8,128)S(1)}, u32[]{:S(2)}, u32[]{:S(2)}) collective-permute-start(f32[1024,512]{1,0:T(8,128)S(1)} %get-tuple-element.10), channel_id=1, source_target_pairs={{0,16},{16,0},{1,17},{17,1},{2,18},{18,2},{3,19},{19,3},{4,20},{20... | collective-permute-start | bytes 6291464 | tf_op jit(solution)/shard_map/ppermute | solution.py:319
  34.9 0.0 copy-done.4
  34.9 6.3 %own.1.own_ref = f32[1024,512]{1,0:T(8,128)S(1)} custom-call(s32[3,128]{1,0:T(4,128)S(1)} %bitcast.17, s32[3,128]{1,0:T(4,128)S(1)} %bitcast.20, bf16[1024,512]{1,0:T(8,128)(2,1)S(1)} %divide_convert_fusion.msg.msg_ref, bf16[1024,512]{1,0:T(8,128)(2,1)S(1)} %copy-done.1, bf16[512,512]{1,0:T(8,128)(2,1)S(1)} %copy-done.4, bf16[384,128,128]{2,1,0:T(8,128)(2,1)} %vals_hbm.5), custom_call_target="tpu_custom_call" | custom-call | flops 2684354560 | bytes 7340032 | tf_op jit(solution)/shard_map/own/pallas_call | solution.py:320
  41.2 0.0 copy-start.2
  41.2 1.3 %copy-done.2 = f32[1024,512]{1,0:T(8,128)} copy-done((f32[1024,512]{1,0:T(8,128)}, f32[1024,512]{1,0:T(8,128)S(1)}, u32[]{:S(2)}) %copy-start.2) | copy-done | bytes 2097176
  42.5 0.0 collective-permute-done.1.came_ref
  42.5 1.7 %hub_pack.1.packed_hbm = bf16[1024,768]{1,0:T(8,128)(2,1)} custom-call(f32[1024,512]{1,0:T(8,128)S(1)} %get-tuple-element.9.keep_ref, f32[1024,512]{1,0:T(8,128)S(1)} %collective-permute-done.1.came_ref), custom_call_target="tpu_custom_call" | custom-call | flops 524288 | bytes 5242880 | tf_op jit(solution)/shard_map/hub_pack/pallas_call | solution.py:328
  44.2 17.3 %all-to-all-done = bf16[128,16,640]{2,1,0:T(8,128)(2,1)} async-done(((bf16[128,16,640]{2,1,0:T(8,128)(2,1)}), bf16[128,16,640]{2,1,0:T(8,128)(2,1)}, u32[]{:S(2)}, u32[]{:S(2)}) %all-to-all-start) | async-done | bytes 2621472 | tf_op jit(solution)/shard_map/all_to_all | solution.py:310
  61.5 2.0 %spread.1 = bf16[1024,768]{1,0:T(8,128)(2,1)} custom-call(bf16[2048,640]{1,0:T(8,128)(2,1)} %bitcast.3.arrived_ref, bf16[1024,768]{1,0:T(8,128)(2,1)} %hub_pack.1.packed_hbm), custom_call_target="tpu_custom_call", output_to_operand_aliasing={{}: (1, {})} | custom-call | flops 262144 | bytes 1048576 | tf_op jit(solution)/shard_map/spread/pallas_call | solution.py:333
  63.5 0.0 copy-start.7
  63.5 5.6 %all-to-all-start.1 = ((bf16[64,16,768]{2,1,0:T(8,128)(2,1)}), bf16[64,16,768]{2,1,0:T(8,128)(2,1)S(1)}, u32[]{:S(2)}, u32[]{:S(2)}) async-start(bf16[64,16,768]{2,1,0:T(8,128)(2,1)} %bitcast.5), calls=%async_computation.1 | async-start | bytes 3145728 | tf_op jit(solution)/shard_map/all_to_all | solution.py:338
  69.1 0.0 copy-done.7
  69.1 0.1 copy.15
  69.2 0.1 reshape.39.targets_ref
  69.3 0.0 copy-start.3
  69.3 1.6 %copy-done.3 = f32[1024,512]{1,0:T(8,128)S(1)} copy-done((f32[1024,512]{1,0:T(8,128)S(1)}, f32[1024,512]{1,0:T(8,128)}, u32[]{:S(2)}) %copy-start.3) | copy-done | bytes 2097176
  70.9 5.2 %landing.1 = f32[1024,512]{1,0:T(8,128)} custom-call(s32[8,256]{1,0:T(8,128)S(1)} %reshape.39.targets_ref, f32[1024,512]{1,0:T(8,128)S(1)} %copy-done.3, bf16[2048,640]{1,0:T(8,128)(2,1)} %bitcast.3.arrived_ref), custom_call_target="tpu_custom_call" | custom-call | flops 2147483648 | bytes 7340032 | tf_op jit(solution)/shard_map/landing/pallas_call | solution.py:342
  76.1 16.1 %all-to-all-done.1 = bf16[64,16,768]{2,1,0:T(8,128)(2,1)S(1)} async-done(((bf16[64,16,768]{2,1,0:T(8,128)(2,1)}), bf16[64,16,768]{2,1,0:T(8,128)(2,1)S(1)}, u32[]{:S(2)}, u32[]{:S(2)}) %all-to-all-start.1) | async-done | bytes 1572896 | tf_op jit(solution)/shard_map/all_to_all | solution.py:338
  92.3 2.5 %collective-permute-start.2 = (bf16[1024,256]{1,0:T(8,128)(2,1)S(1)}, bf16[1024,256]{1,0:T(8,128)(2,1)S(1)}, u32[]{:S(2)}, u32[]{:S(2)}) collective-permute-start(bf16[1024,256]{1,0:T(8,128)(2,1)S(1)} %slice.3.mine_ref), channel_id=1, source_target_pairs={{0,16},{16,0},{1,17},{17,1},{2,18},{18,2},{3,19},{19,3},{4,20},{20... | collective-permute-start | bytes 1572872 | tf_op jit(solution)/shard_map/ppermute | solution.py:349
  94.8 0.8 hub_sum.1
  95.5 0.7 collective-permute-done.2.came_ref
  96.3 1.6 %join.1 = f32[2,512,512]{2,1,0:T(8,128)} custom-call(s32[1]{0:T(128)} %bitcast.4.core, bf16[1024,256]{1,0:T(8,128)(2,1)S(1)} %slice.3.mine_ref, bf16[1024,256]{1,0:T(8,128)(2,1)S(1)} %collective-permute-done.2.came_ref), custom_call_target="tpu_custom_call" | custom-call | flops 524288 | bytes 3145728 | tf_op jit(solution)/shard_map/join/pallas_call | solution.py:354
  (2 shorter events, 0.0 us)
Async XLA Ops:
  0.6 2.5 %copy-start = (bf16[1024,512]{1,0:T(8,128)(2,1)S(1)}, bf16[1024,512]{1,0:T(8,128)(2,1)}, u32[]{:S(2)}) copy-start(bf16[1024,512]{1,0:T(8,128)(2,1)} %param.11) | copy-start | bytes 3145732
  0.7 2.4 %copy-start.1 = (bf16[1024,512]{1,0:T(8,128)(2,1)S(1)}, bf16[1024,512]{1,0:T(8,128)(2,1)}, u32[]{:S(2)}) copy-start(bf16[1024,512]{1,0:T(8,128)(2,1)} %cot_ref.1) | copy-start | bytes 3145732
  3.1 2.3 %copy-start.8 = (s32[1024]{0:T(1024)S(1)}, s32[1024]{0:T(1024)}, u32[]{:S(2)}) copy-start(s32[1024]{0:T(1024)} %param.15) | copy-start | bytes 12292
  3.1 2.3 %copy-start.9 = (bf16[512,512]{1,0:T(8,128)(2,1)S(1)}, bf16[512,512]{1,0:T(8,128)(2,1)}, u32[]{:S(2)}) copy-start(bf16[512,512]{1,0:T(8,128)(2,1)} %param.14) | copy-start | bytes 1572868
  3.9 3.8 %collective-permute-start = (f32[512,512]{1,0:T(8,128)S(1)}, f32[512,512]{1,0:T(8,128)S(1)}, u32[]{:S(2)}, u32[]{:S(2)}) collective-permute-start(f32[512,512]{1,0:T(8,128)S(1)} %get-tuple-element.15), channel_id=1, source_target_pairs={{0,16},{16,0},{1,17},{17,1},{2,18},{18,2},{3,19},{19,3},{4,20},{20... | collective-permute-start | bytes 3145736 | tf_op jit(solution)/shard_map/ppermute | solution.py:289
  5.4 2.3 %copy-start.5 = (s32[384]{0:T(512)S(1)}, s32[384]{0:T(512)}, u32[]{:S(2)}) copy-start(s32[384]{0:T(512)} %param.16) | copy-start | bytes 4612
  5.4 2.3 %copy-start.6 = (s32[384]{0:T(512)S(1)}, s32[384]{0:T(512)}, u32[]{:S(2)}) copy-start(s32[384]{0:T(512)} %param.17) | copy-start | bytes 4612
  14.7 46.8 %all-to-all-start = ((bf16[128,16,640]{2,1,0:T(8,128)(2,1)}), bf16[128,16,640]{2,1,0:T(8,128)(2,1)}, u32[]{:S(2)}, u32[]{:S(2)}) async-start(bf16[128,16,640]{2,1,0:T(8,128)(2,1)} %bitcast.21), calls=%async_computation | async-start | bytes 5242880 | tf_op jit(solution)/shard_map/all_to_all | solution.py:310
  26.9 8.0 %copy-start.4 = (bf16[512,512]{1,0:T(8,128)(2,1)S(1)}, bf16[512,512]{1,0:T(8,128)(2,1)}, u32[]{:S(2)}) copy-start(bf16[512,512]{1,0:T(8,128)(2,1)} %w_ref.1) | copy-start | bytes 1572868
  33.7 8.8 %collective-permute-start.1 = (f32[1024,512]{1,0:T(8,128)S(1)}, f32[1024,512]{1,0:T(8,128)S(1)}, u32[]{:S(2)}, u32[]{:S(2)}) collective-permute-start(f32[1024,512]{1,0:T(8,128)S(1)} %get-tuple-element.10), channel_id=1, source_target_pairs={{0,16},{16,0},{1,17},{17,1},{2,18},{18,2},{3,19},{19,3},{4,20},{20... | collective-permute-start | bytes 6291464 | tf_op jit(solution)/shard_map/ppermute | solution.py:319
  41.2 1.3 %copy-start.2 = (f32[1024,512]{1,0:T(8,128)}, f32[1024,512]{1,0:T(8,128)S(1)}, u32[]{:S(2)}) copy-start(f32[1024,512]{1,0:T(8,128)S(1)} %own.1.own_ref) | copy-start | bytes 6291460
  63.5 5.6 %copy-start.7 = (s32[1,128,16]{1,2,0:T(8,128)S(1)}, s32[1,128,16]{1,2,0:T(8,128)}, u32[]{:S(2)}) copy-start(s32[1,128,16]{1,2,0:T(8,128)} %param.19) | copy-start | bytes 24580
  63.5 28.7 %all-to-all-start.1 = ((bf16[64,16,768]{2,1,0:T(8,128)(2,1)}), bf16[64,16,768]{2,1,0:T(8,128)(2,1)S(1)}, u32[]{:S(2)}, u32[]{:S(2)}) async-start(bf16[64,16,768]{2,1,0:T(8,128)(2,1)} %bitcast.5), calls=%async_computation.1 | async-start | bytes 3145728 | tf_op jit(solution)/shard_map/all_to_all | solution.py:338
  69.3 1.6 %copy-start.3 = (f32[1024,512]{1,0:T(8,128)S(1)}, f32[1024,512]{1,0:T(8,128)}, u32[]{:S(2)}) copy-start(f32[1024,512]{1,0:T(8,128)} %copy-done.2) | copy-start | bytes 6291460
  92.3 4.0 %collective-permute-start.2 = (bf16[1024,256]{1,0:T(8,128)(2,1)S(1)}, bf16[1024,256]{1,0:T(8,128)(2,1)S(1)}, u32[]{:S(2)}, u32[]{:S(2)}) collective-permute-start(bf16[1024,256]{1,0:T(8,128)(2,1)S(1)} %slice.3.mine_ref), channel_id=1, source_target_pairs={{0,16},{16,0},{1,17},{17,1},{2,18},{18,2},{3,19},{19,3},{4,20},{20... | collective-permute-start | bytes 1572872 | tf_op jit(solution)/shard_map/ppermute | solution.py:349

commit v6 on v5

--- a/solution.py
+++ b/solution.py
@@ -18,7 +18,7 @@
 OWN_BLOCKS = 8
 UNROLL = 8
 PLAN = 256
-LAYERS = 3
+LAYERS = 4
 VMEM = 28 << 20
 
 
@@ -110,9 +110,9 @@
     late = (rank >= LAYERS).astype(F32)
     place = contract(jnp.broadcast_to(late, (8, REG)).astype(BF16), before, 1, 0)[0:1, :]
     match = ((lax.broadcasted_iota(jnp.int32, (REG, REG), 0).astype(F32) == place) & (late > 0.0)).astype(BF16)
-    value = jnp.where(line == 3, which, jnp.where(line == 4, rows.astype(F32), jnp.where(line == 5, cols.astype(F32), 0.0)))
+    value = jnp.where(line == 4, which, jnp.where(line == 5, rows.astype(F32), jnp.where(line == 6, cols.astype(F32), 0.0)))
     tables += contract(value.astype(BF16), match, 1, 1)
-    tables = jnp.where(line == 6, jnp.sum(late, axis=1, keepdims=True), tables)
+    tables = jnp.where(line == 7, jnp.sum(late, axis=1, keepdims=True), tables)
     plan_vmem[:, :REG] = tables.astype(jnp.int32)
 
 
@@ -139,12 +139,12 @@
         acc[c * TILE : (c + 4) * TILE, :] = contract(lhs, msg[...], 0, 0)
 
     def late(k, carry):
-        row = pl.multiple_of(plan[4, k] * TILE, TILE)
-        place = pl.ds(pl.multiple_of(plan[5, k] * TILE, TILE), TILE)
-        acc[place, :] += contract(vals[plan[3, k] + REG], msg[pl.ds(row, TILE), :], 0, 0)
+        row = pl.multiple_of(plan[5, k] * TILE, TILE)
+        place = pl.ds(pl.multiple_of(plan[6, k] * TILE, TILE), TILE)
+        acc[place, :] += contract(vals[plan[4, k] + REG], msg[pl.ds(row, TILE), :], 0, 0)
         return carry
 
-    lax.fori_loop(0, plan[6, 0], late, 0)
+    lax.fori_loop(0, plan[7, 0], late, 0)
     sent = []
     piece = 4 * TILE
     for k in range(4):
@@ -283,10 +283,9 @@
 
     steps = 4
     core = lax.axis_index("core")
-    w_first = contract(features, cotangent, 0, 0)
-    w_second = contract(aggregated, cotangent, 0, 0)
-    w_keep = jnp.where(core == 0, w_first, w_second)
-    w_came = lax.ppermute(jnp.where(core == 0, w_second, w_first), "core", swap)
+    w_send = contract(jnp.where(core == 0, aggregated, features), cotangent, 0, 0)
+    w_came = lax.ppermute(w_send, "core", swap)
+    w_keep = contract(jnp.where(core == 0, features, aggregated), cotangent, 0, 0)
     msg = (contract(cotangent, w_neigh, 1, 1) / degrees[:, None].astype(F32)).astype(BF16)
 
     wide = WIDTH + TILE

time: 98.3 us -> 97.2 us (0.989)
  local copies, waits for them, and re-layouts: 3.17 us -> 5.44 us
  starting transfers between devices: 23 us -> 21.5 us
  Pallas kernels: 31.4 us -> 30.1 us
  waiting for transfers between devices: 35.6 us -> 34.6 us
    all_to_all x1, starting transfers between devices: 12.2 us -> 10.5 us  [local(): lax.all_to_all(packed.reshape(128, 16, wide), ALL, split_axis=0, concat_a...]
    pallas_call x1, Pallas kernels: 5.23 us -> 3.64 us  [local(): call(landing_kernel, 'landing', 0, [whole(8, 256), spec_nodes, whole(slot...]
    all_to_all x1, waiting for transfers between devices: 16.1 us -> 17.5 us  [local(): lax.all_to_all(packed.reshape(64, 16, wider), ('y', 'z', 'x'), split_axis...]
    unnamed x21 -> x29, local copies, waits for them, and re-layouts: 3.05 us -> 4.28 us
    pallas_call x1, Pallas kernels: 0.79 us -> 2.01 us  [local(): call(hub_sum_kernel, 'hub_sum', 0, [spec_nodes], whole(16, WIDTH), jax.Sh...]
    slice x1, local copies, waits for them, and re-layouts: 0.03 us -> 1.08 us  [local(): w_mine = shared[:, WIDTH:]]
  transfers between devices with their start and end apart: 5 -> 5, of which waited for: 4 -> 3; matrix products, arithmetic and copies ran while one was open for 1% -> 2% of each run, Pallas kernels for 21% -> 21%
where the time goes in v6:
time: 97.2 us; the launch traced here: 96.5 us
  waiting for transfers between devices  34.6 us (36%)
  Pallas kernels  30.1 us (31%)
  starting transfers between devices  21.5 us (22%)
  local copies, waits for them, and re-layouts  5.44 us (6%)
  matrix products  3.93 us (4%)
    all_to_all x1, waiting for transfers between devices, local(): lax.all_to_all(packed.reshape(64, 16, wider), ('y', 'z', 'x'), split_axis...  17.5 us
    all_to_all x1, waiting for transfers between devices, local(): lax.all_to_all(packed.reshape(128, 16, wide), ALL, split_axis=0, concat_a...  16.4 us
    all_to_all x1, starting transfers between devices, local(): lax.all_to_all(packed.reshape(128, 16, wide), ALL, split_axis=0, concat_a...  10.5 us
    pallas_call x1, Pallas kernels, local(): call(ghost_kernel, 'ghost', 0, [INSIDE] * 5 + [OUTSIDE], OUTSIDE, pltpu.H...  7.01 us
    pallas_call x1, Pallas kernels, local(): call(hub_kernel, 'hub', 1, [spec_rc, spec_rc, spec_nodes, OUTSIDE], [spec...  6.86 us
    pallas_call x1, Pallas kernels, local(): call(own_kernel, 'own', 0, [spec_rc, spec_rc, spec_nodes, spec_nodes, spe...  6.32 us
    all_to_all x1, starting transfers between devices, local(): lax.all_to_all(packed.reshape(64, 16, wider), ('y', 'z', 'x'), split_axis...  5.81 us
    unnamed x29, local copies, waits for them, and re-layouts  4.28 us
  transfers between devices with their start and end apart: 5, of which 3 were waited for; matrix products, arithmetic and copies ran while one was open for 2% of the time, Pallas kernels for 21%

profile of v6, /device:TPU:1, one launch (start us, length us, event | category | flops | bytes accessed | tf_op | source)
XLA Modules:
  0.0 96.5 jit_solution(494944806277697107)
XLA Ops:
  0.6 0.0 copy-start
  0.7 0.0 copy-start.11
  0.7 0.0 copy-start.5
  0.7 0.0 copy-start.12
  0.7 0.0 copy-start.13
  0.7 2.4 %fusion = f32[512,512]{1,0:T(8,128)S(1)} fusion(bf16[1024,512]{1,0:T(8,128)(2,1)} %cot_ref.1, bf16[1024,512]{1,0:T(8,128)(2,1)} %param.11, bf16[1024,512]{1,0:T(8,128)(2,1)} %param.10, pred[]{:T(512)S(6)} %eq.4), kind=kOutput, calls=%fused_computation.1 | convolution fusion | flops 537395200 | bytes 4194305 | tf_op jit(solution)/shard_map/dot_general | solution.py:26
  3.1 1.5 %collective-permute-start = (f32[512,512]{1,0:T(8,128)S(1)}, f32[512,512]{1,0:T(8,128)S(1)}, u32[]{:S(2)}, u32[]{:S(2)}) collective-permute-start(f32[512,512]{1,0:T(8,128)S(1)} %fusion), channel_id=1, source_target_pairs={{0,16},{16,0},{1,17},{17,1},{2,18},{18,2},{3,19},{19,3},{4,20},{20... | collective-permute-start | bytes 3145736 | tf_op jit(solution)/shard_map/ppermute | solution.py:287
  4.6 0.0 copy-done.11
  4.6 0.0 copy-done.5
  4.6 0.0 copy-done.12
  4.6 0.0 copy-done.13
  4.7 0.7 fusion.2.keep
  5.4 0.0 copy-done
  5.4 0.0 copy-start.8
  5.4 0.0 copy-start.9
  5.4 0.7 divide_convert_fusion.msg.msg_ref
  6.2 0.0 copy-start.1
  6.2 0.7 collective-permute-done.came
  6.9 0.0 copy-done.8
  6.9 0.0 copy-done.9
  6.9 7.0 %ghost.1 = bf16[2048,640]{1,0:T(8,128)(2,1)} custom-call(s32[3,128]{1,0:T(4,128)S(1)} %bitcast.13, s32[3,128]{1,0:T(4,128)S(1)} %bitcast.16, bf16[1024,512]{1,0:T(8,128)(2,1)S(1)} %divide_convert_fusion.msg.msg_ref, f32[512,512]{1,0:T(8,128)S(1)} %fusion.2.keep, f32[512,512]{1,0:T(8,128)S(1)} %collective-permute-done.came, bf16[384,128,128]{2,1,0:T(8,128)(2,1)} %vals_hbm.5), custom_call_target="tpu_custom_call" | custom-call | flops 2147483648 | bytes 9437184 | tf_op jit(solution)/shard_map/ghost/pallas_call | solution.py:292
  13.9 0.0 copy-done.1
  14.0 10.5 %all-to-all-start = ((bf16[128,16,640]{2,1,0:T(8,128)(2,1)}), bf16[128,16,640]{2,1,0:T(8,128)(2,1)S(1)}, u32[]{:S(2)}, u32[]{:S(2)}) async-start(bf16[128,16,640]{2,1,0:T(8,128)(2,1)} %bitcast.19), calls=%async_computation | async-start | bytes 5242880 | tf_op jit(solution)/shard_map/all_to_all | solution.py:309
  24.5 0.0 copy-start.2
  24.5 1.2 %copy-done.2 = bf16[1024,512]{1,0:T(8,128)(2,1)S(1)} copy-done((bf16[1024,512]{1,0:T(8,128)(2,1)S(1)}, bf16[1024,512]{1,0:T(8,128)(2,1)}, u32[]{:S(2)}) %copy-start.2) | copy-done | bytes 1048600
  25.7 6.9 %hub.1 = (f32[1024,512]{1,0:T(8,128)S(1)}, f32[1024,512]{1,0:T(8,128)S(1)}) custom-call(s32[1]{0:T(128)} %bitcast.4.core, s32[3,128]{1,0:T(4,128)S(1)} %bitcast.14, s32[3,128]{1,0:T(4,128)S(1)} %bitcast.17, bf16[1024,512]{1,0:T(8,128)(2,1)S(1)} %copy-done.2, bf16[384,128,128]{2,1,0:T(8,128)(2,1)} %vals_hbm.5), custom_call_target="tpu_custom_call" | custom-call | flops 2147483648 | bytes 9437184 | tf_op jit(solution)/shard_map/hub/pallas_call | solution.py:313
  32.6 1.1 %collective-permute-start.1 = (f32[1024,512]{1,0:T(8,128)S(1)}, f32[1024,512]{1,0:T(8,128)S(1)}, u32[]{:S(2)}, u32[]{:S(2)}) collective-permute-start(f32[1024,512]{1,0:T(8,128)S(1)} %get-tuple-element.10), channel_id=1, source_target_pairs={{0,16},{16,0},{1,17},{17,1},{2,18},{18,2},{3,19},{19,3},{4,20},{20... | collective-permute-start | bytes 6291464 | tf_op jit(solution)/shard_map/ppermute | solution.py:318
  33.7 0.0 copy-done.6
  33.7 0.0 copy-done.7
  33.7 6.3 %own.1.own_ref = f32[1024,512]{1,0:T(8,128)S(1)} custom-call(s32[3,128]{1,0:T(4,128)S(1)} %bitcast.15, s32[3,128]{1,0:T(4,128)S(1)} %bitcast.18, bf16[1024,512]{1,0:T(8,128)(2,1)S(1)} %copy-done.2, bf16[1024,512]{1,0:T(8,128)(2,1)S(1)} %copy-done.6, bf16[512,512]{1,0:T(8,128)(2,1)S(1)} %copy-done.7, bf16[384,128,128]{2,1,0:T(8,128)(2,1)} %vals_hbm.5), custom_call_target="tpu_custom_call" | custom-call | flops 2684354560 | bytes 7340032 | tf_op jit(solution)/shard_map/own/pallas_call | solution.py:319
  40.1 0.0 copy-start.3
  40.1 1.3 %copy-done.3 = f32[1024,512]{1,0:T(8,128)} copy-done((f32[1024,512]{1,0:T(8,128)}, f32[1024,512]{1,0:T(8,128)S(1)}, u32[]{:S(2)}) %copy-start.3) | copy-done | bytes 2097176
  41.4 0.0 collective-permute-done.1.came_ref
  41.4 1.6 %hub_pack.1.packed_hbm = bf16[1024,768]{1,0:T(8,128)(2,1)} custom-call(f32[1024,512]{1,0:T(8,128)S(1)} %get-tuple-element.9.keep_ref, f32[1024,512]{1,0:T(8,128)S(1)} %collective-permute-done.1.came_ref), custom_call_target="tpu_custom_call" | custom-call | flops 524288 | bytes 5242880 | tf_op jit(solution)/shard_map/hub_pack/pallas_call | solution.py:327
  43.0 16.4 %all-to-all-done = bf16[128,16,640]{2,1,0:T(8,128)(2,1)S(1)} async-done(((bf16[128,16,640]{2,1,0:T(8,128)(2,1)}), bf16[128,16,640]{2,1,0:T(8,128)(2,1)S(1)}, u32[]{:S(2)}, u32[]{:S(2)}) %all-to-all-start) | async-done | bytes 2621472 | tf_op jit(solution)/shard_map/all_to_all | solution.py:309
  59.4 1.1 %spread.1 = bf16[1024,768]{1,0:T(8,128)(2,1)} custom-call(bf16[2048,640]{1,0:T(8,128)(2,1)S(1)} %bitcast.11, bf16[1024,768]{1,0:T(8,128)(2,1)} %hub_pack.1.packed_hbm), custom_call_target="tpu_custom_call", output_to_operand_aliasing={{}: (1, {})} | custom-call | flops 262144 | bytes 1048576 | tf_op jit(solution)/shard_map/spread/pallas_call | solution.py:332
  60.5 5.8 %all-to-all-start.1 = ((bf16[64,16,768]{2,1,0:T(8,128)(2,1)}), bf16[64,16,768]{2,1,0:T(8,128)(2,1)}, u32[]{:S(2)}, u32[]{:S(2)}) async-start(bf16[64,16,768]{2,1,0:T(8,128)(2,1)} %bitcast.5), calls=%async_computation.1 | async-start | bytes 3145728 | tf_op jit(solution)/shard_map/all_to_all | solution.py:337
  66.3 0.1 copy.15
  66.4 0.1 reshape.39.targets_ref
  66.5 0.0 copy-start.4
  66.5 1.6 %copy-done.4 = f32[1024,512]{1,0:T(8,128)S(1)} copy-done((f32[1024,512]{1,0:T(8,128)S(1)}, f32[1024,512]{1,0:T(8,128)}, u32[]{:S(2)}) %copy-start.4) | copy-done | bytes 2097176
  68.1 3.6 %landing.1 = f32[1024,512]{1,0:T(8,128)} custom-call(s32[8,256]{1,0:T(8,128)S(1)} %reshape.39.targets_ref, f32[1024,512]{1,0:T(8,128)S(1)} %copy-done.4, bf16[2048,640]{1,0:T(8,128)(2,1)S(1)} %bitcast.12), custom_call_target="tpu_custom_call" | custom-call | flops 2147483648 | bytes 7340032 | tf_op jit(solution)/shard_map/landing/pallas_call | solution.py:341
  71.7 17.5 %all-to-all-done.1 = bf16[64,16,768]{2,1,0:T(8,128)(2,1)} async-done(((bf16[64,16,768]{2,1,0:T(8,128)(2,1)}), bf16[64,16,768]{2,1,0:T(8,128)(2,1)}, u32[]{:S(2)}, u32[]{:S(2)}) %all-to-all-start.1) | async-done | bytes 1572896 | tf_op jit(solution)/shard_map/all_to_all | solution.py:337
  89.2 1.1 %slice.3.mine_ref = bf16[1024,256]{1,0:T(8,128)(2,1)S(1)} slice(bf16[1024,768]{1,0:T(8,128)(2,1)} %bitcast.6.arrived_ref), slice={[0:1024], [512:768]} | slice | bytes 1048576 | tf_op jit(solution)/shard_map/slice | solution.py:347
  90.3 2.6 %collective-permute-start.2 = (bf16[1024,256]{1,0:T(8,128)(2,1)S(1)}, bf16[1024,256]{1,0:T(8,128)(2,1)S(1)}, u32[]{:S(2)}, u32[]{:S(2)}) collective-permute-start(bf16[1024,256]{1,0:T(8,128)(2,1)S(1)} %slice.3.mine_ref), channel_id=1, source_target_pairs={{0,16},{16,0},{1,17},{17,1},{2,18},{18,2},{3,19},{19,3},{4,20},{20... | collective-permute-start | bytes 1572872 | tf_op jit(solution)/shard_map/ppermute | solution.py:348
  92.9 2.0 %hub_sum.1 = f32[16,512]{1,0:T(8,128)} custom-call(bf16[1024,768]{1,0:T(8,128)(2,1)} %bitcast.6.arrived_ref), custom_call_target="tpu_custom_call" | custom-call | flops 524288 | bytes 1048576 | tf_op jit(solution)/shard_map/hub_sum/pallas_call | solution.py:349
  94.9 0.0 collective-permute-done.2.came_ref
  94.9 1.6 %join.1 = f32[2,512,512]{2,1,0:T(8,128)} custom-call(s32[1]{0:T(128)} %bitcast.4.core, bf16[1024,256]{1,0:T(8,128)(2,1)S(1)} %slice.3.mine_ref, bf16[1024,256]{1,0:T(8,128)(2,1)S(1)} %collective-permute-done.2.came_ref), custom_call_target="tpu_custom_call" | custom-call | flops 524288 | bytes 3145728 | tf_op jit(solution)/shard_map/join/pallas_call | solution.py:353
  (5 shorter events, 0.0 us)
Async XLA Ops:
  0.6 4.8 %copy-start = (bf16[512,512]{1,0:T(8,128)(2,1)S(1)}, bf16[512,512]{1,0:T(8,128)(2,1)}, u32[]{:S(2)}) copy-start(bf16[512,512]{1,0:T(8,128)(2,1)} %param.14) | copy-start | bytes 1572868
  0.7 4.0 %copy-start.11 = (s32[1024]{0:T(1024)S(1)}, s32[1024]{0:T(1024)}, u32[]{:S(2)}) copy-start(s32[1024]{0:T(1024)} %param.15) | copy-start | bytes 12292
  0.7 4.0 %copy-start.5 = (bf16[1024,512]{1,0:T(8,128)(2,1)S(1)}, bf16[1024,512]{1,0:T(8,128)(2,1)}, u32[]{:S(2)}) copy-start(bf16[1024,512]{1,0:T(8,128)(2,1)} %cot_ref.1) | copy-start | bytes 3145732
  0.7 4.0 %copy-start.12 = (bf16[1024,512]{1,0:T(8,128)(2,1)S(1)}, bf16[1024,512]{1,0:T(8,128)(2,1)}, u32[]{:S(2)}) copy-start(bf16[1024,512]{1,0:T(8,128)(2,1)} %param.10) | copy-start | bytes 3145732
  0.7 4.0 %copy-start.13 = (bf16[1024,512]{1,0:T(8,128)(2,1)S(1)}, bf16[1024,512]{1,0:T(8,128)(2,1)}, u32[]{:S(2)}) copy-start(bf16[1024,512]{1,0:T(8,128)(2,1)} %param.11) | copy-start | bytes 3145732
  3.1 3.8 %collective-permute-start = (f32[512,512]{1,0:T(8,128)S(1)}, f32[512,512]{1,0:T(8,128)S(1)}, u32[]{:S(2)}, u32[]{:S(2)}) collective-permute-start(f32[512,512]{1,0:T(8,128)S(1)} %fusion), channel_id=1, source_target_pairs={{0,16},{16,0},{1,17},{17,1},{2,18},{18,2},{3,19},{19,3},{4,20},{20... | collective-permute-start | bytes 3145736 | tf_op jit(solution)/shard_map/ppermute | solution.py:287
  5.4 1.5 %copy-start.8 = (s32[384]{0:T(512)S(1)}, s32[384]{0:T(512)}, u32[]{:S(2)}) copy-start(s32[384]{0:T(512)} %param.16) | copy-start | bytes 4612
  5.4 1.5 %copy-start.9 = (s32[384]{0:T(512)S(1)}, s32[384]{0:T(512)}, u32[]{:S(2)}) copy-start(s32[384]{0:T(512)} %param.17) | copy-start | bytes 4612
  6.2 7.8 %copy-start.1 = (bf16[1024,512]{1,0:T(8,128)(2,1)}, bf16[1024,512]{1,0:T(8,128)(2,1)S(1)}, u32[]{:S(2)}) copy-start(bf16[1024,512]{1,0:T(8,128)(2,1)S(1)} %divide_convert_fusion.msg.msg_ref) | copy-start | bytes 3145732
  14.0 45.5 %all-to-all-start = ((bf16[128,16,640]{2,1,0:T(8,128)(2,1)}), bf16[128,16,640]{2,1,0:T(8,128)(2,1)S(1)}, u32[]{:S(2)}, u32[]{:S(2)}) async-start(bf16[128,16,640]{2,1,0:T(8,128)(2,1)} %bitcast.19), calls=%async_computation | async-start | bytes 5242880 | tf_op jit(solution)/shard_map/all_to_all | solution.py:309
  24.5 1.2 %copy-start.2 = (bf16[1024,512]{1,0:T(8,128)(2,1)S(1)}, bf16[1024,512]{1,0:T(8,128)(2,1)}, u32[]{:S(2)}) copy-start(bf16[1024,512]{1,0:T(8,128)(2,1)} %copy-done.1) | copy-start | bytes 3145732
  25.7 8.0 %copy-start.6 = (bf16[1024,512]{1,0:T(8,128)(2,1)S(1)}, bf16[1024,512]{1,0:T(8,128)(2,1)}, u32[]{:S(2)}) copy-start(bf16[1024,512]{1,0:T(8,128)(2,1)} %cot_ref.1) | copy-start | bytes 3145732
  25.7 8.0 %copy-start.7 = (bf16[512,512]{1,0:T(8,128)(2,1)S(1)}, bf16[512,512]{1,0:T(8,128)(2,1)}, u32[]{:S(2)}) copy-start(bf16[512,512]{1,0:T(8,128)(2,1)} %w_ref.1) | copy-start | bytes 1572868
  32.6 8.8 %collective-permute-start.1 = (f32[1024,512]{1,0:T(8,128)S(1)}, f32[1024,512]{1,0:T(8,128)S(1)}, u32[]{:S(2)}, u32[]{:S(2)}) collective-permute-start(f32[1024,512]{1,0:T(8,128)S(1)} %get-tuple-element.10), channel_id=1, source_target_pairs={{0,16},{16,0},{1,17},{17,1},{2,18},{18,2},{3,19},{19,3},{4,20},{20... | collective-permute-start | bytes 6291464 | tf_op jit(solution)/shard_map/ppermute | solution.py:318
  40.1 1.3 %copy-start.3 = (f32[1024,512]{1,0:T(8,128)}, f32[1024,512]{1,0:T(8,128)S(1)}, u32[]{:S(2)}) copy-start(f32[1024,512]{1,0:T(8,128)S(1)} %own.1.own_ref) | copy-start | bytes 6291460
  60.5 5.8 %copy-start.10 = (s32[1,128,16]{1,2,0:T(8,128)S(1)}, s32[1,128,16]{1,2,0:T(8,128)}, u32[]{:S(2)}) copy-start(s32[1,128,16]{1,2,0:T(8,128)} %param.19) | copy-start | bytes 24580
  60.5 28.7 %all-to-all-start.1 = ((bf16[64,16,768]{2,1,0:T(8,128)(2,1)}), bf16[64,16,768]{2,1,0:T(8,128)(2,1)}, u32[]{:S(2)}, u32[]{:S(2)}) async-start(bf16[64,16,768]{2,1,0:T(8,128)(2,1)} %bitcast.5), calls=%async_computation.1 | async-start | bytes 3145728 | tf_op jit(solution)/shard_map/all_to_all | solution.py:337
  66.5 1.6 %copy-start.4 = (f32[1024,512]{1,0:T(8,128)S(1)}, f32[1024,512]{1,0:T(8,128)}, u32[]{:S(2)}) copy-start(f32[1024,512]{1,0:T(8,128)} %copy-done.3) | copy-start | bytes 6291460
  90.3 4.6 %collective-permute-start.2 = (bf16[1024,256]{1,0:T(8,128)(2,1)S(1)}, bf16[1024,256]{1,0:T(8,128)(2,1)S(1)}, u32[]{:S(2)}, u32[]{:S(2)}) collective-permute-start(bf16[1024,256]{1,0:T(8,128)(2,1)S(1)} %slice.3.mine_ref), channel_id=1, source_target_pairs={{0,16},{16,0},{1,17},{17,1},{2,18},{18,2},{3,19},{19,3},{4,20},{20... | collective-permute-start | bytes 1572872 | tf_op jit(solution)/shard_map/ppermute | solution.py:348

commit v7 on v6

--- a/solution.py
+++ b/solution.py
@@ -19,7 +19,6 @@
 UNROLL = 8
 PLAN = 256
 LAYERS = 4
-VMEM = 28 << 20
 
 
 def contract(a, b, da, db):
@@ -95,29 +94,35 @@
 def write_cells(region, rows_ref, cols_ref, plan_vmem):
     cols = cols_ref[region : region + 1, :]
     rows = rows_ref[region : region + 1, :]
-    cell = cols * (NODES // TILE) + rows
-    hot = (lax.broadcasted_iota(jnp.int32, (REG, REG), 0) == cell).astype(F32)
-    before = (
-        lax.broadcasted_iota(jnp.int32, (REG, REG), 0) < lax.broadcasted_iota(jnp.int32, (REG, REG), 1)
-    ).astype(BF16)
-    rank = jnp.sum(hot * contract(hot.astype(BF16), before, 1, 0), axis=0, keepdims=True)
-    line = lax.broadcasted_iota(jnp.int32, (8, REG), 0)
-    which = lax.broadcasted_iota(jnp.int32, (8, REG), 1).astype(F32) - REG
-    tables = jnp.zeros((8, REG), F32)
-    for layer in range(LAYERS):
-        value = jnp.where((line == layer) & (rank == layer), which, 0.0).astype(BF16)
-        tables += contract(value, hot.astype(BF16), 1, 1)
-    late = (rank >= LAYERS).astype(F32)
-    place = contract(jnp.broadcast_to(late, (8, REG)).astype(BF16), before, 1, 0)[0:1, :]
-    match = ((lax.broadcasted_iota(jnp.int32, (REG, REG), 0).astype(F32) == place) & (late > 0.0)).astype(BF16)
-    value = jnp.where(line == 4, which, jnp.where(line == 5, rows.astype(F32), jnp.where(line == 6, cols.astype(F32), 0.0)))
-    tables += contract(value.astype(BF16), match, 1, 1)
-    tables = jnp.where(line == 7, jnp.sum(late, axis=1, keepdims=True), tables)
-    plan_vmem[:, :REG] = tables.astype(jnp.int32)
+    across = (cols * (NODES // TILE) + rows).astype(F32)
+    down = jnp.transpose(jnp.broadcast_to(across, (8, REG)))[:, 0:1]
+    sub = lax.broadcasted_iota(jnp.int32, (REG, REG), 0).astype(F32)
+    lane = lax.broadcasted_iota(jnp.int32, (REG, REG), 1).astype(F32)
+
+    def total(mask):
+        return jnp.sum(mask.astype(F32), axis=0, keepdims=True)
+
+    rank = total((down == across) & (sub < lane))
+    order = rank + total(down < across)
+    count = total(down == lane)
+    start = total(down < lane)
+    hot = (sub == across).astype(F32)
+    large = (count > LAYERS).astype(F32)
+    spot = total((jnp.sum(hot, axis=1, keepdims=True) > LAYERS) & (sub < lane))
+    line = lax.broadcasted_iota(jnp.int32, (8, REG), 0).astype(F32)
+    index = lax.broadcasted_iota(jnp.int32, (8, REG), 1).astype(F32)
+    layers = contract(jnp.where(line == rank, index - REG, 0.0).astype(BF16), hot.astype(BF16), 1, 1) + REG
+    layers = jnp.where(large > 0.0, jnp.where(line == 0.0, REG + 1.0 + spot, 1.0 * REG), layers)
+    order = contract(index.astype(BF16), (sub == order).astype(BF16), 1, 1)
+    chosen = contract(index.astype(BF16), ((sub == spot).astype(F32) * large).astype(BF16), 1, 1)
+    many = jnp.sum(large, axis=1, keepdims=True)
+    other = jnp.where(line == 0.0, order, jnp.where(line == 1.0, chosen, jnp.where(line == 2.0, start, jnp.where(line == 3.0, count, many))))
+    plan_vmem[:, :REG] = layers.astype(jnp.int32)
+    plan_vmem[:, REG:] = other.astype(jnp.int32)
 
 
 def ghost_kernel(rows_ref, cols_ref, msg, keep, came, vals_hbm, out_hbm,
-                 vals, dense, acc, out, plan_vmem, plan, sem, out_sems, plan_sem):
+                 vals, dense, out, plan_vmem, plan, sem, out_sems, plan_sem):
     tiles = load_tiles(2, vals_hbm, vals, sem)
     write_cells(2, rows_ref, cols_ref, plan_vmem)
     ready = pltpu.make_async_copy(plan_vmem, plan, plan_sem)
@@ -128,29 +133,30 @@
     ready.wait()
     tiles.wait()
     per = NODES // TILE
-    for c in range(HUB_BLOCKS):
-        for r in range(per):
-            total = vals[plan[0, c * per + r] + REG].astype(F32)
-            for layer in range(1, LAYERS):
-                total += vals[plan[layer, c * per + r] + REG].astype(F32)
-            dense[c, r * TILE : (r + 1) * TILE, :] = total.astype(BF16)
+
+    def large(k, carry):
+        cell = plan[1, REG + k]
+        start = plan[2, REG + cell]
+
+        def add(i, total):
+            return total + vals[plan[0, REG + start + i]].astype(F32)
+
+        total = lax.fori_loop(0, plan[3, REG + cell], add, jnp.zeros((TILE, TILE), F32))
+        vals[REG + 1 + k] = total.astype(BF16)
+        return carry
+
+    lax.fori_loop(0, plan[4, REG], large, 0)
+    sent = []
     for c in range(0, HUB_BLOCKS, 4):
+        for k in range(4):
+            for r in range(per):
+                tile = (c + k) * per + r
+                parts = [vals[plan[layer, tile]] for layer in range(LAYERS)]
+                dense[c + k, r * TILE : (r + 1) * TILE, :] = ((parts[0].astype(F32) + parts[1].astype(F32)) + (parts[2].astype(F32) + parts[3].astype(F32))).astype(BF16)
         lhs = jnp.concatenate([dense[c + k] for k in range(4)], axis=1)
-        acc[c * TILE : (c + 4) * TILE, :] = contract(lhs, msg[...], 0, 0)
-
-    def late(k, carry):
-        row = pl.multiple_of(plan[5, k] * TILE, TILE)
-        place = pl.ds(pl.multiple_of(plan[6, k] * TILE, TILE), TILE)
-        acc[place, :] += contract(vals[plan[4, k] + REG], msg[pl.ds(row, TILE), :], 0, 0)
-        return carry
-
-    lax.fori_loop(0, plan[7, 0], late, 0)
-    sent = []
-    piece = 4 * TILE
-    for k in range(4):
-        part = pl.ds(k * piece, piece)
-        out[part, :WIDTH] = acc[part, :].astype(BF16)
-        sent.append(pltpu.make_async_copy(out.at[part], out_hbm.at[part], out_sems.at[k]))
+        part = pl.ds(c * TILE, 4 * TILE)
+        out[part, :WIDTH] = contract(lhs, msg[...], 0, 0).astype(BF16)
+        sent.append(pltpu.make_async_copy(out.at[part], out_hbm.at[part], out_sems.at[c // 4]))
         sent[-1].start()
     for copy in sent:
         copy.wait()
@@ -237,14 +243,14 @@
 OUTSIDE = pl.BlockSpec(memory_space=pltpu.HBM)
 
 
-def call(kernel, name, scalars, ins, outs, shapes, scratch, flops, moved, grid=(1,), **more):
+def call(kernel, name, scalars, ins, outs, shapes, scratch, flops, moved, mib, grid=(1,), **more):
     return pl.pallas_call(
         kernel,
         grid_spec=pltpu.PrefetchScalarGridSpec(
             num_scalar_prefetch=scalars, grid=grid, in_specs=ins, out_specs=outs, scratch_shapes=scratch
         ),
         out_shape=shapes,
-        compiler_params=pltpu.CompilerParams(vmem_limit_bytes=VMEM),
+        compiler_params=pltpu.CompilerParams(vmem_limit_bytes=mib << 20),
         cost_estimate=pl.CostEstimate(flops=flops, bytes_accessed=moved, transcendentals=0),
         name=name,
         **more,
@@ -294,9 +300,8 @@
         [INSIDE] * 5 + [OUTSIDE], OUTSIDE,
         pltpu.HBM((slots, wide), BF16),
         [
-            pltpu.VMEM((REG + 1, TILE, TILE), BF16),
+            pltpu.VMEM((REG + 32, TILE, TILE), BF16),
             pltpu.VMEM((HUB_BLOCKS, NODES, TILE), BF16),
-            pltpu.VMEM((slots, WIDTH), F32),
             pltpu.VMEM((slots, wide), BF16),
             pltpu.VMEM((8, PLAN), jnp.int32),
             pltpu.SMEM((8, PLAN), jnp.int32),
@@ -304,35 +309,36 @@
             pltpu.SemaphoreType.DMA((4,)),
             pltpu.SemaphoreType.DMA,
         ],
-        region_flops, region_bytes + (2 << 20), grid=(),
+        region_flops, region_bytes + (2 << 20), 18, grid=(),
     )(rows, cols, msg, w_keep, w_came, tile_vals)
     arrived = lax.all_to_all(
         packed.reshape(128, 16, wide), ALL, split_axis=0, concat_axis=0, tiled=True
     ).reshape(slots, wide)
+    arrived = pltpu.with_memory_space_constraint(arrived, pltpu.HBM)
 
     hub_keep, hub_send = call(
         hub_kernel, "hub", 1, [spec_rc, spec_rc, spec_nodes, OUTSIDE], [spec_nodes, spec_nodes],
         [jax.ShapeDtypeStruct((NODES, WIDTH), F32)] * 2,
-        tile_scratch(True), region_flops, region_bytes + (2 << 20),
+        tile_scratch(True), region_flops, region_bytes + (2 << 20), 24,
     )(core_arg, rows, cols, msg, tile_vals)
     hub_came = lax.ppermute(hub_send, "core", swap)
     own = call(
         own_kernel, "own", 0, [spec_rc, spec_rc, spec_nodes, spec_nodes, spec_w, OUTSIDE], spec_nodes,
         jax.ShapeDtypeStruct((NODES, WIDTH), F32),
-        tile_scratch(False), region_flops + 2 * NODES * WIDTH * WIDTH, region_bytes,
+        tile_scratch(False), region_flops + 2 * NODES * WIDTH * WIDTH, region_bytes, 20,
     )(rows, cols, msg, cotangent, w_self, tile_vals)
 
     wider = WIDTH + 2 * TILE
     spec_hub = pl.BlockSpec((NODES // steps, WIDTH), lambda i: (i, 0))
     packed = call(
         hub_pack_kernel, "hub_pack", 0, [spec_hub, spec_hub], spec_hub,
-        jax.ShapeDtypeStruct((NODES, wider), BF16), [], NODES * WIDTH, 5 << 20, grid=(steps,),
+        jax.ShapeDtypeStruct((NODES, wider), BF16), [], NODES * WIDTH, 5 << 20, 8, grid=(steps,),
     )(hub_keep, hub_came)
     packed, own = lax.optimization_barrier((packed, own))
     packed = call(
         spread_kernel, "spread", 0, [pl.BlockSpec((slots, TILE), lambda i: (0, WIDTH // TILE)), ANY],
         pl.BlockSpec((NODES, 2 * TILE), lambda i: (0, WIDTH // (2 * TILE))),
-        jax.ShapeDtypeStruct((NODES, wider), BF16), [], slots * TILE, 1 << 20, input_output_aliases={1: 0},
+        jax.ShapeDtypeStruct((NODES, wider), BF16), [], slots * TILE, 1 << 20, 6, input_output_aliases={1: 0},
     )(arrived, packed)
     shared = lax.all_to_all(
         packed.reshape(64, 16, wider), ("y", "z", "x"), split_axis=0, concat_axis=0, tiled=True
@@ -340,7 +346,7 @@
 
     grad_nodes = call(
         landing_kernel, "landing", 0, [whole(8, 256), spec_nodes, whole(slots, WIDTH)], spec_nodes,
-        jax.ShapeDtypeStruct((NODES, WIDTH), F32), [], 2 * slots * NODES * WIDTH, 7 << 20,
+        jax.ShapeDtypeStruct((NODES, WIDTH), F32), [], 2 * slots * NODES * WIDTH, 7 << 20, 18,
     )(targets, own, arrived)
 
     shared, grad_nodes = lax.optimization_barrier((shared, grad_nodes))
@@ -348,11 +354,11 @@
     w_theirs = lax.ppermute(w_mine, "core", swap)
     grad_hubs = call(
         hub_sum_kernel, "hub_sum", 0, [spec_nodes], whole(16, WIDTH),
-        jax.ShapeDtypeStruct((16, WIDTH), F32), [], NODES * WIDTH, 1 << 20,
+        jax.ShapeDtypeStruct((16, WIDTH), F32), [], NODES * WIDTH, 1 << 20, 6,
     )(shared)
     grad_weights = call(
         join_kernel, "join", 1, [whole(NODES, 2 * TILE)] * 2, whole(2, WIDTH, WIDTH),
-        jax.ShapeDtypeStruct((2, WIDTH, WIDTH), F32), [], NODES * WIDTH, 3 << 20,
+        jax.ShapeDtypeStruct((2, WIDTH, WIDTH), F32), [], NODES * WIDTH, 3 << 20, 10,
     )(core_arg, w_mine, w_theirs)
     return (grad_nodes, grad_hubs, grad_weights)
 

time: 97.2 us -> 95.6 us (0.984)
  local copies, waits for them, and re-layouts: 5.44 us -> 3.17 us
    pallas_call x1, Pallas kernels: 3.64 us -> 5.23 us  [local(): call(landing_kernel, 'landing', 0, [whole(8, 256), spec_nodes, whole(slot...]
    all_to_all x1, waiting for transfers between devices: 17.5 us -> 16.1 us  [local(): lax.all_to_all(packed.reshape(64, 16, wider), ('y', 'z', 'x'), split_axis...]
    unnamed x29 -> x23, local copies, waits for them, and re-layouts: 4.28 us -> 3.05 us
    pallas_call x1, Pallas kernels: 2.01 us -> 0.79 us  [local(): call(hub_sum_kernel, 'hub_sum', 0, [spec_nodes], whole(16, WIDTH), jax.Sh...]
    slice x1, local copies, waits for them, and re-layouts: 1.08 us -> 0.03 us  [local(): w_mine = shared[:, WIDTH:]]
  transfers between devices with their start and end apart: 5 -> 5, of which waited for: 3 -> 4; matrix products, arithmetic and copies ran while one was open for 2% -> 2% of each run, Pallas kernels for 21% -> 22%
where the time goes in v7:
time: 95.6 us; the launch traced here: 95.1 us
  waiting for transfers between devices  34.9 us (37%)
  Pallas kernels  30.7 us (32%)
  starting transfers between devices  21.6 us (23%)
  matrix products  3.92 us (4%)
  local copies, waits for them, and re-layouts  3.17 us (3%)
    all_to_all x1, waiting for transfers between devices, local(): lax.all_to_all(packed.reshape(128, 16, wide), ALL, split_axis=0, concat_a...  17.3 us
    all_to_all x1, waiting for transfers between devices, local(): lax.all_to_all(packed.reshape(64, 16, wider), ('y', 'z', 'x'), split_axis...  16.1 us
    all_to_all x1, starting transfers between devices, local(): lax.all_to_all(packed.reshape(128, 16, wide), ALL, split_axis=0, concat_a...  10.8 us
    pallas_call x1, Pallas kernels, local(): call(hub_kernel, 'hub', 1, [spec_rc, spec_rc, spec_nodes, OUTSIDE], [spec...  6.79 us
    pallas_call x1, Pallas kernels, local(): call(ghost_kernel, 'ghost', 0, [INSIDE] * 5 + [OUTSIDE], OUTSIDE, pltpu.H...  6.36 us
    pallas_call x1, Pallas kernels, local(): call(own_kernel, 'own', 0, [spec_rc, spec_rc, spec_nodes, spec_nodes, spe...  6.29 us
    all_to_all x1, starting transfers between devices, local(): lax.all_to_all(packed.reshape(64, 16, wider), ('y', 'z', 'x'), split_axis...  5.58 us
    pallas_call x1, Pallas kernels, local(): call(landing_kernel, 'landing', 0, [whole(8, 256), spec_nodes, whole(slot...  5.23 us
  transfers between devices with their start and end apart: 5, of which 4 were waited for; matrix products, arithmetic and copies ran while one was open for 2% of the time, Pallas kernels for 22%

profile of v7, /device:TPU:1, one launch (start us, length us, event | category | flops | bytes accessed | tf_op | source)
XLA Modules:
  0.0 95.1 jit_solution(8423822673822290457)
XLA Ops:
  0.6 0.0 copy-start
  0.7 0.0 copy-start.8
  0.7 0.0 copy-start.3
  0.7 0.0 copy-start.9
  0.7 0.0 copy-start.10
  0.7 2.4 %fusion = f32[512,512]{1,0:T(8,128)S(1)} fusion(bf16[1024,512]{1,0:T(8,128)(2,1)} %cot_ref.1, bf16[1024,512]{1,0:T(8,128)(2,1)} %param.11, bf16[1024,512]{1,0:T(8,128)(2,1)} %param.10, pred[]{:T(512)S(6)} %eq.4), kind=kOutput, calls=%fused_computation.1 | convolution fusion | flops 537395200 | bytes 4194305 | tf_op jit(solution)/shard_map/dot_general | solution.py:25
  3.1 1.5 %collective-permute-start = (f32[512,512]{1,0:T(8,128)S(1)}, f32[512,512]{1,0:T(8,128)S(1)}, u32[]{:S(2)}, u32[]{:S(2)}) collective-permute-start(f32[512,512]{1,0:T(8,128)S(1)} %fusion), channel_id=1, source_target_pairs={{0,16},{16,0},{1,17},{17,1},{2,18},{18,2},{3,19},{19,3},{4,20},{20... | collective-permute-start | bytes 3145736 | tf_op jit(solution)/shard_map/ppermute | solution.py:293
  4.6 0.0 copy-done.8
  4.6 0.0 copy-done.3
  4.6 0.0 copy-done.9
  4.7 0.0 copy-done.10
  4.7 0.7 fusion.2.keep
  5.4 0.0 copy-done
  5.4 0.0 copy-start.5
  5.4 0.0 copy-start.6
  5.4 0.7 divide_convert_fusion.msg.msg_ref
  6.2 0.7 collective-permute-done.came
  6.9 0.0 copy-done.5
  6.9 0.0 copy-done.6
  6.9 6.4 %ghost.1 = bf16[2048,640]{1,0:T(8,128)(2,1)} custom-call(s32[3,128]{1,0:T(4,128)S(1)} %bitcast.13, s32[3,128]{1,0:T(4,128)S(1)} %bitcast.16, bf16[1024,512]{1,0:T(8,128)(2,1)S(1)} %divide_convert_fusion.msg.msg_ref, f32[512,512]{1,0:T(8,128)S(1)} %fusion.2.keep, f32[512,512]{1,0:T(8,128)S(1)} %collective-permute-done.came, bf16[384,128,128]{2,1,0:T(8,128)(2,1)} %vals_hbm.5), custom_call_target="tpu_custom_call" | custom-call | flops 2147483648 | bytes 9437184 | tf_op jit(solution)/shard_map/ghost/pallas_call | solution.py:298
  13.3 10.8 %all-to-all-start = ((bf16[128,16,640]{2,1,0:T(8,128)(2,1)}), bf16[128,16,640]{2,1,0:T(8,128)(2,1)}, u32[]{:S(2)}, u32[]{:S(2)}) async-start(bf16[128,16,640]{2,1,0:T(8,128)(2,1)} %bitcast.19), calls=%async_computation | async-start | bytes 5242880 | tf_op jit(solution)/shard_map/all_to_all | solution.py:314
  24.1 0.0 copy-start.4
  24.1 6.8 %hub.1 = (f32[1024,512]{1,0:T(8,128)S(1)}, f32[1024,512]{1,0:T(8,128)S(1)}) custom-call(s32[1]{0:T(128)} %bitcast.4.core, s32[3,128]{1,0:T(4,128)S(1)} %bitcast.14, s32[3,128]{1,0:T(4,128)S(1)} %bitcast.17, bf16[1024,512]{1,0:T(8,128)(2,1)S(1)} %divide_convert_fusion.msg.msg_ref, bf16[384,128,128]{2,1,0:T(8,128)(2,1)} %vals_hbm.5), custom_call_target="tpu_custom_call" | custom-call | flops 2147483648 | bytes 9437184 | tf_op jit(solution)/shard_map/hub/pallas_call | solution.py:319
  30.9 1.2 %collective-permute-start.1 = (f32[1024,512]{1,0:T(8,128)S(1)}, f32[1024,512]{1,0:T(8,128)S(1)}, u32[]{:S(2)}, u32[]{:S(2)}) collective-permute-start(f32[1024,512]{1,0:T(8,128)S(1)} %get-tuple-element.10), channel_id=1, source_target_pairs={{0,16},{16,0},{1,17},{17,1},{2,18},{18,2},{3,19},{19,3},{4,20},{20... | collective-permute-start | bytes 6291464 | tf_op jit(solution)/shard_map/ppermute | solution.py:324
  32.1 0.0 copy-done.4
  32.1 6.3 %own.1.own_ref = f32[1024,512]{1,0:T(8,128)S(1)} custom-call(s32[3,128]{1,0:T(4,128)S(1)} %bitcast.15, s32[3,128]{1,0:T(4,128)S(1)} %bitcast.18, bf16[1024,512]{1,0:T(8,128)(2,1)S(1)} %divide_convert_fusion.msg.msg_ref, bf16[1024,512]{1,0:T(8,128)(2,1)S(1)} %copy-done.3, bf16[512,512]{1,0:T(8,128)(2,1)S(1)} %copy-done.4, bf16[384,128,128]{2,1,0:T(8,128)(2,1)} %vals_hbm.5), custom_call_target="tpu_custom_call" | custom-call | flops 2684354560 | bytes 7340032 | tf_op jit(solution)/shard_map/own/pallas_call | solution.py:325
  38.4 0.0 copy-start.1
  38.4 1.3 %copy-done.1 = f32[1024,512]{1,0:T(8,128)} copy-done((f32[1024,512]{1,0:T(8,128)}, f32[1024,512]{1,0:T(8,128)S(1)}, u32[]{:S(2)}) %copy-start.1) | copy-done | bytes 2097176
  39.7 0.0 collective-permute-done.1.came_ref
  39.7 1.7 %hub_pack.1.packed_hbm = bf16[1024,768]{1,0:T(8,128)(2,1)} custom-call(f32[1024,512]{1,0:T(8,128)S(1)} %get-tuple-element.9.keep_ref, f32[1024,512]{1,0:T(8,128)S(1)} %collective-permute-done.1.came_ref), custom_call_target="tpu_custom_call" | custom-call | flops 524288 | bytes 5242880 | tf_op jit(solution)/shard_map/hub_pack/pallas_call | solution.py:333
  41.4 17.3 %all-to-all-done = bf16[128,16,640]{2,1,0:T(8,128)(2,1)} async-done(((bf16[128,16,640]{2,1,0:T(8,128)(2,1)}), bf16[128,16,640]{2,1,0:T(8,128)(2,1)}, u32[]{:S(2)}, u32[]{:S(2)}) %all-to-all-start) | async-done | bytes 2621472 | tf_op jit(solution)/shard_map/all_to_all | solution.py:314
  58.7 2.0 %spread.1 = bf16[1024,768]{1,0:T(8,128)(2,1)} custom-call(bf16[2048,640]{1,0:T(8,128)(2,1)} %bitcast.3.arrived_ref, bf16[1024,768]{1,0:T(8,128)(2,1)} %hub_pack.1.packed_hbm), custom_call_target="tpu_custom_call", output_to_operand_aliasing={{}: (1, {})} | custom-call | flops 262144 | bytes 1048576 | tf_op jit(solution)/shard_map/spread/pallas_call | solution.py:338
  60.7 0.0 copy-start.7
  60.7 5.6 %all-to-all-start.1 = ((bf16[64,16,768]{2,1,0:T(8,128)(2,1)}), bf16[64,16,768]{2,1,0:T(8,128)(2,1)S(1)}, u32[]{:S(2)}, u32[]{:S(2)}) async-start(bf16[64,16,768]{2,1,0:T(8,128)(2,1)} %bitcast.5), calls=%async_computation.1 | async-start | bytes 3145728 | tf_op jit(solution)/shard_map/all_to_all | solution.py:343
  66.3 0.0 copy-done.7
  66.3 0.1 copy.15
  66.4 0.1 reshape.39.targets_ref
  66.5 0.0 copy-start.2
  66.5 1.6 %copy-done.2 = f32[1024,512]{1,0:T(8,128)S(1)} copy-done((f32[1024,512]{1,0:T(8,128)S(1)}, f32[1024,512]{1,0:T(8,128)}, u32[]{:S(2)}) %copy-start.2) | copy-done | bytes 2097176
  68.1 5.2 %landing.1 = f32[1024,512]{1,0:T(8,128)} custom-call(s32[8,256]{1,0:T(8,128)S(1)} %reshape.39.targets_ref, f32[1024,512]{1,0:T(8,128)S(1)} %copy-done.2, bf16[2048,640]{1,0:T(8,128)(2,1)} %bitcast.3.arrived_ref), custom_call_target="tpu_custom_call" | custom-call | flops 2147483648 | bytes 7340032 | tf_op jit(solution)/shard_map/landing/pallas_call | solution.py:347
  73.4 16.1 %all-to-all-done.1 = bf16[64,16,768]{2,1,0:T(8,128)(2,1)S(1)} async-done(((bf16[64,16,768]{2,1,0:T(8,128)(2,1)}), bf16[64,16,768]{2,1,0:T(8,128)(2,1)S(1)}, u32[]{:S(2)}, u32[]{:S(2)}) %all-to-all-start.1) | async-done | bytes 1572896 | tf_op jit(solution)/shard_map/all_to_all | solution.py:343
  89.5 2.5 %collective-permute-start.2 = (bf16[1024,256]{1,0:T(8,128)(2,1)S(1)}, bf16[1024,256]{1,0:T(8,128)(2,1)S(1)}, u32[]{:S(2)}, u32[]{:S(2)}) collective-permute-start(bf16[1024,256]{1,0:T(8,128)(2,1)S(1)} %slice.3.mine_ref), channel_id=1, source_target_pairs={{0,16},{16,0},{1,17},{17,1},{2,18},{18,2},{3,19},{19,3},{4,20},{20... | collective-permute-start | bytes 1572872 | tf_op jit(solution)/shard_map/ppermute | solution.py:354
  92.0 0.8 hub_sum.1
  92.8 0.7 collective-permute-done.2.came_ref
  93.5 1.6 %join.1 = f32[2,512,512]{2,1,0:T(8,128)} custom-call(s32[1]{0:T(128)} %bitcast.4.core, bf16[1024,256]{1,0:T(8,128)(2,1)S(1)} %slice.3.mine_ref, bf16[1024,256]{1,0:T(8,128)(2,1)S(1)} %collective-permute-done.2.came_ref), custom_call_target="tpu_custom_call" | custom-call | flops 524288 | bytes 3145728 | tf_op jit(solution)/shard_map/join/pallas_call | solution.py:359
  (2 shorter events, 0.0 us)
Async XLA Ops:
  0.6 4.8 %copy-start = (bf16[512,512]{1,0:T(8,128)(2,1)S(1)}, bf16[512,512]{1,0:T(8,128)(2,1)}, u32[]{:S(2)}) copy-start(bf16[512,512]{1,0:T(8,128)(2,1)} %param.14) | copy-start | bytes 1572868
  0.7 4.0 %copy-start.8 = (s32[1024]{0:T(1024)S(1)}, s32[1024]{0:T(1024)}, u32[]{:S(2)}) copy-start(s32[1024]{0:T(1024)} %param.15) | copy-start | bytes 12292
  0.7 4.0 %copy-start.3 = (bf16[1024,512]{1,0:T(8,128)(2,1)S(1)}, bf16[1024,512]{1,0:T(8,128)(2,1)}, u32[]{:S(2)}) copy-start(bf16[1024,512]{1,0:T(8,128)(2,1)} %cot_ref.1) | copy-start | bytes 3145732
  0.7 4.0 %copy-start.9 = (bf16[1024,512]{1,0:T(8,128)(2,1)S(1)}, bf16[1024,512]{1,0:T(8,128)(2,1)}, u32[]{:S(2)}) copy-start(bf16[1024,512]{1,0:T(8,128)(2,1)} %param.10) | copy-start | bytes 3145732
  0.7 4.0 %copy-start.10 = (bf16[1024,512]{1,0:T(8,128)(2,1)S(1)}, bf16[1024,512]{1,0:T(8,128)(2,1)}, u32[]{:S(2)}) copy-start(bf16[1024,512]{1,0:T(8,128)(2,1)} %param.11) | copy-start | bytes 3145732
  3.1 3.8 %collective-permute-start = (f32[512,512]{1,0:T(8,128)S(1)}, f32[512,512]{1,0:T(8,128)S(1)}, u32[]{:S(2)}, u32[]{:S(2)}) collective-permute-start(f32[512,512]{1,0:T(8,128)S(1)} %fusion), channel_id=1, source_target_pairs={{0,16},{16,0},{1,17},{17,1},{2,18},{18,2},{3,19},{19,3},{4,20},{20... | collective-permute-start | bytes 3145736 | tf_op jit(solution)/shard_map/ppermute | solution.py:293
  5.4 1.5 %copy-start.5 = (s32[384]{0:T(512)S(1)}, s32[384]{0:T(512)}, u32[]{:S(2)}) copy-start(s32[384]{0:T(512)} %param.16) | copy-start | bytes 4612
  5.4 1.5 %copy-start.6 = (s32[384]{0:T(512)S(1)}, s32[384]{0:T(512)}, u32[]{:S(2)}) copy-start(s32[384]{0:T(512)} %param.17) | copy-start | bytes 4612
  13.3 45.4 %all-to-all-start = ((bf16[128,16,640]{2,1,0:T(8,128)(2,1)}), bf16[128,16,640]{2,1,0:T(8,128)(2,1)}, u32[]{:S(2)}, u32[]{:S(2)}) async-start(bf16[128,16,640]{2,1,0:T(8,128)(2,1)} %bitcast.19), calls=%async_computation | async-start | bytes 5242880 | tf_op jit(solution)/shard_map/all_to_all | solution.py:314
  24.1 8.0 %copy-start.4 = (bf16[512,512]{1,0:T(8,128)(2,1)S(1)}, bf16[512,512]{1,0:T(8,128)(2,1)}, u32[]{:S(2)}) copy-start(bf16[512,512]{1,0:T(8,128)(2,1)} %w_ref.1) | copy-start | bytes 1572868
  30.9 8.8 %collective-permute-start.1 = (f32[1024,512]{1,0:T(8,128)S(1)}, f32[1024,512]{1,0:T(8,128)S(1)}, u32[]{:S(2)}, u32[]{:S(2)}) collective-permute-start(f32[1024,512]{1,0:T(8,128)S(1)} %get-tuple-element.10), channel_id=1, source_target_pairs={{0,16},{16,0},{1,17},{17,1},{2,18},{18,2},{3,19},{19,3},{4,20},{20... | collective-permute-start | bytes 6291464 | tf_op jit(solution)/shard_map/ppermute | solution.py:324
  38.4 1.3 %copy-start.1 = (f32[1024,512]{1,0:T(8,128)}, f32[1024,512]{1,0:T(8,128)S(1)}, u32[]{:S(2)}) copy-start(f32[1024,512]{1,0:T(8,128)S(1)} %own.1.own_ref) | copy-start | bytes 6291460
  60.7 5.6 %copy-start.7 = (s32[1,128,16]{1,2,0:T(8,128)S(1)}, s32[1,128,16]{1,2,0:T(8,128)}, u32[]{:S(2)}) copy-start(s32[1,128,16]{1,2,0:T(8,128)} %param.19) | copy-start | bytes 24580
  60.7 28.7 %all-to-all-start.1 = ((bf16[64,16,768]{2,1,0:T(8,128)(2,1)}), bf16[64,16,768]{2,1,0:T(8,128)(2,1)S(1)}, u32[]{:S(2)}, u32[]{:S(2)}) async-start(bf16[64,16,768]{2,1,0:T(8,128)(2,1)} %bitcast.5), calls=%async_computation.1 | async-start | bytes 3145728 | tf_op jit(solution)/shard_map/all_to_all | solution.py:343
  66.5 1.6 %copy-start.2 = (f32[1024,512]{1,0:T(8,128)S(1)}, f32[1024,512]{1,0:T(8,128)}, u32[]{:S(2)}) copy-start(f32[1024,512]{1,0:T(8,128)} %copy-done.1) | copy-start | bytes 6291460
  89.5 4.0 %collective-permute-start.2 = (bf16[1024,256]{1,0:T(8,128)(2,1)S(1)}, bf16[1024,256]{1,0:T(8,128)(2,1)S(1)}, u32[]{:S(2)}, u32[]{:S(2)}) collective-permute-start(bf16[1024,256]{1,0:T(8,128)(2,1)S(1)} %slice.3.mine_ref), channel_id=1, source_target_pairs={{0,16},{16,0},{1,17},{17,1},{2,18},{18,2},{3,19},{19,3},{4,20},{20... | collective-permute-start | bytes 1572872 | tf_op jit(solution)/shard_map/ppermute | solution.py:354

commit v8 on v7

--- a/solution.py
+++ b/solution.py
@@ -218,20 +218,34 @@
             nodes_ref[...] += part
 
 
-def hub_sum_kernel(arrived_ref, hubs_ref):
+def write_half(core, source_ref, lanes, half, sent, weights_hbm, sem):
+    for y in range(4):
+        for c in range(2):
+            block = source_ref[y * 256 : (y + 1) * 256, lanes + c * TILE : lanes + (c + 1) * TILE]
+            half[c, :, y * TILE : (y + 1) * TILE] = block.astype(F32)
+    place = pl.ds(pl.multiple_of(core * 256, 256), 256)
+    for c in range(2):
+        sent.append(pltpu.make_async_copy(half.at[c], weights_hbm.at[c, place], sem.at[c]))
+        sent[-1].start()
+
+
+def finish_kernel(core, shared_ref, hubs_ref, weights_hbm, half, sem):
+    sent = []
+    write_half(core[0], shared_ref, WIDTH, half, sent, weights_hbm, sem)
     total = jnp.zeros((16, WIDTH), F32)
     for p in range(64):
-        total += arrived_ref[16 * p : 16 * p + 16, :].astype(F32)
+        total += shared_ref[16 * p : 16 * p + 16, :WIDTH].astype(F32)
     hubs_ref[...] = total
-
-
-def join_kernel(core, mine_ref, came_ref, out_ref):
-    for ref, part in ((mine_ref, core[0]), (came_ref, 1 - core[0])):
-        place = pl.ds(pl.multiple_of(part * 256, 256), 256)
-        for y in range(4):
-            for c in range(2):
-                block = ref[y * 256 : (y + 1) * 256, c * TILE : (c + 1) * TILE]
-                out_ref[c, place, y * TILE : (y + 1) * TILE] = block.astype(F32)
+    for copy in sent:
+        copy.wait()
+
+
+def join_kernel(core, came_ref, partial_hbm, weights_hbm, half, sem):
+    del partial_hbm
+    sent = []
+    write_half(1 - core[0], came_ref, 0, half, sent, weights_hbm, sem)
+    for copy in sent:
+        copy.wait()
 
 
 def whole(*shape):
@@ -240,6 +254,7 @@
 
 ANY = pl.BlockSpec(memory_space=pl.ANY)
 INSIDE = pl.BlockSpec(memory_space=pltpu.VMEM)
+SCALAR = pl.BlockSpec(memory_space=pltpu.SMEM)
 OUTSIDE = pl.BlockSpec(memory_space=pltpu.HBM)
 
 
@@ -352,14 +367,16 @@
     shared, grad_nodes = lax.optimization_barrier((shared, grad_nodes))
     w_mine = shared[:, WIDTH:]
     w_theirs = lax.ppermute(w_mine, "core", swap)
-    grad_hubs = call(
-        hub_sum_kernel, "hub_sum", 0, [spec_nodes], whole(16, WIDTH),
-        jax.ShapeDtypeStruct((16, WIDTH), F32), [], NODES * WIDTH, 1 << 20, 6,
-    )(shared)
+    half = [pltpu.VMEM((2, WIDTH // 2, WIDTH), F32), pltpu.SemaphoreType.DMA((2,))]
+    grad_hubs, grad_weights = call(
+        finish_kernel, "finish", 0, [SCALAR, INSIDE], [INSIDE, OUTSIDE],
+        [jax.ShapeDtypeStruct((16, WIDTH), F32), pltpu.HBM((2, WIDTH, WIDTH), F32)],
+        half, NODES * WIDTH, 3 << 20, 8, grid=(),
+    )(core_arg, shared)
     grad_weights = call(
-        join_kernel, "join", 1, [whole(NODES, 2 * TILE)] * 2, whole(2, WIDTH, WIDTH),
-        jax.ShapeDtypeStruct((2, WIDTH, WIDTH), F32), [], NODES * WIDTH, 3 << 20, 10,
-    )(core_arg, w_mine, w_theirs)
+        join_kernel, "join", 0, [SCALAR, INSIDE, OUTSIDE], OUTSIDE, pltpu.HBM((2, WIDTH, WIDTH), F32),
+        half, NODES * WIDTH, 2 << 20, 8, grid=(), input_output_aliases={2: 0},
+    )(core_arg, w_theirs, pltpu.with_memory_space_constraint(grad_weights, pltpu.HBM))
     return (grad_nodes, grad_hubs, grad_weights)
 
 

time: 95.6 us -> 95.3 us (level)
  transfers between devices with their start and end apart: 5 -> 5, of which waited for: 4 -> 3; matrix products, arithmetic and copies ran while one was open for 2% -> 2% of each run, Pallas kernels for 22% -> 23%
where the time goes in v8:
time: 95.3 us; the launch traced here: 94.8 us
  waiting for transfers between devices  34.1 us (36%)
  Pallas kernels  31.1 us (33%)
  starting transfers between devices  21.6 us (23%)
  matrix products  3.92 us (4%)
  local copies, waits for them, and re-layouts  3.17 us (3%)
    all_to_all x1, waiting for transfers between devices, local(): lax.all_to_all(packed.reshape(128, 16, wide), ALL, split_axis=0, concat_a...  17.3 us
    all_to_all x1, waiting for transfers between devices, local(): lax.all_to_all(packed.reshape(64, 16, wider), ('y', 'z', 'x'), split_axis...  16.1 us
    all_to_all x1, starting transfers between devices, local(): lax.all_to_all(packed.reshape(128, 16, wide), ALL, split_axis=0, concat_a...  10.8 us
    pallas_call x1, Pallas kernels, local(): call(hub_kernel, 'hub', 1, [spec_rc, spec_rc, spec_nodes, OUTSIDE], [spec...  6.79 us
    pallas_call x1, Pallas kernels, local(): call(own_kernel, 'own', 0, [spec_rc, spec_rc, spec_nodes, spec_nodes, spe...  6.29 us
    pallas_call x1, Pallas kernels, local(): call(ghost_kernel, 'ghost', 0, [INSIDE] * 5 + [OUTSIDE], OUTSIDE, pltpu.H...  6.29 us
    all_to_all x1, starting transfers between devices, local(): lax.all_to_all(packed.reshape(64, 16, wider), ('y', 'z', 'x'), split_axis...  5.58 us
    pallas_call x1, Pallas kernels, local(): call(landing_kernel, 'landing', 0, [whole(8, 256), spec_nodes, whole(slot...  5.23 us
  transfers between devices with their start and end apart: 5, of which 3 were waited for; matrix products, arithmetic and copies ran while one was open for 2% of the time, Pallas kernels for 23%

profile of v8, /device:TPU:1, one launch (start us, length us, event | category | flops | bytes accessed | tf_op | source)
XLA Modules:
  0.0 94.8 jit_solution(3948652324586838708)
XLA Ops:
  0.6 0.0 copy-start
  0.7 0.0 copy-start.8
  0.7 0.0 copy-start.3
  0.7 0.0 copy-start.9
  0.7 0.0 copy-start.10
  0.7 2.4 %fusion = f32[512,512]{1,0:T(8,128)S(1)} fusion(bf16[1024,512]{1,0:T(8,128)(2,1)} %cot_ref.1, bf16[1024,512]{1,0:T(8,128)(2,1)} %param.11, bf16[1024,512]{1,0:T(8,128)(2,1)} %param.10, pred[]{:T(512)S(6)} %eq.4), kind=kOutput, calls=%fused_computation.1 | convolution fusion | flops 537395200 | bytes 4194305 | tf_op jit(solution)/shard_map/dot_general | solution.py:25
  3.1 1.5 %collective-permute-start = (f32[512,512]{1,0:T(8,128)S(1)}, f32[512,512]{1,0:T(8,128)S(1)}, u32[]{:S(2)}, u32[]{:S(2)}) collective-permute-start(f32[512,512]{1,0:T(8,128)S(1)} %fusion), channel_id=1, source_target_pairs={{0,16},{16,0},{1,17},{17,1},{2,18},{18,2},{3,19},{19,3},{4,20},{20... | collective-permute-start | bytes 3145736 | tf_op jit(solution)/shard_map/ppermute | solution.py:308
  4.6 0.0 copy-done.8
  4.7 0.0 copy-done.3
  4.7 0.0 copy-done.9
  4.7 0.0 copy-done.10
  4.7 0.7 fusion.2.keep
  5.4 0.0 copy-done
  5.4 0.0 copy-start.5
  5.4 0.0 copy-start.6
  5.4 0.7 divide_convert_fusion.msg.msg_ref
  6.2 0.7 collective-permute-done.came
  6.9 0.0 copy-done.5
  6.9 0.0 copy-done.6
  6.9 6.3 %ghost.1 = bf16[2048,640]{1,0:T(8,128)(2,1)} custom-call(s32[3,128]{1,0:T(4,128)S(1)} %bitcast.13, s32[3,128]{1,0:T(4,128)S(1)} %bitcast.16, bf16[1024,512]{1,0:T(8,128)(2,1)S(1)} %divide_convert_fusion.msg.msg_ref, f32[512,512]{1,0:T(8,128)S(1)} %fusion.2.keep, f32[512,512]{1,0:T(8,128)S(1)} %collective-permute-done.came, bf16[384,128,128]{2,1,0:T(8,128)(2,1)} %vals_hbm.5), custom_call_target="tpu_custom_call" | custom-call | flops 2147483648 | bytes 9437184 | tf_op jit(solution)/shard_map/ghost/pallas_call | solution.py:313
  13.2 10.8 %all-to-all-start = ((bf16[128,16,640]{2,1,0:T(8,128)(2,1)}), bf16[128,16,640]{2,1,0:T(8,128)(2,1)}, u32[]{:S(2)}, u32[]{:S(2)}) async-start(bf16[128,16,640]{2,1,0:T(8,128)(2,1)} %bitcast.19), calls=%async_computation | async-start | bytes 5242880 | tf_op jit(solution)/shard_map/all_to_all | solution.py:329
  24.1 0.0 copy-start.4
  24.1 6.8 %hub.1 = (f32[1024,512]{1,0:T(8,128)S(1)}, f32[1024,512]{1,0:T(8,128)S(1)}) custom-call(s32[1]{0:T(128)} %bitcast.4.core, s32[3,128]{1,0:T(4,128)S(1)} %bitcast.14, s32[3,128]{1,0:T(4,128)S(1)} %bitcast.17, bf16[1024,512]{1,0:T(8,128)(2,1)S(1)} %divide_convert_fusion.msg.msg_ref, bf16[384,128,128]{2,1,0:T(8,128)(2,1)} %vals_hbm.5), custom_call_target="tpu_custom_call" | custom-call | flops 2147483648 | bytes 9437184 | tf_op jit(solution)/shard_map/hub/pallas_call | solution.py:334
  30.9 1.2 %collective-permute-start.1 = (f32[1024,512]{1,0:T(8,128)S(1)}, f32[1024,512]{1,0:T(8,128)S(1)}, u32[]{:S(2)}, u32[]{:S(2)}) collective-permute-start(f32[1024,512]{1,0:T(8,128)S(1)} %get-tuple-element.12), channel_id=1, source_target_pairs={{0,16},{16,0},{1,17},{17,1},{2,18},{18,2},{3,19},{19,3},{4,20},{20... | collective-permute-start | bytes 6291464 | tf_op jit(solution)/shard_map/ppermute | solution.py:339
  32.1 0.0 copy-done.4
  32.1 6.3 %own.1.own_ref = f32[1024,512]{1,0:T(8,128)S(1)} custom-call(s32[3,128]{1,0:T(4,128)S(1)} %bitcast.15, s32[3,128]{1,0:T(4,128)S(1)} %bitcast.18, bf16[1024,512]{1,0:T(8,128)(2,1)S(1)} %divide_convert_fusion.msg.msg_ref, bf16[1024,512]{1,0:T(8,128)(2,1)S(1)} %copy-done.3, bf16[512,512]{1,0:T(8,128)(2,1)S(1)} %copy-done.4, bf16[384,128,128]{2,1,0:T(8,128)(2,1)} %vals_hbm.5), custom_call_target="tpu_custom_call" | custom-call | flops 2684354560 | bytes 7340032 | tf_op jit(solution)/shard_map/own/pallas_call | solution.py:340
  38.4 0.0 copy-start.1
  38.4 1.3 %copy-done.1 = f32[1024,512]{1,0:T(8,128)} copy-done((f32[1024,512]{1,0:T(8,128)}, f32[1024,512]{1,0:T(8,128)S(1)}, u32[]{:S(2)}) %copy-start.1) | copy-done | bytes 2097176
  39.7 0.0 collective-permute-done.1.came_ref
  39.7 1.7 %hub_pack.1.packed_hbm = bf16[1024,768]{1,0:T(8,128)(2,1)} custom-call(f32[1024,512]{1,0:T(8,128)S(1)} %get-tuple-element.11.keep_ref, f32[1024,512]{1,0:T(8,128)S(1)} %collective-permute-done.1.came_ref), custom_call_target="tpu_custom_call" | custom-call | flops 524288 | bytes 5242880 | tf_op jit(solution)/shard_map/hub_pack/pallas_call | solution.py:348
  41.4 17.3 %all-to-all-done = bf16[128,16,640]{2,1,0:T(8,128)(2,1)} async-done(((bf16[128,16,640]{2,1,0:T(8,128)(2,1)}), bf16[128,16,640]{2,1,0:T(8,128)(2,1)}, u32[]{:S(2)}, u32[]{:S(2)}) %all-to-all-start) | async-done | bytes 2621472 | tf_op jit(solution)/shard_map/all_to_all | solution.py:329
  58.7 2.0 %spread.1 = bf16[1024,768]{1,0:T(8,128)(2,1)} custom-call(bf16[2048,640]{1,0:T(8,128)(2,1)} %bitcast.3.arrived_ref, bf16[1024,768]{1,0:T(8,128)(2,1)} %hub_pack.1.packed_hbm), custom_call_target="tpu_custom_call", output_to_operand_aliasing={{}: (1, {})} | custom-call | flops 262144 | bytes 1048576 | tf_op jit(solution)/shard_map/spread/pallas_call | solution.py:353
  60.7 0.0 copy-start.7
  60.7 5.6 %all-to-all-start.1 = ((bf16[64,16,768]{2,1,0:T(8,128)(2,1)}), bf16[64,16,768]{2,1,0:T(8,128)(2,1)S(1)}, u32[]{:S(2)}, u32[]{:S(2)}) async-start(bf16[64,16,768]{2,1,0:T(8,128)(2,1)} %bitcast.5), calls=%async_computation.1 | async-start | bytes 3145728 | tf_op jit(solution)/shard_map/all_to_all | solution.py:358
  66.3 0.0 copy-done.7
  66.3 0.1 copy.16
  66.4 0.1 reshape.39.targets_ref
  66.5 0.0 copy-start.2
  66.5 1.6 %copy-done.2 = f32[1024,512]{1,0:T(8,128)S(1)} copy-done((f32[1024,512]{1,0:T(8,128)S(1)}, f32[1024,512]{1,0:T(8,128)}, u32[]{:S(2)}) %copy-start.2) | copy-done | bytes 2097176
  68.1 5.2 %landing.1 = f32[1024,512]{1,0:T(8,128)} custom-call(s32[8,256]{1,0:T(8,128)S(1)} %reshape.39.targets_ref, f32[1024,512]{1,0:T(8,128)S(1)} %copy-done.2, bf16[2048,640]{1,0:T(8,128)(2,1)} %bitcast.3.arrived_ref), custom_call_target="tpu_custom_call" | custom-call | flops 2147483648 | bytes 7340032 | tf_op jit(solution)/shard_map/landing/pallas_call | solution.py:362
  73.4 16.1 %all-to-all-done.1 = bf16[64,16,768]{2,1,0:T(8,128)(2,1)S(1)} async-done(((bf16[64,16,768]{2,1,0:T(8,128)(2,1)}), bf16[64,16,768]{2,1,0:T(8,128)(2,1)S(1)}, u32[]{:S(2)}, u32[]{:S(2)}) %all-to-all-start.1) | async-done | bytes 1572896 | tf_op jit(solution)/shard_map/all_to_all | solution.py:358
  89.5 2.5 %collective-permute-start.2 = (bf16[1024,256]{1,0:T(8,128)(2,1)S(1)}, bf16[1024,256]{1,0:T(8,128)(2,1)S(1)}, u32[]{:S(2)}, u32[]{:S(2)}) collective-permute-start(bf16[1024,256]{1,0:T(8,128)(2,1)S(1)} %slice.3), channel_id=1, source_target_pairs={{0,16},{16,0},{1,17},{17,1},{2,18},{18,2},{3,19},{19,3},{4,20},{20... | collective-permute-start | bytes 1572872 | tf_op jit(solution)/shard_map/ppermute | solution.py:369
  92.0 1.7 %finish.1 = (f32[16,512]{1,0:T(8,128)}, f32[2,512,512]{2,1,0:T(8,128)}) custom-call(s32[1]{0:T(128)} %bitcast.4.core, bf16[1024,768]{1,0:T(8,128)(2,1)S(1)} %bitcast.12), custom_call_target="tpu_custom_call" | custom-call | flops 524288 | bytes 3145728 | tf_op jit(solution)/shard_map/finish/pallas_call | solution.py:371
  93.7 0.0 collective-permute-done.2.came_ref
  93.7 1.1 %join.1 = f32[2,512,512]{2,1,0:T(8,128)} custom-call(s32[1]{0:T(128)} %bitcast.4.core, bf16[1024,256]{1,0:T(8,128)(2,1)S(1)} %collective-permute-done.2.came_ref, f32[2,512,512]{2,1,0:T(8,128)} %get-tuple-element.18.partial_hbm), custom_call_target="tpu_custom_call", output_to_operand_aliasing={{}: (2, {})} | custom-call | flops 524288 | bytes 2097152 | tf_op jit(solution)/shard_map/join/pallas_call | solution.py:376
  (2 shorter events, 0.0 us)
Async XLA Ops:
  0.6 4.8 %copy-start = (bf16[512,512]{1,0:T(8,128)(2,1)S(1)}, bf16[512,512]{1,0:T(8,128)(2,1)}, u32[]{:S(2)}) copy-start(bf16[512,512]{1,0:T(8,128)(2,1)} %param.14) | copy-start | bytes 1572868
  0.7 4.0 %copy-start.8 = (s32[1024]{0:T(1024)S(1)}, s32[1024]{0:T(1024)}, u32[]{:S(2)}) copy-start(s32[1024]{0:T(1024)} %param.15) | copy-start | bytes 12292
  0.7 4.0 %copy-start.3 = (bf16[1024,512]{1,0:T(8,128)(2,1)S(1)}, bf16[1024,512]{1,0:T(8,128)(2,1)}, u32[]{:S(2)}) copy-start(bf16[1024,512]{1,0:T(8,128)(2,1)} %cot_ref.1) | copy-start | bytes 3145732
  0.7 4.0 %copy-start.9 = (bf16[1024,512]{1,0:T(8,128)(2,1)S(1)}, bf16[1024,512]{1,0:T(8,128)(2,1)}, u32[]{:S(2)}) copy-start(bf16[1024,512]{1,0:T(8,128)(2,1)} %param.10) | copy-start | bytes 3145732
  0.7 4.0 %copy-start.10 = (bf16[1024,512]{1,0:T(8,128)(2,1)S(1)}, bf16[1024,512]{1,0:T(8,128)(2,1)}, u32[]{:S(2)}) copy-start(bf16[1024,512]{1,0:T(8,128)(2,1)} %param.11) | copy-start | bytes 3145732
  3.1 3.8 %collective-permute-start = (f32[512,512]{1,0:T(8,128)S(1)}, f32[512,512]{1,0:T(8,128)S(1)}, u32[]{:S(2)}, u32[]{:S(2)}) collective-permute-start(f32[512,512]{1,0:T(8,128)S(1)} %fusion), channel_id=1, source_target_pairs={{0,16},{16,0},{1,17},{17,1},{2,18},{18,2},{3,19},{19,3},{4,20},{20... | collective-permute-start | bytes 3145736 | tf_op jit(solution)/shard_map/ppermute | solution.py:308
  5.4 1.5 %copy-start.5 = (s32[384]{0:T(512)S(1)}, s32[384]{0:T(512)}, u32[]{:S(2)}) copy-start(s32[384]{0:T(512)} %param.16) | copy-start | bytes 4612
  5.4 1.5 %copy-start.6 = (s32[384]{0:T(512)S(1)}, s32[384]{0:T(512)}, u32[]{:S(2)}) copy-start(s32[384]{0:T(512)} %param.17) | copy-start | bytes 4612
  13.2 45.5 %all-to-all-start = ((bf16[128,16,640]{2,1,0:T(8,128)(2,1)}), bf16[128,16,640]{2,1,0:T(8,128)(2,1)}, u32[]{:S(2)}, u32[]{:S(2)}) async-start(bf16[128,16,640]{2,1,0:T(8,128)(2,1)} %bitcast.19), calls=%async_computation | async-start | bytes 5242880 | tf_op jit(solution)/shard_map/all_to_all | solution.py:329
  24.1 8.0 %copy-start.4 = (bf16[512,512]{1,0:T(8,128)(2,1)S(1)}, bf16[512,512]{1,0:T(8,128)(2,1)}, u32[]{:S(2)}) copy-start(bf16[512,512]{1,0:T(8,128)(2,1)} %w_ref.1) | copy-start | bytes 1572868
  30.9 8.8 %collective-permute-start.1 = (f32[1024,512]{1,0:T(8,128)S(1)}, f32[1024,512]{1,0:T(8,128)S(1)}, u32[]{:S(2)}, u32[]{:S(2)}) collective-permute-start(f32[1024,512]{1,0:T(8,128)S(1)} %get-tuple-element.12), channel_id=1, source_target_pairs={{0,16},{16,0},{1,17},{17,1},{2,18},{18,2},{3,19},{19,3},{4,20},{20... | collective-permute-start | bytes 6291464 | tf_op jit(solution)/shard_map/ppermute | solution.py:339
  38.4 1.3 %copy-start.1 = (f32[1024,512]{1,0:T(8,128)}, f32[1024,512]{1,0:T(8,128)S(1)}, u32[]{:S(2)}) copy-start(f32[1024,512]{1,0:T(8,128)S(1)} %own.1.own_ref) | copy-start | bytes 6291460
  60.7 5.6 %copy-start.7 = (s32[1,128,16]{1,2,0:T(8,128)S(1)}, s32[1,128,16]{1,2,0:T(8,128)}, u32[]{:S(2)}) copy-start(s32[1,128,16]{1,2,0:T(8,128)} %param.19) | copy-start | bytes 24580
  60.7 28.7 %all-to-all-start.1 = ((bf16[64,16,768]{2,1,0:T(8,128)(2,1)}), bf16[64,16,768]{2,1,0:T(8,128)(2,1)S(1)}, u32[]{:S(2)}, u32[]{:S(2)}) async-start(bf16[64,16,768]{2,1,0:T(8,128)(2,1)} %bitcast.5), calls=%async_computation.1 | async-start | bytes 3145728 | tf_op jit(solution)/shard_map/all_to_all | solution.py:358
  66.5 1.6 %copy-start.2 = (f32[1024,512]{1,0:T(8,128)S(1)}, f32[1024,512]{1,0:T(8,128)}, u32[]{:S(2)}) copy-start(f32[1024,512]{1,0:T(8,128)} %copy-done.1) | copy-start | bytes 6291460
  89.5 4.2 %collective-permute-start.2 = (bf16[1024,256]{1,0:T(8,128)(2,1)S(1)}, bf16[1024,256]{1,0:T(8,128)(2,1)S(1)}, u32[]{:S(2)}, u32[]{:S(2)}) collective-permute-start(bf16[1024,256]{1,0:T(8,128)(2,1)S(1)} %slice.3), channel_id=1, source_target_pairs={{0,16},{16,0},{1,17},{17,1},{2,18},{18,2},{3,19},{19,3},{4,20},{20... | collective-permute-start | bytes 1572872 | tf_op jit(solution)/shard_map/ppermute | solution.py:369

commit v9 on v8

--- a/solution.py
+++ b/solution.py
@@ -18,7 +18,7 @@
 OWN_BLOCKS = 8
 UNROLL = 8
 PLAN = 256
-LAYERS = 4
+LAYERS = 3
 
 
 def contract(a, b, da, db):
@@ -121,38 +121,46 @@
     plan_vmem[:, REG:] = other.astype(jnp.int32)
 
 
-def ghost_kernel(rows_ref, cols_ref, msg, keep, came, vals_hbm, out_hbm,
-                 vals, dense, out, plan_vmem, plan, sem, out_sems, plan_sem):
+def ready_kernel(rows_ref, cols_ref, deg_ref, cot_ref, w_ref, vals_hbm, msg, vals, tables, plan, sem, plan_sem):
     tiles = load_tiles(2, vals_hbm, vals, sem)
-    write_cells(2, rows_ref, cols_ref, plan_vmem)
-    ready = pltpu.make_async_copy(plan_vmem, plan, plan_sem)
+    write_cells(2, rows_ref, cols_ref, tables)
+    ready = pltpu.make_async_copy(tables, plan, plan_sem)
     ready.start()
+    scale = jnp.transpose(1.0 / deg_ref[...].astype(F32))
+    for r in range(NODES // TILE):
+        block = slice(r * TILE, (r + 1) * TILE)
+        msg[block, :] = (contract(cot_ref[block, :], w_ref[...], 1, 1) * scale[:, r : r + 1]).astype(BF16)
+    ready.wait()
+    tiles.wait()
+
+    def large(k, carry):
+        cell = plan[1, REG + k]
+        start = plan[2, REG + cell]
+
+        def add(i, total):
+            return total + vals[plan[0, REG + start + i]].astype(F32)
+
+        total = lax.fori_loop(0, plan[3, REG + cell], add, jnp.zeros((TILE, TILE), F32))
+        vals[REG + 1 + k] = total.astype(BF16)
+        return carry
+
+    lax.fori_loop(0, plan[4, REG], large, 0)
+
+
+def ghost_kernel(plan, msg, keep, came, vals, out_hbm, dense, out, out_sems):
+    per = NODES // TILE
     for b in range(4):
         lanes = slice(b * TILE, (b + 1) * TILE)
         out[b * WIDTH : (b + 1) * WIDTH, WIDTH:] = (keep[:, lanes] + came[:, lanes]).astype(BF16)
-    ready.wait()
-    tiles.wait()
-    per = NODES // TILE
-
-    def large(k, carry):
-        cell = plan[1, REG + k]
-        start = plan[2, REG + cell]
-
-        def add(i, total):
-            return total + vals[plan[0, REG + start + i]].astype(F32)
-
-        total = lax.fori_loop(0, plan[3, REG + cell], add, jnp.zeros((TILE, TILE), F32))
-        vals[REG + 1 + k] = total.astype(BF16)
-        return carry
-
-    lax.fori_loop(0, plan[4, REG], large, 0)
     sent = []
     for c in range(0, HUB_BLOCKS, 4):
         for k in range(4):
             for r in range(per):
                 tile = (c + k) * per + r
                 parts = [vals[plan[layer, tile]] for layer in range(LAYERS)]
-                dense[c + k, r * TILE : (r + 1) * TILE, :] = ((parts[0].astype(F32) + parts[1].astype(F32)) + (parts[2].astype(F32) + parts[3].astype(F32))).astype(BF16)
+                dense[c + k, r * TILE : (r + 1) * TILE, :] = (
+                    (parts[0].astype(F32) + parts[1].astype(F32)) + parts[2].astype(F32)
+                ).astype(BF16)
         lhs = jnp.concatenate([dense[c + k] for k in range(4)], axis=1)
         part = pl.ds(c * TILE, 4 * TILE)
         out[part, :WIDTH] = contract(lhs, msg[...], 0, 0).astype(BF16)
@@ -307,25 +315,28 @@
     w_send = contract(jnp.where(core == 0, aggregated, features), cotangent, 0, 0)
     w_came = lax.ppermute(w_send, "core", swap)
     w_keep = contract(jnp.where(core == 0, features, aggregated), cotangent, 0, 0)
-    msg = (contract(cotangent, w_neigh, 1, 1) / degrees[:, None].astype(F32)).astype(BF16)
+    msg, vals, tables = call(
+        ready_kernel, "ready", 0, [INSIDE] * 5 + [OUTSIDE], [INSIDE] * 3,
+        [
+            pltpu.VMEM((NODES, WIDTH), BF16),
+            pltpu.VMEM((REG + 40, TILE, TILE), BF16),
+            jax.ShapeDtypeStruct((8, PLAN), jnp.int32),
+        ],
+        [pltpu.SMEM((8, PLAN), jnp.int32), pltpu.SemaphoreType.DMA, pltpu.SemaphoreType.DMA],
+        2 * NODES * WIDTH * WIDTH, 6 << 20, 16, grid=(),
+    )(rows, cols, degrees.reshape(NODES // TILE, TILE), cotangent, w_neigh, tile_vals)
 
     wide = WIDTH + TILE
     packed = call(
-        ghost_kernel, "ghost", 0,
-        [INSIDE] * 5 + [OUTSIDE], OUTSIDE,
+        ghost_kernel, "ghost", 0, [SCALAR] + [INSIDE] * 4, OUTSIDE,
         pltpu.HBM((slots, wide), BF16),
         [
-            pltpu.VMEM((REG + 32, TILE, TILE), BF16),
             pltpu.VMEM((HUB_BLOCKS, NODES, TILE), BF16),
             pltpu.VMEM((slots, wide), BF16),
-            pltpu.VMEM((8, PLAN), jnp.int32),
-            pltpu.SMEM((8, PLAN), jnp.int32),
-            pltpu.SemaphoreType.DMA,
             pltpu.SemaphoreType.DMA((4,)),
-            pltpu.SemaphoreType.DMA,
         ],
         region_flops, region_bytes + (2 << 20), 18, grid=(),
-    )(rows, cols, msg, w_keep, w_came, tile_vals)
+    )(tables, msg, w_keep, w_came, vals)
     arrived = lax.all_to_all(
         packed.reshape(128, 16, wide), ALL, split_axis=0, concat_axis=0, tiled=True
     ).reshape(slots, wide)

time: 95.3 us -> 94.9 us (level)
  Pallas kernels: 31.1 us -> 32.2 us
    pallas_call x1 -> x2, Pallas kernels: 6.29 us -> 7.3 us  [the longest x1 4.82 us: local(): call(ghost_kernel, 'ghost', 0, [SCALAR] + [INSIDE] * 4, OUTSIDE, pltpu.HB...]
    dot_general x3 -> x2, matrix products: 3.92 us -> 3.15 us  [contract(): lax.dot_general(a, b, (((da,), (db,)), ((), ())), preferred_element_type=...]
  transfers between devices with their start and end apart: 5 -> 5, of which waited for: 3 -> 2; matrix products, arithmetic and copies ran while one was open for 2% -> 1% of each run, Pallas kernels for 23% -> 26%
where the time goes in v9:
time: 94.9 us; the launch traced here: 94.4 us
  waiting for transfers between devices  33.4 us (35%)
  Pallas kernels  32.2 us (34%)
  starting transfers between devices  21.4 us (23%)
  local copies, waits for them, and re-layouts  3.44 us (4%)
  matrix products  3.15 us (3%)
    all_to_all x1, waiting for transfers between devices, local(): lax.all_to_all(packed.reshape(128, 16, wide), ALL, split_axis=0, concat_a...  17.3 us
    all_to_all x1, waiting for transfers between devices, local(): lax.all_to_all(packed.reshape(64, 16, wider), ('y', 'z', 'x'), split_axis...  16.1 us
    all_to_all x1, starting transfers between devices, local(): lax.all_to_all(packed.reshape(128, 16, wide), ALL, split_axis=0, concat_a...  10.6 us
    pallas_call x1, Pallas kernels, local(): call(hub_kernel, 'hub', 1, [spec_rc, spec_rc, spec_nodes, OUTSIDE], [spec...  6.79 us
    pallas_call x1, Pallas kernels, local(): call(own_kernel, 'own', 0, [spec_rc, spec_rc, spec_nodes, spec_nodes, spe...  6.29 us
    all_to_all x1, starting transfers between devices, local(): lax.all_to_all(packed.reshape(64, 16, wider), ('y', 'z', 'x'), split_axis...  5.58 us
    pallas_call x1, Pallas kernels, local(): call(landing_kernel, 'landing', 0, [whole(8, 256), spec_nodes, whole(slot...  5.23 us
    pallas_call x1, Pallas kernels, local(): call(ghost_kernel, 'ghost', 0, [SCALAR] + [INSIDE] * 4, OUTSIDE, pltpu.HB...  4.82 us
  transfers between devices with their start and end apart: 5, of which 2 were waited for; matrix products, arithmetic and copies ran while one was open for 1% of the time, Pallas kernels for 26%

profile of v9, /device:TPU:1, one launch (start us, length us, event | category | flops | bytes accessed | tf_op | source)
XLA Modules:
  0.0 94.4 jit_solution(16976112311724011149)
XLA Ops:
  0.6 0.0 copy-start
  0.6 0.0 copy-start.3
  0.7 0.0 copy-start.5
  0.7 0.0 copy-start.6
  0.7 0.0 copy-start.7
  0.7 2.4 %fusion = f32[512,512]{1,0:T(8,128)S(1)} fusion(bf16[1024,512]{1,0:T(8,128)(2,1)} %cot_ref.3, bf16[1024,512]{1,0:T(8,128)(2,1)} %param.11, bf16[1024,512]{1,0:T(8,128)(2,1)} %param.10, pred[]{:T(512)S(6)} %eq.4), kind=kOutput, calls=%fused_computation | convolution fusion | flops 537395200 | bytes 4194305 | tf_op jit(solution)/shard_map/dot_general | solution.py:25
  3.1 1.5 %collective-permute-start = (f32[512,512]{1,0:T(8,128)S(1)}, f32[512,512]{1,0:T(8,128)S(1)}, u32[]{:S(2)}, u32[]{:S(2)}) collective-permute-start(f32[512,512]{1,0:T(8,128)S(1)} %fusion), channel_id=1, source_target_pairs={{0,16},{16,0},{1,17},{17,1},{2,18},{18,2},{3,19},{19,3},{4,20},{20... | collective-permute-start | bytes 3145736 | tf_op jit(solution)/shard_map/ppermute | solution.py:316
  4.6 0.0 copy-done
  4.6 0.0 copy-done.3
  4.6 0.0 copy-done.5
  4.6 0.0 copy-done.6
  4.6 0.0 copy-done.7
  4.6 0.0 copy-start.9
  4.6 0.0 copy-start.10
  4.6 2.5 %ready.1 = (bf16[1024,512]{1,0:T(8,128)(2,1)S(1)}, bf16[168,128,128]{2,1,0:T(8,128)(2,1)S(1)}, s32[8,256]{1,0:T(8,128)S(1)}) custom-call(s32[3,128]{1,0:T(4,128)S(1)} %bitcast.12, s32[3,128]{1,0:T(4,128)S(1)} %bitcast.15, s32[8,128]{1,0:T(8,128)S(1)} %bitcast.18, bf16[1024,512]{1,0:T(8,128)(2,1)S(1)} %copy-done, bf16[512,512]{1,0:T(8,128)(2,1)S(1)} %copy-done.3, ...), custom_call_target="tpu_custom_call" | custom-call | flops 536870912 | bytes 6291456 | tf_op jit(solution)/shard_map/ready/pallas_call | solution.py:318
  7.1 0.0 copy-done.9
  7.1 0.3 copy-done.10
  7.4 0.7 fusion.2.keep
  8.2 0.0 collective-permute-done.came
  8.2 4.8 %ghost.1 = bf16[2048,640]{1,0:T(8,128)(2,1)} custom-call(s32[8,256]{1,0:T(8,128)S(1)} %get-tuple-element.14.plan, bf16[1024,512]{1,0:T(8,128)(2,1)S(1)} %get-tuple-element.15.msg.msg_ref, f32[512,512]{1,0:T(8,128)S(1)} %fusion.2.keep, f32[512,512]{1,0:T(8,128)S(1)} %collective-permute-done.came, bf16[168,128,128]{2,1,0:T(8,128)(2,1)S(1)} %get-tuple-element.16.vals), custom_call_target="tpu_custom_call" | custom-call | flops 2147483648 | bytes 9437184 | tf_op jit(solution)/shard_map/ghost/pallas_call | solution.py:330
  13.0 10.6 %all-to-all-start = ((bf16[128,16,640]{2,1,0:T(8,128)(2,1)}), bf16[128,16,640]{2,1,0:T(8,128)(2,1)}, u32[]{:S(2)}, u32[]{:S(2)}) async-start(bf16[128,16,640]{2,1,0:T(8,128)(2,1)} %bitcast.19), calls=%async_computation | async-start | bytes 5242880 | tf_op jit(solution)/shard_map/all_to_all | solution.py:340
  23.6 0.0 copy-start.4
  23.6 6.8 %hub.1 = (f32[1024,512]{1,0:T(8,128)S(1)}, f32[1024,512]{1,0:T(8,128)S(1)}) custom-call(s32[1]{0:T(128)} %bitcast.5.core, s32[3,128]{1,0:T(4,128)S(1)} %bitcast.13, s32[3,128]{1,0:T(4,128)S(1)} %bitcast.16, bf16[1024,512]{1,0:T(8,128)(2,1)S(1)} %get-tuple-element.15.msg.msg_ref, bf16[384,128,128]{2,1,0:T(8,128)(2,1)} %vals_hbm.5), custom_call_target="tpu_custom_call" | custom-call | flops 2147483648 | bytes 9437184 | tf_op jit(solution)/shard_map/hub/pallas_call | solution.py:345
  30.4 1.2 %collective-permute-start.1 = (f32[1024,512]{1,0:T(8,128)S(1)}, f32[1024,512]{1,0:T(8,128)S(1)}, u32[]{:S(2)}, u32[]{:S(2)}) collective-permute-start(f32[1024,512]{1,0:T(8,128)S(1)} %get-tuple-element.18), channel_id=1, source_target_pairs={{0,16},{16,0},{1,17},{17,1},{2,18},{18,2},{3,19},{19,3},{4,20},{20... | collective-permute-start | bytes 6291464 | tf_op jit(solution)/shard_map/ppermute | solution.py:350
  31.6 0.0 copy-done.4
  31.6 6.3 %own.1.own_ref = f32[1024,512]{1,0:T(8,128)S(1)} custom-call(s32[3,128]{1,0:T(4,128)S(1)} %bitcast.14, s32[3,128]{1,0:T(4,128)S(1)} %bitcast.17, bf16[1024,512]{1,0:T(8,128)(2,1)S(1)} %get-tuple-element.15.msg.msg_ref, bf16[1024,512]{1,0:T(8,128)(2,1)S(1)} %copy-done, bf16[512,512]{1,0:T(8,128)(2,1)S(1)} %copy-done.4, bf16[384,128,128]{2,1,0:T(8,128)(2,1)} %vals_hbm.5), custom_call_target="tpu_custom_call" | custom-call | flops 2684354560 | bytes 7340032 | tf_op jit(solution)/shard_map/own/pallas_call | solution.py:351
  37.9 0.0 copy-start.1
  37.9 1.3 %copy-done.1 = f32[1024,512]{1,0:T(8,128)} copy-done((f32[1024,512]{1,0:T(8,128)}, f32[1024,512]{1,0:T(8,128)S(1)}, u32[]{:S(2)}) %copy-start.1) | copy-done | bytes 2097176
  39.3 0.0 collective-permute-done.1.came_ref
  39.3 1.6 %hub_pack.1.packed_hbm = bf16[1024,768]{1,0:T(8,128)(2,1)} custom-call(f32[1024,512]{1,0:T(8,128)S(1)} %get-tuple-element.17.keep_ref, f32[1024,512]{1,0:T(8,128)S(1)} %collective-permute-done.1.came_ref), custom_call_target="tpu_custom_call" | custom-call | flops 524288 | bytes 5242880 | tf_op jit(solution)/shard_map/hub_pack/pallas_call | solution.py:359
  40.9 17.3 %all-to-all-done = bf16[128,16,640]{2,1,0:T(8,128)(2,1)} async-done(((bf16[128,16,640]{2,1,0:T(8,128)(2,1)}), bf16[128,16,640]{2,1,0:T(8,128)(2,1)}, u32[]{:S(2)}, u32[]{:S(2)}) %all-to-all-start) | async-done | bytes 2621472 | tf_op jit(solution)/shard_map/all_to_all | solution.py:340
  58.2 2.1 %spread.1 = bf16[1024,768]{1,0:T(8,128)(2,1)} custom-call(bf16[2048,640]{1,0:T(8,128)(2,1)} %bitcast.4.arrived_ref, bf16[1024,768]{1,0:T(8,128)(2,1)} %hub_pack.1.packed_hbm), custom_call_target="tpu_custom_call", output_to_operand_aliasing={{}: (1, {})} | custom-call | flops 262144 | bytes 1048576 | tf_op jit(solution)/shard_map/spread/pallas_call | solution.py:364
  60.3 0.0 copy-start.8
  60.3 5.6 %all-to-all-start.1 = ((bf16[64,16,768]{2,1,0:T(8,128)(2,1)}), bf16[64,16,768]{2,1,0:T(8,128)(2,1)S(1)}, u32[]{:S(2)}, u32[]{:S(2)}) async-start(bf16[64,16,768]{2,1,0:T(8,128)(2,1)} %bitcast.6), calls=%async_computation.1 | async-start | bytes 3145728 | tf_op jit(solution)/shard_map/all_to_all | solution.py:369
  65.9 0.0 copy-done.8
  65.9 0.1 copy.16
  66.0 0.1 reshape.41.targets_ref
  66.1 0.0 copy-start.2
  66.1 1.6 %copy-done.2 = f32[1024,512]{1,0:T(8,128)S(1)} copy-done((f32[1024,512]{1,0:T(8,128)S(1)}, f32[1024,512]{1,0:T(8,128)}, u32[]{:S(2)}) %copy-start.2) | copy-done | bytes 2097176
  67.7 5.2 %landing.1 = f32[1024,512]{1,0:T(8,128)} custom-call(s32[8,256]{1,0:T(8,128)S(1)} %reshape.41.targets_ref, f32[1024,512]{1,0:T(8,128)S(1)} %copy-done.2, bf16[2048,640]{1,0:T(8,128)(2,1)} %bitcast.4.arrived_ref), custom_call_target="tpu_custom_call" | custom-call | flops 2147483648 | bytes 7340032 | tf_op jit(solution)/shard_map/landing/pallas_call | solution.py:373
  73.0 16.1 %all-to-all-done.1 = bf16[64,16,768]{2,1,0:T(8,128)(2,1)S(1)} async-done(((bf16[64,16,768]{2,1,0:T(8,128)(2,1)}), bf16[64,16,768]{2,1,0:T(8,128)(2,1)S(1)}, u32[]{:S(2)}, u32[]{:S(2)}) %all-to-all-start.1) | async-done | bytes 1572896 | tf_op jit(solution)/shard_map/all_to_all | solution.py:369
  89.1 2.5 %collective-permute-start.2 = (bf16[1024,256]{1,0:T(8,128)(2,1)S(1)}, bf16[1024,256]{1,0:T(8,128)(2,1)S(1)}, u32[]{:S(2)}, u32[]{:S(2)}) collective-permute-start(bf16[1024,256]{1,0:T(8,128)(2,1)S(1)} %slice.3), channel_id=1, source_target_pairs={{0,16},{16,0},{1,17},{17,1},{2,18},{18,2},{3,19},{19,3},{4,20},{20... | collective-permute-start | bytes 1572872 | tf_op jit(solution)/shard_map/ppermute | solution.py:380
  91.6 1.7 %finish.1 = (f32[16,512]{1,0:T(8,128)}, f32[2,512,512]{2,1,0:T(8,128)}) custom-call(s32[1]{0:T(128)} %bitcast.5.core, bf16[1024,768]{1,0:T(8,128)(2,1)S(1)} %bitcast.11), custom_call_target="tpu_custom_call" | custom-call | flops 524288 | bytes 3145728 | tf_op jit(solution)/shard_map/finish/pallas_call | solution.py:382
  93.3 0.0 collective-permute-done.2.came_ref
  93.3 1.1 %join.1 = f32[2,512,512]{2,1,0:T(8,128)} custom-call(s32[1]{0:T(128)} %bitcast.5.core, bf16[1024,256]{1,0:T(8,128)(2,1)S(1)} %collective-permute-done.2.came_ref, f32[2,512,512]{2,1,0:T(8,128)} %get-tuple-element.24.partial_hbm), custom_call_target="tpu_custom_call", output_to_operand_aliasing={{}: (2, {})} | custom-call | flops 524288 | bytes 2097152 | tf_op jit(solution)/shard_map/join/pallas_call | solution.py:387
  (1 shorter events, 0.0 us)
Async XLA Ops:
  0.6 4.0 %copy-start = (bf16[1024,512]{1,0:T(8,128)(2,1)S(1)}, bf16[1024,512]{1,0:T(8,128)(2,1)}, u32[]{:S(2)}) copy-start(bf16[1024,512]{1,0:T(8,128)(2,1)} %cot_ref.3) | copy-start | bytes 3145732
  0.6 4.0 %copy-start.3 = (bf16[512,512]{1,0:T(8,128)(2,1)S(1)}, bf16[512,512]{1,0:T(8,128)(2,1)}, u32[]{:S(2)}) copy-start(bf16[512,512]{1,0:T(8,128)(2,1)} %w_ref.2) | copy-start | bytes 1572868
  0.7 3.9 %copy-start.5 = (s32[384]{0:T(512)S(1)}, s32[384]{0:T(512)}, u32[]{:S(2)}) copy-start(s32[384]{0:T(512)} %param.16) | copy-start | bytes 4612
  0.7 3.9 %copy-start.6 = (s32[384]{0:T(512)S(1)}, s32[384]{0:T(512)}, u32[]{:S(2)}) copy-start(s32[384]{0:T(512)} %param.17) | copy-start | bytes 4612
  0.7 3.9 %copy-start.7 = (s32[1024]{0:T(1024)S(1)}, s32[1024]{0:T(1024)}, u32[]{:S(2)}) copy-start(s32[1024]{0:T(1024)} %param.15) | copy-start | bytes 12292
  3.1 5.1 %collective-permute-start = (f32[512,512]{1,0:T(8,128)S(1)}, f32[512,512]{1,0:T(8,128)S(1)}, u32[]{:S(2)}, u32[]{:S(2)}) collective-permute-start(f32[512,512]{1,0:T(8,128)S(1)} %fusion), channel_id=1, source_target_pairs={{0,16},{16,0},{1,17},{17,1},{2,18},{18,2},{3,19},{19,3},{4,20},{20... | collective-permute-start | bytes 3145736 | tf_op jit(solution)/shard_map/ppermute | solution.py:316
  4.6 2.5 %copy-start.9 = (bf16[1024,512]{1,0:T(8,128)(2,1)S(1)}, bf16[1024,512]{1,0:T(8,128)(2,1)}, u32[]{:S(2)}) copy-start(bf16[1024,512]{1,0:T(8,128)(2,1)} %param.10) | copy-start | bytes 3145732
  4.6 2.8 %copy-start.10 = (bf16[1024,512]{1,0:T(8,128)(2,1)S(1)}, bf16[1024,512]{1,0:T(8,128)(2,1)}, u32[]{:S(2)}) copy-start(bf16[1024,512]{1,0:T(8,128)(2,1)} %param.11) | copy-start | bytes 3145732
  13.0 45.2 %all-to-all-start = ((bf16[128,16,640]{2,1,0:T(8,128)(2,1)}), bf16[128,16,640]{2,1,0:T(8,128)(2,1)}, u32[]{:S(2)}, u32[]{:S(2)}) async-start(bf16[128,16,640]{2,1,0:T(8,128)(2,1)} %bitcast.19), calls=%async_computation | async-start | bytes 5242880 | tf_op jit(solution)/shard_map/all_to_all | solution.py:340
  23.6 8.0 %copy-start.4 = (bf16[512,512]{1,0:T(8,128)(2,1)S(1)}, bf16[512,512]{1,0:T(8,128)(2,1)}, u32[]{:S(2)}) copy-start(bf16[512,512]{1,0:T(8,128)(2,1)} %w_ref.3) | copy-start | bytes 1572868
  30.4 8.8 %collective-permute-start.1 = (f32[1024,512]{1,0:T(8,128)S(1)}, f32[1024,512]{1,0:T(8,128)S(1)}, u32[]{:S(2)}, u32[]{:S(2)}) collective-permute-start(f32[1024,512]{1,0:T(8,128)S(1)} %get-tuple-element.18), channel_id=1, source_target_pairs={{0,16},{16,0},{1,17},{17,1},{2,18},{18,2},{3,19},{19,3},{4,20},{20... | collective-permute-start | bytes 6291464 | tf_op jit(solution)/shard_map/ppermute | solution.py:350
  37.9 1.3 %copy-start.1 = (f32[1024,512]{1,0:T(8,128)}, f32[1024,512]{1,0:T(8,128)S(1)}, u32[]{:S(2)}) copy-start(f32[1024,512]{1,0:T(8,128)S(1)} %own.1.own_ref) | copy-start | bytes 6291460
  60.3 5.6 %copy-start.8 = (s32[1,128,16]{1,2,0:T(8,128)S(1)}, s32[1,128,16]{1,2,0:T(8,128)}, u32[]{:S(2)}) copy-start(s32[1,128,16]{1,2,0:T(8,128)} %param.19) | copy-start | bytes 24580
  60.3 28.7 %all-to-all-start.1 = ((bf16[64,16,768]{2,1,0:T(8,128)(2,1)}), bf16[64,16,768]{2,1,0:T(8,128)(2,1)S(1)}, u32[]{:S(2)}, u32[]{:S(2)}) async-start(bf16[64,16,768]{2,1,0:T(8,128)(2,1)} %bitcast.6), calls=%async_computation.1 | async-start | bytes 3145728 | tf_op jit(solution)/shard_map/all_to_all | solution.py:369
  66.1 1.6 %copy-start.2 = (f32[1024,512]{1,0:T(8,128)S(1)}, f32[1024,512]{1,0:T(8,128)}, u32[]{:S(2)}) copy-start(f32[1024,512]{1,0:T(8,128)} %copy-done.1) | copy-start | bytes 6291460
  89.1 4.2 %collective-permute-start.2 = (bf16[1024,256]{1,0:T(8,128)(2,1)S(1)}, bf16[1024,256]{1,0:T(8,128)(2,1)S(1)}, u32[]{:S(2)}, u32[]{:S(2)}) collective-permute-start(bf16[1024,256]{1,0:T(8,128)(2,1)S(1)} %slice.3), channel_id=1, source_target_pairs={{0,16},{16,0},{1,17},{17,1},{2,18},{18,2},{3,19},{19,3},{4,20},{20... | collective-permute-start | bytes 1572872 | tf_op jit(solution)/shard_map/ppermute | solution.py:380
